TPU v7x, 32 devices: a whole 2x2x4 slice. The times are simulated.
32 devices in a mesh: replica: 8 (over y, x, core), fsdp: 4 (over z).
Axes of the slice: x: 2, y: 2, z: 4, core: 2. Of those that a mesh axis runs over, the one named last changes fastest.
Arguments:
- activations: bfloat16 [8, 1792, 4096], P('replica', 'fsdp'), may hold values from -84 to 84
- targets: bfloat16 [8, 1792, 512], P('replica', 'fsdp'), may hold values from -8 to 8
- weights: float32 [8, 4096, 512], P('replica', 'fsdp'), may hold values from -19 to 19
- lengths: int32 [8, 28], P('replica'), may hold values from 1 to 64, 896 in all within a row
Outputs:
- averaged: float32 [8, 4096, 512], P('replica', 'fsdp')
Inputs may be any that keep to these rules, and one draw needn't show every extreme that they name: `lengths`: each row sums to 896; sequence s of a replica fills slot s from its first position.
All inputs are finite; a program needn't handle non-finite values.
Results may differ from a plain program's by a relative error of at most 0.0014.
Values may be sent and summed in bfloat16 or wider, within the bound.
No kernel may reach another device: no remote copies, remote signals or barrier semaphores. Data moves between devices by JAX's collectives and lax.ppermute only.
A program may use at most 64 MiB of HBM per device.

v0:
```python
import functools

import jax
import jax.numpy as jnp
from jax import lax
from jax.experimental import pallas as pl
from jax.experimental.pallas import tpu as pltpu
from jax.sharding import PartitionSpec as P

SLOT = 64
STEP = 3
ALIGN = 16
HALVES = 2

learning_rate = 0.1
epsilon = 1e-06


def swapped(value, axis, bit):
    mask = 2**bit
    pairs = [(source, source ^ mask) for source in range(lax.axis_size(axis))]
    return lax.ppermute(value, axis, pairs)


def turned(value, distance):
    members = lax.axis_size("fsdp")
    ring = [(source, (source + distance) % members) for source in range(members)]
    return lax.ppermute(value, "fsdp", ring)


def live_before(lengths_ref, members):
    sequences = lengths_ref.shape[1] // members
    totals = [jnp.int32(0)]
    for member in range(members):
        total = totals[-1]
        for q in range(sequences):
            total = total + lengths_ref[0, member * sequences + q]
        totals.append(total)
    return totals


def chosen(values, index):
    value = values[0]
    for i in range(1, len(values)):
        value = jnp.where(index == i, values[i], value)
    return value


def aligned(place):
    return pl.multiple_of(place // ALIGN * ALIGN, ALIGN)


def token_places(lengths_ref, member, before, tokens):
    sequences = tokens // SLOT
    place = before % ALIGN
    slot = lax.broadcasted_iota(jnp.int32, (1, tokens), 1)
    places = jnp.full((1, tokens), -1, jnp.int32)
    for s in range(sequences):
        length = lengths_ref[0, member * sequences + s]
        position = slot - s * SLOT
        places = jnp.where((position >= 0) & (position < length), position + place, places)
        place = place + length
    return places


def picking(places, start, rows):
    row = lax.broadcasted_iota(jnp.int32, (rows, places.shape[1]), 0) + start
    return jnp.where(row == places, 1.0, 0.0).astype(jnp.bfloat16)


class Block:
    def __init__(self, features_ref, member, block_ref, sems):
        self.block_ref, self.width = block_ref, block_ref.shape[1] // sems.shape[0]
        start = member * block_ref.shape[1]
        self.copies = []
        for j in range(sems.shape[0]):
            there = pl.ds(pl.multiple_of(start + j * self.width, 128), self.width)
            here = pl.ds(j * self.width, self.width)
            copy = pltpu.make_async_copy(
                features_ref.at[:, there], block_ref.at[:, here], sems.at[j]
            )
            copy.start()
            self.copies.append(copy)

    def picked(self, pick, store, wait):
        for j, copy in enumerate(self.copies):
            if wait:
                copy.wait()
            here = slice(j * self.width, (j + 1) * self.width)
            rows = jnp.dot(pick, self.block_ref[:, here], preferred_element_type=jnp.float32)
            store(here, rows.astype(jnp.bfloat16))


def sent_kernel(members, offsets, sizes, lengths_ref, features_ref, *refs):
    parts, (choice_ref, block_ref, sems) = refs[:-3], refs[-3:]
    count = len(offsets)
    index = lax.axis_index("fsdp")
    blocks = [
        Block(features_ref, lax.rem(index + i, members), block_ref.at[n], sems.at[n])
        for n, i in enumerate(offsets)
    ]
    totals = live_before(lengths_ref, members)
    longest = jnp.int32(0)
    for member in range(members):
        longest = jnp.maximum(longest, totals[member + 1] - aligned(totals[member]))
    first = parts[0].shape[0]
    choice = jnp.int32(0)
    for size in sizes[:-1]:
        choice = choice + jnp.where(longest > first + size, 1, 0)
    choice_ref[0] = choice
    choice_ref[1] = jnp.where(longest > first + sizes[-1], 1, 0)
    before, end = chosen(totals[:-1], index), chosen(totals[1:], index)
    places = token_places(lengths_ref, index, before, block_ref.shape[1])
    used = end - aligned(before)

    def fill(refs, start, wait):
        pick = picking(places, start, refs[0].shape[0])
        for block, ref in zip(blocks, refs):

            def store(here, rows, ref=ref):
                ref[:, here] = rows

            block.picked(pick, store, wait)

    start = 0
    for j in range(3):
        group = parts[j * count : (j + 1) * count]
        if j:
            pl.when(used > start)(functools.partial(fill, group, start, False))
        else:
            fill(group, start, True)
        start = start + group[0].shape[0]


def own_kernel(
    members,
    lengths_ref,
    features_ref,
    targets_ref,
    master_ref,
    partner_ref,
    rows_ref,
    wanted_ref,
    low_ref,
    halves_ref,
    block_ref,
    sems,
):
    index = lax.axis_index("fsdp")
    block = Block(features_ref, index, block_ref, sems)
    rows_ref[...] = jnp.zeros_like(rows_ref)
    low_ref[...] = master_ref[...].astype(jnp.bfloat16)
    halves_ref[...] = 0.5 * (master_ref[...] + partner_ref[...])
    totals = live_before(lengths_ref, members)
    before = chosen(totals[:-1], index)
    places = token_places(lengths_ref, index, before, block_ref.shape[0])
    pick = picking(places, 0, wanted_ref.shape[0])
    wanted_ref[...] = jnp.dot(pick, targets_ref[...], preferred_element_type=jnp.float32)

    def store(here, rows):
        rows_ref[pl.ds(aligned(before), wanted_ref.shape[0]), here] = rows

    block.picked(pick, store, True)


def half_keys(members, half, scale, lengths_ref, wanted_ref, low_ref, rows_ref, sums, total_ref):
    index = lax.axis_index("fsdp")
    share, width = sums[0].shape
    here = slice(half * width, (half + 1) * width)

    @pl.loop(0, members)
    def _(j):
        rows = pl.ds(pl.multiple_of(j * share, ALIGN), share)
        total_ref[rows] = (
            jnp.dot(rows_ref[rows], low_ref[:, here], preferred_element_type=jnp.float32) * scale
        )

    own_start = aligned(chosen(live_before(lengths_ref, members)[:-1], index))
    total_ref[pl.ds(own_start, wanted_ref.shape[0])] -= wanted_ref[:, here]
    for i in range(members):
        owner = lax.rem(index + i, members)
        block = total_ref[pl.ds(pl.multiple_of(owner * share, ALIGN), share)]
        sums[i][...] = block.astype(sums[i].dtype)


def keys_kernel(members, offsets, scale, lengths_ref, wanted_ref, low_ref, rows_ref, *refs):
    others = members - 1
    held, sums = refs[: 3 * others], refs[3 * others : 3 * others + HALVES * members]
    all_ref, total_ref, first_ref, *rest_refs, first_sems, rest_sems = refs[
        3 * others + HALVES * members :
    ]
    del rows_ref
    index = lax.axis_index("fsdp")
    share = sums[0].shape[0]
    totals = live_before(lengths_ref, members)
    copies = [
        pltpu.make_async_copy(held[3 * i], first_ref.at[i], first_sems.at[i]) for i in range(others)
    ]
    for copy in copies:
        copy.start()
    for i in range(others):
        member = lax.rem(index + members - offsets[i], members)
        begin = aligned(chosen(totals[:-1], member))
        used = chosen(totals[1:], member) - begin
        copies[i].wait()
        start = first_ref.shape[1]
        all_ref[pl.ds(begin, start)] += first_ref[i]
        for j in range(2):
            part_ref = rest_refs[j]

            @pl.when(used > start)
            def _(i=i, j=j, begin=begin, used=used, start=start, part_ref=part_ref):
                copy = pltpu.make_async_copy(held[3 * i + 1 + j], part_ref, rest_sems.at[2 * i + j])
                copy.start()
                copy.wait()
                for k in range(0, part_ref.shape[0], ALIGN):

                    @pl.when(used > start + k)
                    def _(k=k):
                        all_ref[pl.ds(begin + start + k, ALIGN)] += part_ref[k : k + ALIGN]

            start = start + part_ref.shape[0]

    for half in range(HALVES):
        here = sums[half * members : (half + 1) * members]
        half_keys(members, half, scale, lengths_ref, wanted_ref, low_ref, all_ref, here, total_ref)


def turn_kernel(all_ref, turned_ref):
    for start in range(0, turned_ref.shape[1], 128):
        turned_ref[:, start : start + 128] = all_ref[start : start + 128, :].T


def gradient_kernel(members, turned_ref, *refs):
    residuals, (gradient_ref, low_ref, squares_ref, all_ref) = refs[:members], refs[members:]
    index = lax.axis_index("fsdp")
    share = residuals[0].shape[0]
    for i in range(members):
        owner = lax.rem(index + members - i, members)
        all_ref[pl.ds(pl.multiple_of(owner * share, ALIGN), share)] = residuals[i][...]
    squares_ref[...] = jnp.zeros_like(squares_ref)
    height = min(256, turned_ref.shape[0])

    @pl.loop(0, turned_ref.shape[0] // height)
    def _(j):
        rows = pl.ds(pl.multiple_of(j * height, height), height)
        gradient = jnp.dot(turned_ref[rows], all_ref[...], preferred_element_type=jnp.float32)
        gradient_ref[rows] = gradient
        low_ref[rows] = gradient.astype(low_ref.dtype)
        squares = jnp.sum((gradient * gradient).reshape(-1, 8, gradient.shape[1]), axis=0)
        lanes = squares.shape[1] // 128
        squares_ref[...] += sum(squares[:, 128 * k : 128 * (k + 1)] for k in range(lanes))


def average_kernel(entries, own_ref, other_ref, halves_ref, *refs):
    gradients, partners, (out_ref, done_ref, sems) = refs[:HALVES], refs[HALVES:-3], refs[-3:]
    rate = 0.5 * learning_rate
    own = rate * lax.rsqrt(jnp.sum(own_ref[...], keepdims=True) / entries + epsilon)
    other = rate * lax.rsqrt(jnp.sum(other_ref[...], keepdims=True) / entries + epsilon)
    pieces = sems.shape[0]
    height = done_ref.shape[0] // pieces
    width = done_ref.shape[1] // HALVES
    copies = []
    for j in range(pieces):
        rows = pl.ds(j * height, height)
        for half in range(HALVES):
            here = slice(half * width, (half + 1) * width)
            done_ref[rows, here] = (
                halves_ref[rows, here]
                - gradients[half][rows] * own
                - partners[half][rows].astype(jnp.float32) * other
            )
        copies.append(pltpu.make_async_copy(done_ref.at[rows], out_ref.at[rows], sems.at[j]))
        copies[-1].start()
    for copy in copies:
        copy.wait()


def more_rows(size, offsets, blocks):
    if size == 0:
        return list(blocks)
    moved = [turned(block[:size], i) for i, block in zip(offsets, blocks)]
    return [jnp.pad(m, ((0, b.shape[0] - size), (0, 0))) for m, b in zip(moved, blocks)]


def local(activations, targets, weights, lengths):
    features = activations[0]
    wanted = targets[0]
    master = weights[0]
    tokens_here = features.shape[0]
    local_rows, columns = master.shape
    members = lax.axis_size("fsdp")
    distance_bit = STEP % (lax.axis_size("replica").bit_length() - 1)
    share = tokens_here // 2
    first = -(-(share + 32) // ALIGN) * ALIGN
    sizes = list(range(0, 97, ALIGN))
    parts = [first, sizes[-1], -(-(tokens_here + ALIGN - first - sizes[-1]) // ALIGN) * ALIGN]
    most = sum(parts)
    scale = features.shape[1] ** (-0.5)
    places = members * share + most

    vmem = pl.BlockSpec(memory_space=pltpu.VMEM)
    anywhere = pl.BlockSpec(memory_space=pl.ANY)
    smem = pl.BlockSpec(memory_space=pltpu.SMEM)
    params = pltpu.CompilerParams(vmem_limit_bytes=40 * 2**20)
    large = pltpu.CompilerParams(vmem_limit_bytes=56 * 2**20)

    def array(rows, width, dtype):
        return jax.ShapeDtypeStruct((rows, width), dtype)

    def cost(flops, moved):
        return pl.CostEstimate(flops=flops, bytes_accessed=moved, transcendentals=0)

    def block_scratch(*count):
        return [
            pltpu.VMEM((*count, tokens_here, local_rows), jnp.bfloat16),
            pltpu.SemaphoreType.DMA((*count, max(1, local_rows // 256))),
        ]

    def sent_to(offsets):
        count = len(offsets)
        *arrays, choice = pl.pallas_call(
            functools.partial(sent_kernel, members, offsets, sizes),
            in_specs=[smem, anywhere],
            out_specs=[vmem] * (3 * count) + [smem],
            out_shape=[array(rows, local_rows, jnp.bfloat16) for rows in parts for _ in offsets]
            + [jax.ShapeDtypeStruct((2,), jnp.int32)],
            scratch_shapes=block_scratch(count),
            compiler_params=large,
            cost_estimate=cost(
                2 * count * first * tokens_here * local_rows,
                2 * count * (tokens_here + first) * local_rows,
            ),
        )(lengths, features)
        return [arrays[j * count : (j + 1) * count] for j in range(3)], choice

    far = members // 2
    near = [i for i in range(1, members) if i != far]
    far_parts, choice = sent_to([far])
    near_parts, _ = sent_to(near)
    held_far = turned(far_parts[0][0], far)
    offsets = [far] + near
    held_more = lax.switch(
        choice[0],
        [functools.partial(more_rows, size, offsets) for size in sizes],
        far_parts[1] + near_parts[1],
    )
    held_rest = lax.cond(
        choice[1] > 0,
        functools.partial(more_rows, parts[2], offsets),
        functools.partial(more_rows, 0, offsets),
        far_parts[2] + near_parts[2],
    )
    near_first, held_more, held_rest, late_lengths = lax.optimization_barrier(
        (near_parts[0], held_more, held_rest, lengths)
    )
    held_first = [held_far] + [turned(block, i) for i, block in zip(near, near_first)]
    held = [part for group in zip(held_first, held_more, held_rest) for part in group]

    partner_master = swapped(master, "replica", distance_bit)
    own_rows, own_wanted, low, halves = pl.pallas_call(
        functools.partial(own_kernel, members),
        in_specs=[smem, anywhere, vmem, vmem, vmem],
        out_specs=[vmem] * 4,
        out_shape=[
            array(places, local_rows, jnp.bfloat16),
            array(most, columns, jnp.float32),
            array(local_rows, columns, jnp.bfloat16),
            array(local_rows, columns, jnp.float32),
        ],
        scratch_shapes=block_scratch(),
        compiler_params=params,
        cost_estimate=cost(
            2 * most * tokens_here * (local_rows + columns), 20 * local_rows * columns
        ),
    )(late_lengths, features, wanted, master, partner_master)

    width = columns // HALVES
    sum_shapes = [array(share, width, jnp.bfloat16 if i else jnp.float32) for i in range(members)]
    *sums, rows = pl.pallas_call(
        functools.partial(keys_kernel, members, offsets, scale),
        in_specs=[smem, vmem, vmem, vmem] + [anywhere] * (3 * members - 3),
        out_specs=[vmem] * (HALVES * members + 1),
        out_shape=sum_shapes * HALVES + [array(places, local_rows, jnp.bfloat16)],
        input_output_aliases={3: HALVES * members},
        scratch_shapes=[
            pltpu.VMEM((places, width), jnp.float32),
            pltpu.VMEM((members - 1, first, local_rows), jnp.bfloat16),
            pltpu.VMEM((parts[1], local_rows), jnp.bfloat16),
            pltpu.VMEM((parts[2], local_rows), jnp.bfloat16),
            pltpu.SemaphoreType.DMA((members - 1,)),
            pltpu.SemaphoreType.DMA((2 * members - 2,)),
        ],
        compiler_params=params,
        cost_estimate=cost(
            2 * members * share * local_rows * columns, 4 * places * (local_rows + columns)
        ),
    )(lengths, own_wanted, low, own_rows, *held)
    sums = [sums[half * members : (half + 1) * members] for half in range(HALVES)]

    turned_rows = pl.pallas_call(
        turn_kernel,
        in_specs=[vmem],
        out_specs=vmem,
        out_shape=array(local_rows, members * share, jnp.bfloat16),
        compiler_params=params,
        cost_estimate=cost(0, 4 * members * share * local_rows),
    )(rows)

    gradients, partners, squares = [], [], 0.0
    for half in range(HALVES):
        residual = sums[half][0]
        for i in range(1, members):
            residual = residual + turned(sums[half][i], i).astype(jnp.float32)
        residual = residual.astype(jnp.bfloat16)
        residuals = [residual] + [turned(residual, i) for i in range(1, members)]
        gradient, low_gradient, own_squares = pl.pallas_call(
            functools.partial(gradient_kernel, members),
            in_specs=[vmem] + [vmem] * members,
            out_specs=[vmem] * 3,
            out_shape=[
                array(local_rows, width, jnp.float32),
                array(local_rows, width, jnp.bfloat16),
                array(8, 128, jnp.float32),
            ],
            scratch_shapes=[pltpu.VMEM((members * share, width), jnp.bfloat16)],
            compiler_params=params,
            cost_estimate=cost(
                2 * members * share * local_rows * width, 8 * local_rows * width
            ),
        )(turned_rows, *residuals)
        gradients.append(gradient)
        partners.append(swapped(low_gradient, "replica", distance_bit))
        squares = squares + own_squares

    total = squares
    for i in range(1, members):
        total = total + turned(squares, i)
    partner_total = swapped(total, "replica", distance_bit)

    averaged = pl.pallas_call(
        functools.partial(average_kernel, members * local_rows * columns),
        in_specs=[vmem] * (3 + 2 * HALVES),
        out_specs=anywhere,
        out_shape=array(local_rows, columns, jnp.float32),
        scratch_shapes=[
            pltpu.VMEM((local_rows, columns), jnp.float32),
            pltpu.SemaphoreType.DMA((4,)),
        ],
        compiler_params=params,
    )(total, partner_total, halves, *gradients, *partners)
    return averaged[None]


def solution(mesh):
    return jax.shard_map(
        local,
        mesh=mesh,
        in_specs=(
            P("replica", "fsdp", None),
            P("replica", "fsdp", None),
            P("replica", "fsdp", None),
            P("replica", None),
        ),
        out_specs=P("replica", "fsdp", None),
        check_vma=False,
    )
```

profile of v0, /device:TPU:7, one launch (start us, length us, event | category | flops | bytes accessed | tf_op | source)
XLA Modules:
  0.0 121.5 jit_solution(4806321840441881233)
XLA Ops:
  0.7 3.9 %shard_map.47 = (bf16[256,1024]{1,0:T(8,128)(2,1)}, bf16[96,1024]{1,0:T(8,128)(2,1)S(1)}, bf16[112,1024]{1,0:T(8,128)(2,1)}, s32[2]{0:T(128)}) custom-call(s32[1,28]{1,0:T(1,128)} %lengths_ref.6, bf16[448,4096]{1,0:T(8,128)(2,1)} %bitcast.9), custom_call_target="tpu_custom_call" | custom-call | flops 234881024 | bytes 1441792 | tf_op jit(solution)/shard_map/pallas_call | solution.py:322
  4.6 2.4 %collective-permute-start.22 = (bf16[256,1024]{1,0:T(8,128)(2,1)}, bf16[256,1024]{1,0:T(8,128)(2,1)S(1)}, u32[]{:S(2)}, u32[]{:S(2)}) collective-permute-start(bf16[256,1024]{1,0:T(8,128)(2,1)} %get-tuple-element.143), channel_id=1, source_target_pairs={{0,2},{1,3},{2,0},{3,1},{4,6},{5,7},{6,4},{7,5},{8,10},{9,11},{10,... | collective-permute-start | bytes 1572872 | tf_op jit(solution)/shard_map/ppermute | solution.py:28
  7.0 1.4 %fusion = (s32[1]{0:T(128)}, s32[1]{0:T(128)}) fusion(s32[2]{0:T(128)} %get-tuple-element.126), kind=kLoop, calls=%fused_computation.3 | loop fusion | bytes 16 | tf_op jit(solution)/shard_map/slice | solution.py:349
  9.8 5.6 %shard_map.46 = (bf16[256,1024]{1,0:T(8,128)(2,1)}, bf16[256,1024]{1,0:T(8,128)(2,1)}, bf16[96,1024]{1,0:T(8,128)(2,1)}, bf16[96,1024]{1,0:T(8,128)(2,1)S(1)}, b...) custom-call(s32[1,28]{1,0:T(1,128)} %lengths_ref.6, bf16[448,4096]{1,0:T(8,128)(2,1)} %bitcast.10), custom_call_target="tpu_custom_call" | custom-call | flops 469762048 | bytes 2883584 | tf_op jit(solution)/shard_map/pallas_call | solution.py:322
  15.4 22.3 %conditional.2 = ((bf16[96,1024]{1,0:T(8,128)(2,1)S(1)}, bf16[96,1024]{1,0:T(8,128)(2,1)}, bf16[96,1024]{1,0:T(8,128)(2,1)S(1)})) conditional(s32[]{:T(128)} %bitcast.1, (bf16[96,1024]{1,0:T(8,128)(2,1)S(1)}, bf16[96,1024]{1,0:T(8,128)(2,1)}, bf16[96,1024]{1,0:T(8,128)(2,1)S(1)}) %tuple.40, ...), branch_computations={%region_0.0_spmd, %region_1.2_spmd, %region_2.3_spmd, %region_3.4_... | conditional | bytes 4030622 | solution.py:343
  15.9 1.1 slice.41
  18.3 2.6 %collective-permute-done.8 = bf16[48,1024]{1,0:T(8,128)(2,1)S(1)} collective-permute-done((bf16[48,1024]{1,0:T(8,128)(2,1)S(1)}, bf16[48,1024]{1,0:T(8,128)(2,1)S(1)}, u32[]{:S(2)}, u32[]{:S(2)}) %collective-permute-start.8) | collective-permute-done | bytes 98336 | tf_op jit(solution)/shard_map/cond/branch_3_fun/ppermute | solution.py:28
  20.9 3.1 %collective-permute-done.7 = bf16[48,1024]{1,0:T(8,128)(2,1)S(1)} collective-permute-done((bf16[48,1024]{1,0:T(8,128)(2,1)S(1)}, bf16[48,1024]{1,0:T(8,128)(2,1)S(1)}, u32[]{:S(2)}, u32[]{:S(2)}) %collective-permute-start.7) | collective-permute-done | bytes 98336 | tf_op jit(solution)/shard_map/cond/branch_3_fun/ppermute | solution.py:28
  24.7 13.0 %collective-permute-done.6 = bf16[48,1024]{1,0:T(8,128)(2,1)S(1)} collective-permute-done((bf16[48,1024]{1,0:T(8,128)(2,1)S(1)}, bf16[48,1024]{1,0:T(8,128)(2,1)S(1)}, u32[]{:S(2)}, u32[]{:S(2)}) %collective-permute-start.6) | collective-permute-done | bytes 98336 | tf_op jit(solution)/shard_map/cond/branch_3_fun/ppermute | solution.py:28
  38.4 2.7 %collective-permute-start.24 = (bf16[256,1024]{1,0:T(8,128)(2,1)}, bf16[256,1024]{1,0:T(8,128)(2,1)S(1)}, u32[]{:S(2)}, u32[]{:S(2)}) collective-permute-start(bf16[256,1024]{1,0:T(8,128)(2,1)} %get-tuple-element.149), channel_id=1, source_target_pairs={{0,3},{1,0},{2,1},{3,2},{4,7},{5,4},{6,5},{7,6},{8,11},{9,8},{10,9... | collective-permute-start | bytes 1572872 | tf_op jit(solution)/shard_map/ppermute | solution.py:28
  41.2 5.0 %shard_map.48 = (bf16[1360,1024]{1,0:T(8,128)(2,1)S(1)}, f32[464,512]{1,0:T(8,128)S(1)}, bf16[1024,512]{1,0:T(8,128)(2,1)S(1)}, f32[1024,512]{1,0:T(8,128)S(1)}) custom-call(s32[1,28]{1,0:T(1,128)S(1)} %copy-done.2, bf16[448,4096]{1,0:T(8,128)(2,1)} %bitcast.11, bf16[448,512]{1,0:T(8,128)(2,1)S(1)} %bitcast.8, f32[1024,512]{1,0:T(8,128)S(1)} %bitcast.7, ...), custom_call_target="tpu_custom_call" | custom-call | flops 638582784 | bytes 10485760 | tf_op jit(solution)/shard_map/pallas_call | solution.py:361
  46.2 7.5 %collective-permute-done.23.refs_3_ = bf16[256,1024]{1,0:T(8,128)(2,1)S(1)} collective-permute-done((bf16[256,1024]{1,0:T(8,128)(2,1)}, bf16[256,1024]{1,0:T(8,128)(2,1)S(1)}, u32[]{:S(2)}, u32[]{:S(2)}) %collective-permute-start.23) | collective-permute-done | bytes 524320 | tf_op jit(solution)/shard_map/ppermute | solution.py:28
  53.7 8.7 %collective-permute-done.24.refs_6_ = bf16[256,1024]{1,0:T(8,128)(2,1)S(1)} collective-permute-done((bf16[256,1024]{1,0:T(8,128)(2,1)}, bf16[256,1024]{1,0:T(8,128)(2,1)S(1)}, u32[]{:S(2)}, u32[]{:S(2)}) %collective-permute-start.24) | collective-permute-done | bytes 524320 | tf_op jit(solution)/shard_map/ppermute | solution.py:28
  62.4 3.8 %shard_map.49 = (f32[224,256]{1,0:T(8,128)S(1)}, bf16[224,256]{1,0:T(8,128)(2,1)S(1)}, bf16[224,256]{1,0:T(8,128)(2,1)S(1)}, bf16[224,256]{1,0:T(8,128)(2,1)S(1)...) custom-call(s32[1,28]{1,0:T(1,128)S(1)} %copy-done.2, ...), custom_call_target="tpu_custom_call", output_to_operand_aliasing={{8}: (3, {})} | custom-call | flops 939524096 | bytes 8355840 | tf_op jit(solution)/shard_map/pallas_call | solution.py:380
  66.2 3.2 %collective-permute-start.31 = (bf16[224,256]{1,0:T(8,128)(2,1)S(1)}, bf16[224,256]{1,0:T(8,128)(2,1)S(1)}, u32[]{:S(2)}, u32[]{:S(2)}) collective-permute-start(bf16[224,256]{1,0:T(8,128)(2,1)S(1)} %get-tuple-element.159), channel_id=1, source_target_pairs={{0,1},{1,2},{2,3},{3,0},{4,5},{5,6},{6,7},{7,4},{8,9},{9,10},{10,1... | collective-permute-start | bytes 344072 | tf_op jit(solution)/shard_map/ppermute | solution.py:28
  69.4 1.4 %collective-permute-start.32 = (bf16[224,256]{1,0:T(8,128)(2,1)S(1)}, bf16[224,256]{1,0:T(8,128)(2,1)S(1)}, u32[]{:S(2)}, u32[]{:S(2)}) collective-permute-start(bf16[224,256]{1,0:T(8,128)(2,1)S(1)} %get-tuple-element.160), channel_id=1, source_target_pairs={{0,2},{1,3},{2,0},{3,1},{4,6},{5,7},{6,4},{7,5},{8,10},{9,11},{10,... | collective-permute-start | bytes 344072 | tf_op jit(solution)/shard_map/ppermute | solution.py:28
  72.3 1.0 collective-permute-start.26
  73.3 2.9 %collective-permute-start.27 = (bf16[224,256]{1,0:T(8,128)(2,1)S(1)}, bf16[224,256]{1,0:T(8,128)(2,1)S(1)}, u32[]{:S(2)}, u32[]{:S(2)}) collective-permute-start(bf16[224,256]{1,0:T(8,128)(2,1)S(1)} %get-tuple-element.156), channel_id=1, source_target_pairs={{0,3},{1,0},{2,1},{3,2},{4,7},{5,4},{6,5},{7,6},{8,11},{9,8},{10,9... | collective-permute-start | bytes 344072 | tf_op jit(solution)/shard_map/ppermute | solution.py:28
  76.1 4.5 %collective-permute-done.32 = bf16[224,256]{1,0:T(8,128)(2,1)S(1)} collective-permute-done((bf16[224,256]{1,0:T(8,128)(2,1)S(1)}, bf16[224,256]{1,0:T(8,128)(2,1)S(1)}, u32[]{:S(2)}, u32[]{:S(2)}) %collective-permute-start.32) | collective-permute-done | bytes 114720 | tf_op jit(solution)/shard_map/ppermute | solution.py:28
  81.5 6.6 %collective-permute-start.35 = (bf16[224,256]{1,0:T(8,128)(2,1)S(1)}, bf16[224,256]{1,0:T(8,128)(2,1)S(1)}, u32[]{:S(2)}, u32[]{:S(2)}) collective-permute-start(bf16[224,256]{1,0:T(8,128)(2,1)S(1)} %add_convert_fusion.refs_0_), channel_id=1, source_target_pairs={{0,2},{1,3},{2,0},{3,1},{4,6},{5,7},{6,4},{7,5},{8,10},{9,11},{10,... | collective-permute-start | bytes 344072 | tf_op jit(solution)/shard_map/ppermute | solution.py:28
  89.0 7.5 %collective-permute-start.30 = (bf16[224,256]{1,0:T(8,128)(2,1)S(1)}, bf16[224,256]{1,0:T(8,128)(2,1)S(1)}, u32[]{:S(2)}, u32[]{:S(2)}) collective-permute-start(bf16[224,256]{1,0:T(8,128)(2,1)S(1)} %add_convert_fusion.1.refs_0_), channel_id=1, source_target_pairs={{0,3},{1,0},{2,1},{3,2},{4,7},{5,4},{6,5},{7,6},{8,11},{9,8},{10,9... | collective-permute-start | bytes 344072 | tf_op jit(solution)/shard_map/ppermute | solution.py:28
  96.5 1.4 %collective-permute-start.29 = (bf16[224,256]{1,0:T(8,128)(2,1)S(1)}, bf16[224,256]{1,0:T(8,128)(2,1)S(1)}, u32[]{:S(2)}, u32[]{:S(2)}) collective-permute-start(bf16[224,256]{1,0:T(8,128)(2,1)S(1)} %add_convert_fusion.1.refs_0_), channel_id=1, source_target_pairs={{0,2},{1,3},{2,0},{3,1},{4,6},{5,7},{6,4},{7,5},{8,10},{9,11},{10,... | collective-permute-start | bytes 344072 | tf_op jit(solution)/shard_map/ppermute | solution.py:28
  97.9 1.2 collective-permute-start.28
  99.5 2.9 %collective-permute-done.35.refs_2_ = bf16[224,256]{1,0:T(8,128)(2,1)S(1)} collective-permute-done((bf16[224,256]{1,0:T(8,128)(2,1)S(1)}, bf16[224,256]{1,0:T(8,128)(2,1)S(1)}, u32[]{:S(2)}, u32[]{:S(2)}) %collective-permute-start.35) | collective-permute-done | bytes 114720 | tf_op jit(solution)/shard_map/ppermute | solution.py:28
  102.5 1.3 %shard_map.52 = (f32[1024,256]{1,0:T(8,128)S(1)}, bf16[1024,256]{1,0:T(8,128)(2,1)S(1)}, f32[8,128]{1,0:T(8,128)S(1)}) custom-call(bf16[1024,896]{1,0:T(8,128)(2,1)S(1)} %shard_map.50.turned_ref, bf16[224,256]{1,0:T(8,128)(2,1)S(1)} %add_convert_fusion.refs_0_, bf16[224,256]{1,0:T(8,128)(2,1)S(1)} %collective-permute-done.34.refs_1_, ...), custom_call_target="tpu_custom_call" | custom-call | flops 469762048 | bytes 2097152 | tf_op jit(solution)/shard_map/pallas_call | solution.py:417
  103.8 4.3 %collective-permute-start.42 = (bf16[1024,256]{1,0:T(8,128)(2,1)S(1)}, bf16[1024,256]{1,0:T(8,128)(2,1)S(1)}, u32[]{:S(2)}, u32[]{:S(2)}) collective-permute-start(bf16[1024,256]{1,0:T(8,128)(2,1)S(1)} %get-tuple-element.167), channel_id=1, source_target_pairs={{0,4},{4,0},{8,12},{12,8},{16,20},{20,16},{24,28},{28,24},{1,5},{5... | collective-permute-start | bytes 1572872 | tf_op jit(solution)/shard_map/ppermute | solution.py:22
  108.1 3.0 %collective-permute-done.29.refs_2_ = bf16[224,256]{1,0:T(8,128)(2,1)S(1)} collective-permute-done((bf16[224,256]{1,0:T(8,128)(2,1)S(1)}, bf16[224,256]{1,0:T(8,128)(2,1)S(1)}, u32[]{:S(2)}, u32[]{:S(2)}) %collective-permute-start.29) | collective-permute-done | bytes 114720 | tf_op jit(solution)/shard_map/ppermute | solution.py:28
  111.1 1.3 %shard_map.51 = (f32[1024,256]{1,0:T(8,128)S(1)}, bf16[1024,256]{1,0:T(8,128)(2,1)S(1)}, f32[8,128]{1,0:T(8,128)S(1)}) custom-call(bf16[1024,896]{1,0:T(8,128)(2,1)S(1)} %shard_map.50.turned_ref, bf16[224,256]{1,0:T(8,128)(2,1)S(1)} %add_convert_fusion.1.refs_0_, bf16[224,256]{1,0:T(8,128)(2,1)S(1)} %collective-permute-done.28.refs_1_, ...), custom_call_target="tpu_custom_call" | custom-call | flops 469762048 | bytes 2097152 | tf_op jit(solution)/shard_map/pallas_call | solution.py:417
  113.0 1.5 %collective-permute-start.37 = (f32[8,128]{1,0:T(8,128)S(1)}, f32[8,128]{1,0:T(8,128)S(1)}, u32[]{:S(2)}, u32[]{:S(2)}) collective-permute-start(f32[8,128]{1,0:T(8,128)S(1)} %add.66), channel_id=1, source_target_pairs={{0,1},{1,2},{2,3},{3,0},{4,5},{5,6},{6,7},{7,4},{8,9},{9,10},{10,1... | collective-permute-start | bytes 12296 | tf_op jit(solution)/shard_map/ppermute | solution.py:28
  116.3 1.2 %collective-permute-done.37 = f32[8,128]{1,0:T(8,128)S(1)} collective-permute-done((f32[8,128]{1,0:T(8,128)S(1)}, f32[8,128]{1,0:T(8,128)S(1)}, u32[]{:S(2)}, u32[]{:S(2)}) %collective-permute-start.37) | collective-permute-done | bytes 4128 | tf_op jit(solution)/shard_map/ppermute | solution.py:28
  117.5 1.5 %collective-permute-start.40 = (f32[8,128]{1,0:T(8,128)S(1)}, f32[8,128]{1,0:T(8,128)S(1)}, u32[]{:S(2)}, u32[]{:S(2)}) collective-permute-start(f32[8,128]{1,0:T(8,128)S(1)} %add_add_fusion.own_ref), channel_id=1, source_target_pairs={{0,4},{4,0},{8,12},{12,8},{16,20},{20,16},{24,28},{28,24},{1,5},{5... | collective-permute-start | bytes 12296 | tf_op jit(solution)/shard_map/ppermute | solution.py:22
  119.8 1.7 %shard_map.53 = f32[1024,512]{1,0:T(8,128)} custom-call(f32[8,128]{1,0:T(8,128)S(1)} %add_add_fusion.own_ref, f32[8,128]{1,0:T(8,128)S(1)} %collective-permute-done.40.other_ref, f32[1024,512]{1,0:T(8,128)S(1)} %get-tuple-element.163.halves_ref, f32[1024,256]{1,0:T(8,128)S(1)} %get-tuple-element.164.refs_0_, f32[1024,256]{1,0:T(8,128)S(1)} %get-tuple-element.165.refs_1_, ...), custom_call_target="tpu_custom_call" | custom-call | tf_op jit(solution)/shard_map/pallas_call | solution.py:441
  (53 shorter events, 10.8 us)
Async XLA Ops:
  0.0 41.1 %collective-permute-start.21 = (f32[1024,512]{1,0:T(8,128)}, f32[1024,512]{1,0:T(8,128)}, u32[]{:S(2)}, u32[]{:S(2)}) collective-permute-start(f32[1024,512]{1,0:T(8,128)} %bitcast.6), channel_id=1, source_target_pairs={{0,4},{4,0},{8,12},{12,8},{16,20},{20,16},{24,28},{28,24},{1,5},{5... | collective-permute-start | bytes 6291464 | tf_op jit(solution)/shard_map/ppermute | solution.py:22
  4.6 41.6 %collective-permute-start.22 = (bf16[256,1024]{1,0:T(8,128)(2,1)}, bf16[256,1024]{1,0:T(8,128)(2,1)S(1)}, u32[]{:S(2)}, u32[]{:S(2)}) collective-permute-start(bf16[256,1024]{1,0:T(8,128)(2,1)} %get-tuple-element.143), channel_id=1, source_target_pairs={{0,2},{1,3},{2,0},{3,1},{4,6},{5,7},{6,4},{7,5},{8,10},{9,11},{10,... | collective-permute-start | bytes 1572872 | tf_op jit(solution)/shard_map/ppermute | solution.py:28
  15.4 25.7 %copy-start = (f32[1,1024,512]{2,1,0:T(8,128)S(1)}, f32[1,1024,512]{2,1,0:T(8,128)}, u32[]{:S(2)}) copy-start(f32[1,1024,512]{2,1,0:T(8,128)} %param.15) | copy-start | bytes 6291460
  15.4 25.7 %copy-start.1 = (bf16[1,448,512]{2,1,0:T(8,128)(2,1)S(1)}, bf16[1,448,512]{2,1,0:T(8,128)(2,1)}, u32[]{:S(2)}) copy-start(bf16[1,448,512]{2,1,0:T(8,128)(2,1)} %param.14) | copy-start | bytes 1376260
  15.4 25.7 %copy-start.2 = (s32[1,28]{1,0:T(1,128)S(1)}, s32[1,28]{1,0:T(1,128)}, u32[]{:S(2)}) copy-start(s32[1,28]{1,0:T(1,128)} %lengths_ref.6) | copy-start | bytes 340
  15.5 5.4 %collective-permute-start.8 = (bf16[48,1024]{1,0:T(8,128)(2,1)S(1)}, bf16[48,1024]{1,0:T(8,128)(2,1)S(1)}, u32[]{:S(2)}, u32[]{:S(2)}) collective-permute-start(bf16[48,1024]{1,0:T(8,128)(2,1)S(1)} %slice.42), channel_id=1, source_target_pairs={{0,3},{1,0},{2,1},{3,2},{4,7},{5,4},{6,5},{7,6},{8,11},{9,8},{10,9... | collective-permute-start | bytes 294920 | tf_op jit(solution)/shard_map/cond/branch_3_fun/ppermute | solution.py:28
  17.1 7.0 %collective-permute-start.7 = (bf16[48,1024]{1,0:T(8,128)(2,1)S(1)}, bf16[48,1024]{1,0:T(8,128)(2,1)S(1)}, u32[]{:S(2)}, u32[]{:S(2)}) collective-permute-start(bf16[48,1024]{1,0:T(8,128)(2,1)S(1)} %slice.41), channel_id=1, source_target_pairs={{0,1},{1,2},{2,3},{3,0},{4,5},{5,6},{6,7},{7,4},{8,9},{9,10},{10,1... | collective-permute-start | bytes 294920 | tf_op jit(solution)/shard_map/cond/branch_3_fun/ppermute | solution.py:28
  17.9 19.8 %collective-permute-start.6 = (bf16[48,1024]{1,0:T(8,128)(2,1)S(1)}, bf16[48,1024]{1,0:T(8,128)(2,1)S(1)}, u32[]{:S(2)}, u32[]{:S(2)}) collective-permute-start(bf16[48,1024]{1,0:T(8,128)(2,1)S(1)} %slice.40), channel_id=1, source_target_pairs={{0,2},{1,3},{2,0},{3,1},{4,6},{5,7},{6,4},{7,5},{8,10},{9,11},{10,... | collective-permute-start | bytes 294920 | tf_op jit(solution)/shard_map/cond/branch_3_fun/ppermute | solution.py:28
  37.8 15.9 %collective-permute-start.23 = (bf16[256,1024]{1,0:T(8,128)(2,1)}, bf16[256,1024]{1,0:T(8,128)(2,1)S(1)}, u32[]{:S(2)}, u32[]{:S(2)}) collective-permute-start(bf16[256,1024]{1,0:T(8,128)(2,1)} %get-tuple-element.146), channel_id=1, source_target_pairs={{0,1},{1,2},{2,3},{3,0},{4,5},{5,6},{6,7},{7,4},{8,9},{9,10},{10,1... | collective-permute-start | bytes 1572872 | tf_op jit(solution)/shard_map/ppermute | solution.py:28
  38.4 24.0 %collective-permute-start.24 = (bf16[256,1024]{1,0:T(8,128)(2,1)}, bf16[256,1024]{1,0:T(8,128)(2,1)S(1)}, u32[]{:S(2)}, u32[]{:S(2)}) collective-permute-start(bf16[256,1024]{1,0:T(8,128)(2,1)} %get-tuple-element.149), channel_id=1, source_target_pairs={{0,3},{1,0},{2,1},{3,2},{4,7},{5,4},{6,5},{7,6},{8,11},{9,8},{10,9... | collective-permute-start | bytes 1572872 | tf_op jit(solution)/shard_map/ppermute | solution.py:28
  41.1 21.3 %copy-start.3 = (bf16[96,1024]{1,0:T(8,128)(2,1)S(1)}, bf16[96,1024]{1,0:T(8,128)(2,1)}, u32[]{:S(2)}) copy-start(bf16[96,1024]{1,0:T(8,128)(2,1)} %get-tuple-element.147.refs_4_) | copy-start | bytes 589828
  41.1 21.2 %copy-start.4 = (bf16[112,1024]{1,0:T(8,128)(2,1)S(1)}, bf16[112,1024]{1,0:T(8,128)(2,1)}, u32[]{:S(2)}) copy-start(bf16[112,1024]{1,0:T(8,128)(2,1)} %get-tuple-element.145.refs_2_) | copy-start | bytes 688132
  41.2 21.2 %copy-start.5 = (bf16[112,1024]{1,0:T(8,128)(2,1)S(1)}, bf16[112,1024]{1,0:T(8,128)(2,1)}, u32[]{:S(2)}) copy-start(bf16[112,1024]{1,0:T(8,128)(2,1)} %get-tuple-element.151.refs_8_) | copy-start | bytes 688132
  41.2 21.2 %copy-start.6 = (bf16[112,1024]{1,0:T(8,128)(2,1)S(1)}, bf16[112,1024]{1,0:T(8,128)(2,1)}, u32[]{:S(2)}) copy-start(bf16[112,1024]{1,0:T(8,128)(2,1)} %get-tuple-element.148.refs_5_) | copy-start | bytes 688132
  66.2 7.0 %collective-permute-start.31 = (bf16[224,256]{1,0:T(8,128)(2,1)S(1)}, bf16[224,256]{1,0:T(8,128)(2,1)S(1)}, u32[]{:S(2)}, u32[]{:S(2)}) collective-permute-start(bf16[224,256]{1,0:T(8,128)(2,1)S(1)} %get-tuple-element.159), channel_id=1, source_target_pairs={{0,1},{1,2},{2,3},{3,0},{4,5},{5,6},{6,7},{7,4},{8,9},{9,10},{10,1... | collective-permute-start | bytes 344072 | tf_op jit(solution)/shard_map/ppermute | solution.py:28
  69.4 11.2 %collective-permute-start.32 = (bf16[224,256]{1,0:T(8,128)(2,1)S(1)}, bf16[224,256]{1,0:T(8,128)(2,1)S(1)}, u32[]{:S(2)}, u32[]{:S(2)}) collective-permute-start(bf16[224,256]{1,0:T(8,128)(2,1)S(1)} %get-tuple-element.160), channel_id=1, source_target_pairs={{0,2},{1,3},{2,0},{3,1},{4,6},{5,7},{6,4},{7,5},{8,10},{9,11},{10,... | collective-permute-start | bytes 344072 | tf_op jit(solution)/shard_map/ppermute | solution.py:28
  70.8 9.8 %collective-permute-start.33 = (bf16[224,256]{1,0:T(8,128)(2,1)S(1)}, bf16[224,256]{1,0:T(8,128)(2,1)S(1)}, u32[]{:S(2)}, u32[]{:S(2)}) collective-permute-start(bf16[224,256]{1,0:T(8,128)(2,1)S(1)} %get-tuple-element.161), channel_id=1, source_target_pairs={{0,3},{1,0},{2,1},{3,2},{4,7},{5,4},{6,5},{7,6},{8,11},{9,8},{10,9... | collective-permute-start | bytes 344072 | tf_op jit(solution)/shard_map/ppermute | solution.py:28
  71.6 16.4 %collective-permute-start.25 = (bf16[224,256]{1,0:T(8,128)(2,1)S(1)}, bf16[224,256]{1,0:T(8,128)(2,1)S(1)}, u32[]{:S(2)}, u32[]{:S(2)}) collective-permute-start(bf16[224,256]{1,0:T(8,128)(2,1)S(1)} %get-tuple-element.154), channel_id=1, source_target_pairs={{0,1},{1,2},{2,3},{3,0},{4,5},{5,6},{6,7},{7,4},{8,9},{9,10},{10,1... | collective-permute-start | bytes 344072 | tf_op jit(solution)/shard_map/ppermute | solution.py:28
  72.3 16.6 %collective-permute-start.26 = (bf16[224,256]{1,0:T(8,128)(2,1)S(1)}, bf16[224,256]{1,0:T(8,128)(2,1)S(1)}, u32[]{:S(2)}, u32[]{:S(2)}) collective-permute-start(bf16[224,256]{1,0:T(8,128)(2,1)S(1)} %get-tuple-element.155), channel_id=1, source_target_pairs={{0,2},{1,3},{2,0},{3,1},{4,6},{5,7},{6,4},{7,5},{8,10},{9,11},{10,... | collective-permute-start | bytes 344072 | tf_op jit(solution)/shard_map/ppermute | solution.py:28
  73.3 15.6 %collective-permute-start.27 = (bf16[224,256]{1,0:T(8,128)(2,1)S(1)}, bf16[224,256]{1,0:T(8,128)(2,1)S(1)}, u32[]{:S(2)}, u32[]{:S(2)}) collective-permute-start(bf16[224,256]{1,0:T(8,128)(2,1)S(1)} %get-tuple-element.156), channel_id=1, source_target_pairs={{0,3},{1,0},{2,1},{3,2},{4,7},{5,4},{6,5},{7,6},{8,11},{9,8},{10,9... | collective-permute-start | bytes 344072 | tf_op jit(solution)/shard_map/ppermute | solution.py:28
  80.7 17.2 %collective-permute-start.36 = (bf16[224,256]{1,0:T(8,128)(2,1)S(1)}, bf16[224,256]{1,0:T(8,128)(2,1)S(1)}, u32[]{:S(2)}, u32[]{:S(2)}) collective-permute-start(bf16[224,256]{1,0:T(8,128)(2,1)S(1)} %add_convert_fusion.refs_0_), channel_id=1, source_target_pairs={{0,3},{1,0},{2,1},{3,2},{4,7},{5,4},{6,5},{7,6},{8,11},{9,8},{10,9... | collective-permute-start | bytes 344072 | tf_op jit(solution)/shard_map/ppermute | solution.py:28
  81.5 21.0 %collective-permute-start.35 = (bf16[224,256]{1,0:T(8,128)(2,1)S(1)}, bf16[224,256]{1,0:T(8,128)(2,1)S(1)}, u32[]{:S(2)}, u32[]{:S(2)}) collective-permute-start(bf16[224,256]{1,0:T(8,128)(2,1)S(1)} %add_convert_fusion.refs_0_), channel_id=1, source_target_pairs={{0,2},{1,3},{2,0},{3,1},{4,6},{5,7},{6,4},{7,5},{8,10},{9,11},{10,... | collective-permute-start | bytes 344072 | tf_op jit(solution)/shard_map/ppermute | solution.py:28
  88.0 14.5 %collective-permute-start.34 = (bf16[224,256]{1,0:T(8,128)(2,1)S(1)}, bf16[224,256]{1,0:T(8,128)(2,1)S(1)}, u32[]{:S(2)}, u32[]{:S(2)}) collective-permute-start(bf16[224,256]{1,0:T(8,128)(2,1)S(1)} %add_convert_fusion.refs_0_), channel_id=1, source_target_pairs={{0,1},{1,2},{2,3},{3,0},{4,5},{5,6},{6,7},{7,4},{8,9},{9,10},{10,1... | collective-permute-start | bytes 344072 | tf_op jit(solution)/shard_map/ppermute | solution.py:28
  89.0 19.1 %collective-permute-start.30 = (bf16[224,256]{1,0:T(8,128)(2,1)S(1)}, bf16[224,256]{1,0:T(8,128)(2,1)S(1)}, u32[]{:S(2)}, u32[]{:S(2)}) collective-permute-start(bf16[224,256]{1,0:T(8,128)(2,1)S(1)} %add_convert_fusion.1.refs_0_), channel_id=1, source_target_pairs={{0,3},{1,0},{2,1},{3,2},{4,7},{5,4},{6,5},{7,6},{8,11},{9,8},{10,9... | collective-permute-start | bytes 344072 | tf_op jit(solution)/shard_map/ppermute | solution.py:28
  96.5 14.6 %collective-permute-start.29 = (bf16[224,256]{1,0:T(8,128)(2,1)S(1)}, bf16[224,256]{1,0:T(8,128)(2,1)S(1)}, u32[]{:S(2)}, u32[]{:S(2)}) collective-permute-start(bf16[224,256]{1,0:T(8,128)(2,1)S(1)} %add_convert_fusion.1.refs_0_), channel_id=1, source_target_pairs={{0,2},{1,3},{2,0},{3,1},{4,6},{5,7},{6,4},{7,5},{8,10},{9,11},{10,... | collective-permute-start | bytes 344072 | tf_op jit(solution)/shard_map/ppermute | solution.py:28
  97.9 13.2 %collective-permute-start.28 = (bf16[224,256]{1,0:T(8,128)(2,1)S(1)}, bf16[224,256]{1,0:T(8,128)(2,1)S(1)}, u32[]{:S(2)}, u32[]{:S(2)}) collective-permute-start(bf16[224,256]{1,0:T(8,128)(2,1)S(1)} %add_convert_fusion.1.refs_0_), channel_id=1, source_target_pairs={{0,1},{1,2},{2,3},{3,0},{4,5},{5,6},{6,7},{7,4},{8,9},{9,10},{10,1... | collective-permute-start | bytes 344072 | tf_op jit(solution)/shard_map/ppermute | solution.py:28
  103.8 16.0 %collective-permute-start.42 = (bf16[1024,256]{1,0:T(8,128)(2,1)S(1)}, bf16[1024,256]{1,0:T(8,128)(2,1)S(1)}, u32[]{:S(2)}, u32[]{:S(2)}) collective-permute-start(bf16[1024,256]{1,0:T(8,128)(2,1)S(1)} %get-tuple-element.167), channel_id=1, source_target_pairs={{0,4},{4,0},{8,12},{12,8},{16,20},{20,16},{24,28},{28,24},{1,5},{5... | collective-permute-start | bytes 1572872 | tf_op jit(solution)/shard_map/ppermute | solution.py:22
  112.4 7.5 %collective-permute-start.41 = (bf16[1024,256]{1,0:T(8,128)(2,1)S(1)}, bf16[1024,256]{1,0:T(8,128)(2,1)S(1)}, u32[]{:S(2)}, u32[]{:S(2)}) collective-permute-start(bf16[1024,256]{1,0:T(8,128)(2,1)S(1)} %get-tuple-element.166), channel_id=1, source_target_pairs={{0,4},{4,0},{8,12},{12,8},{16,20},{20,16},{24,28},{28,24},{1,5},{5... | collective-permute-start | bytes 1572872 | tf_op jit(solution)/shard_map/ppermute | solution.py:22
  112.9 2.5 %collective-permute-start.39 = (f32[8,128]{1,0:T(8,128)S(1)}, f32[8,128]{1,0:T(8,128)S(1)}, u32[]{:S(2)}, u32[]{:S(2)}) collective-permute-start(f32[8,128]{1,0:T(8,128)S(1)} %add.66), channel_id=1, source_target_pairs={{0,3},{1,0},{2,1},{3,2},{4,7},{5,4},{6,5},{7,6},{8,11},{9,8},{10,9... | collective-permute-start | bytes 12296 | tf_op jit(solution)/shard_map/ppermute | solution.py:28
  112.9 3.4 %collective-permute-start.38 = (f32[8,128]{1,0:T(8,128)S(1)}, f32[8,128]{1,0:T(8,128)S(1)}, u32[]{:S(2)}, u32[]{:S(2)}) collective-permute-start(f32[8,128]{1,0:T(8,128)S(1)} %add.66), channel_id=1, source_target_pairs={{0,2},{1,3},{2,0},{3,1},{4,6},{5,7},{6,4},{7,5},{8,10},{9,11},{10,... | collective-permute-start | bytes 12296 | tf_op jit(solution)/shard_map/ppermute | solution.py:28
  113.0 4.5 %collective-permute-start.37 = (f32[8,128]{1,0:T(8,128)S(1)}, f32[8,128]{1,0:T(8,128)S(1)}, u32[]{:S(2)}, u32[]{:S(2)}) collective-permute-start(f32[8,128]{1,0:T(8,128)S(1)} %add.66), channel_id=1, source_target_pairs={{0,1},{1,2},{2,3},{3,0},{4,5},{5,6},{6,7},{7,4},{8,9},{9,10},{10,1... | collective-permute-start | bytes 12296 | tf_op jit(solution)/shard_map/ppermute | solution.py:28
  117.5 2.3 %collective-permute-start.40 = (f32[8,128]{1,0:T(8,128)S(1)}, f32[8,128]{1,0:T(8,128)S(1)}, u32[]{:S(2)}, u32[]{:S(2)}) collective-permute-start(f32[8,128]{1,0:T(8,128)S(1)} %add_add_fusion.own_ref), channel_id=1, source_target_pairs={{0,4},{4,0},{8,12},{12,8},{16,20},{20,16},{24,28},{28,24},{1,5},{5... | collective-permute-start | bytes 12296 | tf_op jit(solution)/shard_map/ppermute | solution.py:22
where the time goes:
time: 124 us; the launch traced here: 122 us
  waiting for transfers between devices  50.1 us (40%)
  starting transfers between devices  43.2 us (35%)
  Pallas kernels  23.1 us (19%)
  local copies, waits for them, and re-layouts  3.32 us (3%)
  between operations  1.56 us (1%)
    ppermute x21, waiting for transfers between devices, turned(): return lax.ppermute(value, 'fsdp', ring)  49.2 us
    ppermute x21, starting transfers between devices, turned(): return lax.ppermute(value, 'fsdp', ring)  36.2 us
    pallas_call x2, Pallas kernels, sent_to(): pl.pallas_call(functools.partial(sent_kernel, members, offsets, sizes), i...  9.55 us
    ppermute x4, starting transfers between devices, swapped(): return lax.ppermute(value, axis, pairs)  7.02 us
    pallas_call x1, Pallas kernels, local(): pl.pallas_call(functools.partial(own_kernel, members), in_specs=[smem, an...  4.99 us
    pallas_call x1, Pallas kernels, local(): pl.pallas_call(functools.partial(keys_kernel, members, offsets, scale), i...  3.84 us
    pallas_call x2, Pallas kernels, local(): pl.pallas_call(functools.partial(gradient_kernel, members), in_specs=[vme...  2.56 us
  transfers between devices with their start and end apart: 25, of which 13 were waited for; matrix products, arithmetic and copies ran while one was open for 3% of the time, Pallas kernels for 15%

commit v1 on v0

v1 whole, which is shorter than its diff:
```python
import functools

import jax
import jax.numpy as jnp
from jax import lax
from jax.experimental import pallas as pl
from jax.experimental.pallas import tpu as pltpu
from jax.sharding import PartitionSpec as P

SLOT = 64
STEP = 3
ALIGN = 16
HALVES = 2

learning_rate = 0.1
epsilon = 1e-06


def swapped(value, axis, bit):
    mask = 2**bit
    pairs = [(source, source ^ mask) for source in range(lax.axis_size(axis))]
    return lax.ppermute(value, axis, pairs)


def turned(value, distance):
    members = lax.axis_size("fsdp")
    ring = [(source, (source + distance) % members) for source in range(members)]
    return lax.ppermute(value, "fsdp", ring)


def live_before(lengths_ref, members):
    sequences = lengths_ref.shape[1] // members
    totals = [jnp.int32(0)]
    for member in range(members):
        total = totals[-1]
        for q in range(sequences):
            total = total + lengths_ref[0, member * sequences + q]
        totals.append(total)
    return totals


def chosen(values, index):
    value = values[0]
    for i in range(1, len(values)):
        value = jnp.where(index == i, values[i], value)
    return value


def aligned(place):
    return pl.multiple_of(place // ALIGN * ALIGN, ALIGN)


def token_places(lengths_ref, member, before, tokens):
    sequences = tokens // SLOT
    place = before % ALIGN
    slot = lax.broadcasted_iota(jnp.int32, (1, tokens), 1)
    places = jnp.full((1, tokens), -1, jnp.int32)
    for s in range(sequences):
        length = lengths_ref[0, member * sequences + s]
        position = slot - s * SLOT
        places = jnp.where((position >= 0) & (position < length), position + place, places)
        place = place + length
    return places


def picking(places, start, rows):
    row = lax.broadcasted_iota(jnp.int32, (rows, places.shape[1]), 0) + start
    return jnp.where(row == places, 1.0, 0.0).astype(jnp.bfloat16)


class Block:
    def __init__(self, features_ref, member, block_ref, sems):
        self.block_ref, self.width = block_ref, block_ref.shape[1] // sems.shape[0]
        start = member * block_ref.shape[1]
        self.copies = []
        for j in range(sems.shape[0]):
            there = pl.ds(pl.multiple_of(start + j * self.width, 128), self.width)
            here = pl.ds(j * self.width, self.width)
            copy = pltpu.make_async_copy(
                features_ref.at[:, there], block_ref.at[:, here], sems.at[j]
            )
            copy.start()
            self.copies.append(copy)

    def picked(self, pick, store, wait):
        for j, copy in enumerate(self.copies):
            if wait:
                copy.wait()
            here = slice(j * self.width, (j + 1) * self.width)
            rows = jnp.dot(pick, self.block_ref[:, here], preferred_element_type=jnp.float32)
            store(here, rows.astype(jnp.bfloat16))


def used_places(totals, first, sizes):
    choices = []
    for member in range(len(totals) - 1):
        used = totals[member + 1] - aligned(totals[member])
        choice = jnp.int32(0)
        for size in sizes[:-1]:
            choice = choice + jnp.where(used > first + size, 1, 0)
        choices.append(choice)
    return choices


def sent_kernel(members, offsets, sizes, lengths_ref, features_ref, *refs):
    count = len(offsets)
    outs, choice_ref = refs[: 2 * count], refs[2 * count]
    block_ref, first_ref, more_ref, sems, out_sems, more_sems = refs[2 * count + 1 :]
    index = lax.axis_index("fsdp")
    blocks = [
        Block(features_ref, lax.rem(index + i, members), block_ref.at[n], sems.at[n])
        for n, i in enumerate(offsets)
    ]
    totals = live_before(lengths_ref, members)
    before, end = chosen(totals[:-1], index), chosen(totals[1:], index)
    places = token_places(lengths_ref, index, before, block_ref.shape[1])
    first, more = first_ref.shape[1], more_ref.shape[1]
    pick = picking(places, 0, first)
    copies = []
    for n, block in enumerate(blocks):

        def store(here, rows, n=n):
            first_ref[n, :, here] = rows
            copy = pltpu.make_async_copy(
                first_ref.at[n, :, here],
                outs[n].at[:, here],
                out_sems.at[n, here.start // (here.stop - here.start)],
            )
            copy.start()
            copies.append(copy)

        block.picked(pick, store, True)

    @pl.when(end - aligned(before) > first)
    def _():
        further = picking(places, first, more)
        for n, block in enumerate(blocks):

            def store(here, rows, n=n):
                more_ref[n, :, here] = rows

            block.picked(further, store, False)
            copy = pltpu.make_async_copy(more_ref.at[n], outs[count + n], more_sems.at[n])
            copy.start()
            copy.wait()

    for member, choice in enumerate(used_places(totals, first, sizes)):
        choice_ref[member] = choice
    for copy in copies:
        copy.wait()


def own_kernel(
    members,
    far,
    scale,
    lengths_ref,
    features_ref,
    targets_ref,
    master_ref,
    partner_ref,
    far_ref,
    *refs,
):
    held_more = refs[:members]
    rows_ref, keys_ref, low_ref, halves_ref = refs[members : members + 4]
    block_ref, first_ref, more_ref, sems, first_sem, more_sems = refs[members + 4 :]
    index = lax.axis_index("fsdp")
    block = Block(features_ref, index, block_ref, sems)
    far_copy = pltpu.make_async_copy(far_ref, first_ref, first_sem)
    far_copy.start()
    rows_ref[...] = jnp.zeros_like(rows_ref)
    low_ref[...] = master_ref[...].astype(jnp.bfloat16)
    halves_ref[...] = 0.5 * (master_ref[...] + partner_ref[...])
    totals = live_before(lengths_ref, members)
    before = chosen(totals[:-1], index)
    first, more = first_ref.shape[0], more_ref.shape[0]
    places = token_places(lengths_ref, index, before, block_ref.shape[0])
    pick = picking(places, 0, first + more)

    def store(here, rows):
        rows_ref[pl.ds(aligned(before), first + more), here] = rows

    block.picked(pick, store, True)
    far_start = aligned(chosen(totals[:-1], lax.rem(index + members - far, members)))
    far_copy.wait()
    rows_ref[pl.ds(far_start, first)] += first_ref[...]
    for member in range(members):
        start = aligned(totals[member])
        used = totals[member + 1] - start

        @pl.when((member != index) & (used > first))
        def _(member=member, start=start, used=used):
            copy = pltpu.make_async_copy(held_more[member], more_ref, more_sems.at[member])
            copy.start()
            copy.wait()
            for k in range(0, more, ALIGN):

                @pl.when(used > first + k)
                def _(k=k):
                    rows_ref[pl.ds(start + first + k, ALIGN)] += more_ref[k : k + ALIGN]

    height = (rows_ref.shape[0] - first - more) // members

    @pl.loop(0, members)
    def _(j):
        here = pl.ds(pl.multiple_of(j * height, ALIGN), height)
        keys_ref[here] = (
            jnp.dot(rows_ref[here], low_ref[...], preferred_element_type=jnp.float32) * scale
        )

    keys_ref[pl.ds(aligned(before), first + more)] -= jnp.dot(
        pick, targets_ref[...], preferred_element_type=jnp.float32
    )


def keys_kernel(members, near, scale, lengths_ref, low_ref, keys_ref, *refs):
    blocks, sums, total_ref = refs[: len(near)], refs[len(near) : -1], refs[-1]
    del keys_ref
    index = lax.axis_index("fsdp")
    totals = live_before(lengths_ref, members)
    for i, block_ref in zip(near, blocks):
        start = aligned(chosen(totals[:-1], lax.rem(index + members - i, members)))
        total_ref[pl.ds(start, block_ref.shape[0])] += (
            jnp.dot(block_ref[...], low_ref[...], preferred_element_type=jnp.float32) * scale
        )
    share, width = sums[0].shape
    for half in range(HALVES):
        for i in range(members):
            owner = lax.rem(index + i, members)
            rows = pl.ds(pl.multiple_of(owner * share, ALIGN), share)
            out_ref = sums[half * members + i]
            here = slice(half * width, (half + 1) * width)
            out_ref[...] = total_ref[rows, here].astype(out_ref.dtype)


def turn_kernel(members, near, lengths_ref, rows_ref, *refs):
    blocks, (turned_ref, all_ref) = refs[: len(near)], refs[len(near) :]
    index = lax.axis_index("fsdp")
    totals = live_before(lengths_ref, members)
    all_ref[...] = rows_ref[...]
    for i, block_ref in zip(near, blocks):
        start = aligned(chosen(totals[:-1], lax.rem(index + members - i, members)))
        all_ref[pl.ds(start, block_ref.shape[0])] += block_ref[...]
    for start in range(0, turned_ref.shape[1], 128):
        turned_ref[:, start : start + 128] = all_ref[start : start + 128, :].T


def gradient_kernel(members, turned_ref, *refs):
    residuals, (gradient_ref, low_ref, squares_ref, all_ref) = refs[:members], refs[members:]
    index = lax.axis_index("fsdp")
    share = residuals[0].shape[0]
    for i in range(members):
        owner = lax.rem(index + members - i, members)
        all_ref[pl.ds(pl.multiple_of(owner * share, ALIGN), share)] = residuals[i][...]
    squares_ref[...] = jnp.zeros_like(squares_ref)
    height = min(256, turned_ref.shape[0])

    @pl.loop(0, turned_ref.shape[0] // height)
    def _(j):
        rows = pl.ds(pl.multiple_of(j * height, height), height)
        gradient = jnp.dot(turned_ref[rows], all_ref[...], preferred_element_type=jnp.float32)
        gradient_ref[rows] = gradient
        low_ref[rows] = gradient.astype(low_ref.dtype)
        squares = jnp.sum((gradient * gradient).reshape(-1, 8, gradient.shape[1]), axis=0)
        lanes = squares.shape[1] // 128
        squares_ref[...] += sum(squares[:, 128 * k : 128 * (k + 1)] for k in range(lanes))


def average_kernel(entries, own_ref, other_ref, halves_ref, *refs):
    gradients, partners, (out_ref, done_ref, sems) = refs[:HALVES], refs[HALVES:-3], refs[-3:]
    rate = 0.5 * learning_rate
    own = rate * lax.rsqrt(jnp.sum(own_ref[...], keepdims=True) / entries + epsilon)
    other = rate * lax.rsqrt(jnp.sum(other_ref[...], keepdims=True) / entries + epsilon)
    pieces = sems.shape[0]
    height = done_ref.shape[0] // pieces
    width = done_ref.shape[1] // HALVES
    copies = []
    for j in range(pieces):
        rows = pl.ds(j * height, height)
        for half in range(HALVES):
            here = slice(half * width, (half + 1) * width)
            done_ref[rows, here] = (
                halves_ref[rows, here]
                - gradients[half][rows] * own
                - partners[half][rows].astype(jnp.float32) * other
            )
        copies.append(pltpu.make_async_copy(done_ref.at[rows], out_ref.at[rows], sems.at[j]))
        copies[-1].start()
    for copy in copies:
        copy.wait()


def more_rows(size, source, offsets, blocks):
    if size == 0:
        return blocks[0]
    members = lax.axis_size("fsdp")
    moved = [
        lax.ppermute(block[:size], "fsdp", [(source, (source + i) % members)])
        for i, block in zip(offsets, blocks)
    ]
    return jnp.pad(sum(moved[1:], moved[0]), ((0, blocks[0].shape[0] - size), (0, 0)))


def local(activations, targets, weights, lengths):
    features = activations[0]
    wanted = targets[0]
    master = weights[0]
    tokens_here = features.shape[0]
    local_rows, columns = master.shape
    members = lax.axis_size("fsdp")
    distance_bit = STEP % (lax.axis_size("replica").bit_length() - 1)
    share = tokens_here // 2
    first = -(-(share + 32) // ALIGN) * ALIGN
    more = -(-(tokens_here + ALIGN - first) // ALIGN) * ALIGN
    steps = (16, 32, 48, 64, 80, 96, 128) if members <= 4 else (96,)
    sizes = [0] + [size for size in steps if size < more] + [more]
    most = first + more
    scale = features.shape[1] ** (-0.5)
    places = members * share + most

    vmem = pl.BlockSpec(memory_space=pltpu.VMEM)
    anywhere = pl.BlockSpec(memory_space=pl.ANY)
    smem = pl.BlockSpec(memory_space=pltpu.SMEM)
    params = pltpu.CompilerParams(vmem_limit_bytes=40 * 2**20)
    large = pltpu.CompilerParams(vmem_limit_bytes=56 * 2**20)

    def array(rows, width, dtype):
        return jax.ShapeDtypeStruct((rows, width), dtype)

    def cost(flops, moved):
        return pl.CostEstimate(flops=flops, bytes_accessed=moved, transcendentals=0)

    def sent_to(offsets):
        count = len(offsets)
        pieces = max(1, local_rows // 256)
        *arrays, choice = pl.pallas_call(
            functools.partial(sent_kernel, members, offsets, sizes),
            in_specs=[smem, anywhere],
            out_specs=[anywhere] * (2 * count) + [smem],
            out_shape=[
                array(rows, local_rows, jnp.bfloat16) for rows in (first, more) for _ in offsets
            ]
            + [jax.ShapeDtypeStruct((members,), jnp.int32)],
            scratch_shapes=[
                pltpu.VMEM((count, tokens_here, local_rows), jnp.bfloat16),
                pltpu.VMEM((count, first, local_rows), jnp.bfloat16),
                pltpu.VMEM((count, more, local_rows), jnp.bfloat16),
                pltpu.SemaphoreType.DMA((count, pieces)),
                pltpu.SemaphoreType.DMA((count, pieces)),
                pltpu.SemaphoreType.DMA((count,)),
            ],
            compiler_params=large,
            cost_estimate=cost(
                2 * count * first * tokens_here * local_rows,
                2 * count * (tokens_here + first) * local_rows,
            ),
        )(lengths, features)
        return arrays[:count], arrays[count:], choice

    far = members // 2
    near = [i for i in range(1, members) if i != far]
    far_first, far_more, choice = sent_to([far])
    near_first, near_more, _ = sent_to(near)
    held_far = turned(far_first[0], far)
    offsets = [far] + near
    held_more = [
        lax.switch(
            choice[source],
            [functools.partial(more_rows, size, source, offsets) for size in sizes],
            far_more + near_more,
        )
        for source in range(members)
    ]
    near_first, held_more, late_lengths = lax.optimization_barrier((near_first, held_more, lengths))
    held = [turned(block, i) for i, block in zip(near, near_first)]

    partner_master = swapped(master, "replica", distance_bit)
    rows, keys, low, halves = pl.pallas_call(
        functools.partial(own_kernel, members, far, scale),
        in_specs=[smem, anywhere, vmem, vmem, vmem, anywhere] + [anywhere] * members,
        out_specs=[vmem] * 4,
        out_shape=[
            array(places, local_rows, jnp.bfloat16),
            array(places, columns, jnp.float32),
            array(local_rows, columns, jnp.bfloat16),
            array(local_rows, columns, jnp.float32),
        ],
        scratch_shapes=[
            pltpu.VMEM((tokens_here, local_rows), jnp.bfloat16),
            pltpu.VMEM((first, local_rows), jnp.bfloat16),
            pltpu.VMEM((more, local_rows), jnp.bfloat16),
            pltpu.SemaphoreType.DMA((max(1, local_rows // 256),)),
            pltpu.SemaphoreType.DMA,
            pltpu.SemaphoreType.DMA((members,)),
        ],
        compiler_params=params,
        cost_estimate=cost(
            2 * (most * tokens_here + members * share * columns) * (local_rows + columns),
            20 * local_rows * columns,
        ),
    )(late_lengths, features, wanted, master, partner_master, held_far, *held_more)

    width = columns // HALVES
    sum_shapes = [array(share, width, jnp.bfloat16 if i else jnp.float32) for i in range(members)]
    *sums, _ = pl.pallas_call(
        functools.partial(keys_kernel, members, near, scale),
        in_specs=[smem, vmem, vmem] + [vmem] * len(near),
        out_specs=[vmem] * (HALVES * members + 1),
        out_shape=sum_shapes * HALVES + [array(places, columns, jnp.float32)],
        input_output_aliases={2: HALVES * members},
        compiler_params=params,
        cost_estimate=cost(
            2 * len(near) * first * local_rows * columns, 8 * places * columns
        ),
    )(lengths, low, keys, *held)
    sums = [sums[half * members : (half + 1) * members] for half in range(HALVES)]

    turned_rows = pl.pallas_call(
        functools.partial(turn_kernel, members, near),
        in_specs=[smem, vmem] + [vmem] * len(near),
        out_specs=vmem,
        out_shape=array(local_rows, members * share, jnp.bfloat16),
        scratch_shapes=[pltpu.VMEM((places, local_rows), jnp.bfloat16)],
        compiler_params=params,
        cost_estimate=cost(0, 4 * members * share * local_rows),
    )(lengths, rows, *held)

    gradients, partners, squares = [], [], 0.0
    for half in range(HALVES):
        residual = sums[half][0]
        for i in range(1, members):
            residual = residual + turned(sums[half][i], i).astype(jnp.float32)
        residual = residual.astype(jnp.bfloat16)
        residuals = [residual] + [turned(residual, i) for i in range(1, members)]
        gradient, low_gradient, own_squares = pl.pallas_call(
            functools.partial(gradient_kernel, members),
            in_specs=[vmem] + [vmem] * members,
            out_specs=[vmem] * 3,
            out_shape=[
                array(local_rows, width, jnp.float32),
                array(local_rows, width, jnp.bfloat16),
                array(8, 128, jnp.float32),
            ],
            scratch_shapes=[pltpu.VMEM((members * share, width), jnp.bfloat16)],
            compiler_params=params,
            cost_estimate=cost(
                2 * members * share * local_rows * width, 8 * local_rows * width
            ),
        )(turned_rows, *residuals)
        gradients.append(gradient)
        partners.append(swapped(low_gradient, "replica", distance_bit))
        squares = squares + own_squares

    total = squares
    for i in range(1, members):
        total = total + turned(squares, i)
    partner_total = swapped(total, "replica", distance_bit)

    averaged = pl.pallas_call(
        functools.partial(average_kernel, members * local_rows * columns),
        in_specs=[vmem] * (3 + 2 * HALVES),
        out_specs=anywhere,
        out_shape=array(local_rows, columns, jnp.float32),
        scratch_shapes=[
            pltpu.VMEM((local_rows, columns), jnp.float32),
            pltpu.SemaphoreType.DMA((4,)),
        ],
        compiler_params=params,
    )(total, partner_total, halves, *gradients, *partners)
    return averaged[None]


def solution(mesh):
    return jax.shard_map(
        local,
        mesh=mesh,
        in_specs=(
            P("replica", "fsdp", None),
            P("replica", "fsdp", None),
            P("replica", "fsdp", None),
            P("replica", None),
        ),
        out_specs=P("replica", "fsdp", None),
        check_vma=False,
    )
```

time: 124 us -> 117 us (0.944); the launches traced: 122 us -> 118 us
  waiting for transfers between devices: 50.1 us -> 44.8 us
  starting transfers between devices: 43.2 us -> 41.1 us
  Pallas kernels: 23.1 us -> 24.6 us
  between operations: 1.56 us -> 2.95 us
    ppermute x21 -> x18, waiting for transfers between devices: 49.2 us -> 19 us  [turned(): return lax.ppermute(value, 'fsdp', ring)]
    ppermute x0 -> x6, waiting for transfers between devices: none -> 25 us  [more_rows(): lax.ppermute(block[:size], 'fsdp', [(source, (source + i) % members)])]
    ppermute x0 -> x6, starting transfers between devices: none -> 5.22 us  [more_rows(): lax.ppermute(block[:size], 'fsdp', [(source, (source + i) % members)])]
    ppermute x4, starting transfers between devices: 7.02 us -> 2.88 us  [swapped(): return lax.ppermute(value, axis, pairs)]
    ppermute x21 -> x18, starting transfers between devices: 36.2 us -> 33 us  [turned(): return lax.ppermute(value, 'fsdp', ring)]
    unnamed x14 -> x16, local copies, waits for them, and re-layouts: 0.04 us -> 2.43 us
    pallas_call x3, Pallas kernels: 9.35 us -> 11.1 us  [the longest x1 8.41 us: local(): pl.pallas_call(functools.partial(own_kernel, members, far, scale), in_spe...]
    slice x4 -> x7, local copies, waits for them, and re-layouts: 2.57 us -> 1.47 us  [the longest x1 1.44 us: local(): choice[source]]
  transfers between devices with their start and end apart: 25 -> 28, of which waited for: 13 -> 11; matrix products, arithmetic and copies ran while one was open for 3% -> 1% of each run, Pallas kernels for 15% -> 18%
where the time goes in v1:
time: 117 us; the launch traced here: 118 us
  waiting for transfers between devices  44.8 us (38%)
  starting transfers between devices  41.1 us (35%)
  Pallas kernels  24.6 us (21%)
  local copies, waits for them, and re-layouts  4.01 us (3%)
  between operations  2.95 us (3%)
    ppermute x18, starting transfers between devices, turned(): return lax.ppermute(value, 'fsdp', ring)  33 us
    ppermute x6, waiting for transfers between devices, more_rows(): lax.ppermute(block[:size], 'fsdp', [(source, (source + i) % members)])  25 us
    ppermute x18, waiting for transfers between devices, turned(): return lax.ppermute(value, 'fsdp', ring)  19 us
    pallas_call x2, Pallas kernels, sent_to(): pl.pallas_call(functools.partial(sent_kernel, members, offsets, sizes), i...  9.26 us
    pallas_call x1, Pallas kernels, local(): pl.pallas_call(functools.partial(own_kernel, members, far, scale), in_spe...  8.41 us
    ppermute x6, starting transfers between devices, more_rows(): lax.ppermute(block[:size], 'fsdp', [(source, (source + i) % members)])  5.22 us
    ppermute x4, starting transfers between devices, swapped(): return lax.ppermute(value, axis, pairs)  2.88 us
    pallas_call x2, Pallas kernels, local(): pl.pallas_call(functools.partial(gradient_kernel, members), in_specs=[vme...  2.54 us
  transfers between devices with their start and end apart: 28, of which 11 were waited for; matrix products, arithmetic and copies ran while one was open for 1% of the time, Pallas kernels for 18%

profile of v1, /device:TPU:7, one launch (start us, length us, event | category | flops | bytes accessed | tf_op | source)
XLA Modules:
  0.0 117.8 jit_solution(16169497152188769315)
XLA Ops:
  0.7 4.0 %shard_map.47 = (bf16[256,1024]{1,0:T(8,128)(2,1)}, bf16[208,1024]{1,0:T(8,128)(2,1)S(1)}, s32[4]{0:T(128)}) custom-call(s32[1,28]{1,0:T(1,128)} %lengths_ref.8, bf16[448,4096]{1,0:T(8,128)(2,1)} %bitcast.11), custom_call_target="tpu_custom_call" | custom-call | flops 234881024 | bytes 1441792 | tf_op jit(solution)/shard_map/pallas_call | solution.py:337
  4.7 2.4 %collective-permute-start.97 = (bf16[256,1024]{1,0:T(8,128)(2,1)}, bf16[256,1024]{1,0:T(8,128)(2,1)S(1)}, u32[]{:S(2)}, u32[]{:S(2)}) collective-permute-start(bf16[256,1024]{1,0:T(8,128)(2,1)} %get-tuple-element.376), channel_id=1, source_target_pairs={{0,2},{1,3},{2,0},{3,1},{4,6},{5,7},{6,4},{7,5},{8,10},{9,11},{10,... | collective-permute-start | bytes 1572872 | tf_op jit(solution)/shard_map/ppermute | solution.py:28
  7.1 1.4 %fusion = (s32[1]{0:T(128)}, s32[1]{0:T(128)}, s32[1]{0:T(128)}, s32[1]{0:T(128)}) fusion(s32[4]{0:T(128)} %get-tuple-element.371), kind=kLoop, calls=%fused_computation.35 | loop fusion | bytes 32 | tf_op jit(solution)/shard_map/slice | solution.py:369
  11.1 5.3 %shard_map.46 = (bf16[256,1024]{1,0:T(8,128)(2,1)}, bf16[256,1024]{1,0:T(8,128)(2,1)}, bf16[208,1024]{1,0:T(8,128)(2,1)S(1)}, bf16[208,1024]{1,0:T(8,128)(2,1)S(1)}, s32[4]{0:T(128)}) custom-call(s32[1,28]{1,0:T(1,128)} %lengths_ref.8, bf16[448,4096]{1,0:T(8,128)(2,1)} %bitcast.12), custom_call_target="tpu_custom_call" | custom-call | flops 469762048 | bytes 2883584 | tf_op jit(solution)/shard_map/pallas_call | solution.py:337
  17.4 25.8 %conditional.6 = (bf16[208,1024]{1,0:T(8,128)(2,1)S(1)}) conditional(s32[]{:T(128)} %bitcast.3, bf16[208,1024]{1,0:T(8,128)(2,1)S(1)} %get-tuple-element.372, (bf16[208,1024]{1,0:T(8,128)(2,1)S(1)}, bf16[208,1024]{1,0:T(8,128)(2,1)S(1)}, bf16[208,1024]{1,0:T(8,128)(2,1)S(1)}) %tuple.114, ...), branch_computations={%region_18.19_spmd, %region_19.20_spmd, %region_20.21_spmd, %regio... | conditional | flops 425984 | bytes 6815872 | solution.py:368
  18.7 1.3 %collective-permute-start.51 = (bf16[32,1024]{1,0:T(8,128)(2,1)S(1)}, bf16[32,1024]{1,0:T(8,128)(2,1)S(1)}, u32[]{:S(2)}, u32[]{:S(2)}) collective-permute-start(bf16[32,1024]{1,0:T(8,128)(2,1)S(1)} %slice.221), channel_id=1, source_target_pairs={{2,0},{6,4},{10,8},{14,12},{18,16},{22,20},{26,24},{30,28}} | collective-permute-start | bytes 196616 | tf_op jit(solution)/shard_map/cond/branch_2_fun/ppermute | solution.py:299
  20.1 23.0 %collective-permute-done.51 = bf16[32,1024]{1,0:T(8,128)(2,1)S(1)} collective-permute-done((bf16[32,1024]{1,0:T(8,128)(2,1)S(1)}, bf16[32,1024]{1,0:T(8,128)(2,1)S(1)}, u32[]{:S(2)}, u32[]{:S(2)}) %collective-permute-start.51) | collective-permute-done | bytes 65568 | tf_op jit(solution)/shard_map/cond/branch_2_fun/ppermute | solution.py:299
  43.9 4.7 %conditional.5 = (bf16[208,1024]{1,0:T(8,128)(2,1)S(1)}) conditional(s32[]{:T(128)} %bitcast.2, bf16[208,1024]{1,0:T(8,128)(2,1)S(1)} %get-tuple-element.372, (bf16[208,1024]{1,0:T(8,128)(2,1)S(1)}, bf16[208,1024]{1,0:T(8,128)(2,1)S(1)}, bf16[208,1024]{1,0:T(8,128)(2,1)S(1)}) %tuple.114, ...), branch_computations={%region_9.10_spmd, %region_10.11_spmd, %region_11.12_spmd, %region... | conditional | flops 425984 | bytes 6815872 | solution.py:368
  43.9 1.3 %collective-permute-start.26 = (bf16[16,1024]{1,0:T(8,128)(2,1)S(1)}, bf16[16,1024]{1,0:T(8,128)(2,1)S(1)}, u32[]{:S(2)}, u32[]{:S(2)}) collective-permute-start(bf16[16,1024]{1,0:T(8,128)(2,1)S(1)} %slice.199), channel_id=1, source_target_pairs={{1,0},{5,4},{9,8},{13,12},{17,16},{21,20},{25,24},{29,28}} | collective-permute-start | bytes 98312 | tf_op jit(solution)/shard_map/cond/branch_1_fun/ppermute | solution.py:299
  46.6 2.0 %collective-permute-done.26 = bf16[16,1024]{1,0:T(8,128)(2,1)S(1)} collective-permute-done((bf16[16,1024]{1,0:T(8,128)(2,1)S(1)}, bf16[16,1024]{1,0:T(8,128)(2,1)S(1)}, u32[]{:S(2)}, u32[]{:S(2)}) %collective-permute-start.26) | collective-permute-done | bytes 32800 | tf_op jit(solution)/shard_map/cond/branch_1_fun/ppermute | solution.py:299
  49.4 2.4 %collective-permute-start.98 = (bf16[256,1024]{1,0:T(8,128)(2,1)}, bf16[256,1024]{1,0:T(8,128)(2,1)S(1)}, u32[]{:S(2)}, u32[]{:S(2)}) collective-permute-start(bf16[256,1024]{1,0:T(8,128)(2,1)} %get-tuple-element.382), channel_id=1, source_target_pairs={{0,1},{1,2},{2,3},{3,0},{4,5},{5,6},{6,7},{7,4},{8,9},{9,10},{10,1... | collective-permute-start | bytes 1572872 | tf_op jit(solution)/shard_map/ppermute | solution.py:28
  51.8 2.5 %collective-permute-start.99 = (bf16[256,1024]{1,0:T(8,128)(2,1)}, bf16[256,1024]{1,0:T(8,128)(2,1)S(1)}, u32[]{:S(2)}, u32[]{:S(2)}) collective-permute-start(bf16[256,1024]{1,0:T(8,128)(2,1)} %get-tuple-element.383), channel_id=1, source_target_pairs={{0,3},{1,0},{2,1},{3,2},{4,7},{5,4},{6,5},{7,6},{8,11},{9,8},{10,9... | collective-permute-start | bytes 1572872 | tf_op jit(solution)/shard_map/ppermute | solution.py:28
  54.3 8.4 %shard_map.48 = (bf16[1360,1024]{1,0:T(8,128)(2,1)S(1)}, f32[1360,512]{1,0:T(8,128)S(1)}, bf16[1024,512]{1,0:T(8,128)(2,1)S(1)}, f32[1024,512]{1,0:T(8,128)S(1)}) custom-call(s32[1,28]{1,0:T(1,128)S(1)} %copy-done.2, bf16[448,4096]{1,0:T(8,128)(2,1)} %bitcast.13, bf16[448,512]{1,0:T(8,128)(2,1)S(1)} %bitcast.10, f32[1024,512]{1,0:T(8,128)S(1)} %bitcast.9, ...), custom_call_target="tpu_custom_call" | custom-call | flops 2047868928 | bytes 10485760 | tf_op jit(solution)/shard_map/pallas_call | solution.py:379
  62.8 4.0 %collective-permute-done.98.refs_0_ = bf16[256,1024]{1,0:T(8,128)(2,1)S(1)} collective-permute-done((bf16[256,1024]{1,0:T(8,128)(2,1)}, bf16[256,1024]{1,0:T(8,128)(2,1)S(1)}, u32[]{:S(2)}, u32[]{:S(2)}) %collective-permute-start.98) | collective-permute-done | bytes 524320 | tf_op jit(solution)/shard_map/ppermute | solution.py:28
  66.8 7.5 %collective-permute-done.99.refs_1_ = bf16[256,1024]{1,0:T(8,128)(2,1)S(1)} collective-permute-done((bf16[256,1024]{1,0:T(8,128)(2,1)}, bf16[256,1024]{1,0:T(8,128)(2,1)S(1)}, u32[]{:S(2)}, u32[]{:S(2)}) %collective-permute-start.99) | collective-permute-done | bytes 524320 | tf_op jit(solution)/shard_map/ppermute | solution.py:28
  74.2 1.4 %shard_map.50 = (f32[224,256]{1,0:T(8,128)S(1)}, bf16[224,256]{1,0:T(8,128)(2,1)S(1)}, bf16[224,256]{1,0:T(8,128)(2,1)S(1)}, bf16[224,256]{1,0:T(8,128)(2,1)S(1)...) custom-call(s32[1,28]{1,0:T(1,128)S(1)} %copy-done.2, ...), custom_call_target="tpu_custom_call", output_to_operand_aliasing={{8}: (2, {})} | custom-call | flops 536870912 | bytes 5570560 | tf_op jit(solution)/shard_map/pallas_call | solution.py:406
  75.6 9.7 %collective-permute-start.106 = (bf16[224,256]{1,0:T(8,128)(2,1)S(1)}, bf16[224,256]{1,0:T(8,128)(2,1)S(1)}, u32[]{:S(2)}, u32[]{:S(2)}) collective-permute-start(bf16[224,256]{1,0:T(8,128)(2,1)S(1)} %get-tuple-element.392), channel_id=1, source_target_pairs={{0,1},{1,2},{2,3},{3,0},{4,5},{5,6},{6,7},{7,4},{8,9},{9,10},{10,1... | collective-permute-start | bytes 344072 | tf_op jit(solution)/shard_map/ppermute | solution.py:28
  85.4 2.2 %collective-permute-start.108 = (bf16[224,256]{1,0:T(8,128)(2,1)S(1)}, bf16[224,256]{1,0:T(8,128)(2,1)S(1)}, u32[]{:S(2)}, u32[]{:S(2)}) collective-permute-start(bf16[224,256]{1,0:T(8,128)(2,1)S(1)} %get-tuple-element.394), channel_id=1, source_target_pairs={{0,3},{1,0},{2,1},{3,2},{4,7},{5,4},{6,5},{7,6},{8,11},{9,8},{10,9... | collective-permute-start | bytes 344072 | tf_op jit(solution)/shard_map/ppermute | solution.py:28
  87.5 1.7 %collective-permute-start.101 = (bf16[224,256]{1,0:T(8,128)(2,1)S(1)}, bf16[224,256]{1,0:T(8,128)(2,1)S(1)}, u32[]{:S(2)}, u32[]{:S(2)}) collective-permute-start(bf16[224,256]{1,0:T(8,128)(2,1)S(1)} %get-tuple-element.388), channel_id=1, source_target_pairs={{0,2},{1,3},{2,0},{3,1},{4,6},{5,7},{6,4},{7,5},{8,10},{9,11},{10,... | collective-permute-start | bytes 344072 | tf_op jit(solution)/shard_map/ppermute | solution.py:28
  89.2 1.6 %collective-permute-start.102 = (bf16[224,256]{1,0:T(8,128)(2,1)S(1)}, bf16[224,256]{1,0:T(8,128)(2,1)S(1)}, u32[]{:S(2)}, u32[]{:S(2)}) collective-permute-start(bf16[224,256]{1,0:T(8,128)(2,1)S(1)} %get-tuple-element.389), channel_id=1, source_target_pairs={{0,3},{1,0},{2,1},{3,2},{4,7},{5,4},{6,5},{7,6},{8,11},{9,8},{10,9... | collective-permute-start | bytes 344072 | tf_op jit(solution)/shard_map/ppermute | solution.py:28
  91.0 2.6 %collective-permute-start.111 = (bf16[224,256]{1,0:T(8,128)(2,1)S(1)}, bf16[224,256]{1,0:T(8,128)(2,1)S(1)}, u32[]{:S(2)}, u32[]{:S(2)}) collective-permute-start(bf16[224,256]{1,0:T(8,128)(2,1)S(1)} %add_convert_fusion.refs_0_), channel_id=1, source_target_pairs={{0,3},{1,0},{2,1},{3,2},{4,7},{5,4},{6,5},{7,6},{8,11},{9,8},{10,9... | collective-permute-start | bytes 344072 | tf_op jit(solution)/shard_map/ppermute | solution.py:28
  93.6 2.6 %collective-permute-start.110 = (bf16[224,256]{1,0:T(8,128)(2,1)S(1)}, bf16[224,256]{1,0:T(8,128)(2,1)S(1)}, u32[]{:S(2)}, u32[]{:S(2)}) collective-permute-start(bf16[224,256]{1,0:T(8,128)(2,1)S(1)} %add_convert_fusion.refs_0_), channel_id=1, source_target_pairs={{0,2},{1,3},{2,0},{3,1},{4,6},{5,7},{6,4},{7,5},{8,10},{9,11},{10,... | collective-permute-start | bytes 344072 | tf_op jit(solution)/shard_map/ppermute | solution.py:28
  96.3 3.3 %collective-permute-start.105 = (bf16[224,256]{1,0:T(8,128)(2,1)S(1)}, bf16[224,256]{1,0:T(8,128)(2,1)S(1)}, u32[]{:S(2)}, u32[]{:S(2)}) collective-permute-start(bf16[224,256]{1,0:T(8,128)(2,1)S(1)} %add_convert_fusion.1.refs_0_), channel_id=1, source_target_pairs={{0,3},{1,0},{2,1},{3,2},{4,7},{5,4},{6,5},{7,6},{8,11},{9,8},{10,9... | collective-permute-start | bytes 344072 | tf_op jit(solution)/shard_map/ppermute | solution.py:28
  99.9 1.3 %shard_map.49.turned_ref = bf16[1024,896]{1,0:T(8,128)(2,1)S(1)} custom-call(s32[1,28]{1,0:T(1,128)S(1)} %copy-done.2, bf16[1360,1024]{1,0:T(8,128)(2,1)S(1)} %get-tuple-element.381.rows_ref, bf16[256,1024]{1,0:T(8,128)(2,1)S(1)} %collective-permute-done.98.refs_0_, bf16[256,1024]{1,0:T(8,128)(2,1)S(1)} %collective-permute-done.99.refs_1_), custom_call_target="tpu_custom_call" | custom-call | bytes 3670016 | tf_op jit(solution)/shard_map/pallas_call | solution.py:419
  102.2 1.3 %shard_map.52 = (f32[1024,256]{1,0:T(8,128)S(1)}, bf16[1024,256]{1,0:T(8,128)(2,1)S(1)}, f32[8,128]{1,0:T(8,128)S(1)}) custom-call(bf16[1024,896]{1,0:T(8,128)(2,1)S(1)} %shard_map.49.turned_ref, bf16[224,256]{1,0:T(8,128)(2,1)S(1)} %add_convert_fusion.refs_0_, bf16[224,256]{1,0:T(8,128)(2,1)S(1)} %collective-permute-done.109.refs_1_, ...), custom_call_target="tpu_custom_call" | custom-call | flops 469762048 | bytes 2097152 | tf_op jit(solution)/shard_map/pallas_call | solution.py:436
  103.5 3.5 %collective-permute-done.104.refs_2_ = bf16[224,256]{1,0:T(8,128)(2,1)S(1)} collective-permute-done((bf16[224,256]{1,0:T(8,128)(2,1)S(1)}, bf16[224,256]{1,0:T(8,128)(2,1)S(1)}, u32[]{:S(2)}, u32[]{:S(2)}) %collective-permute-start.104) | collective-permute-done | bytes 114720 | tf_op jit(solution)/shard_map/ppermute | solution.py:28
  107.0 1.3 %shard_map.51 = (f32[1024,256]{1,0:T(8,128)S(1)}, bf16[1024,256]{1,0:T(8,128)(2,1)S(1)}, f32[8,128]{1,0:T(8,128)S(1)}) custom-call(bf16[1024,896]{1,0:T(8,128)(2,1)S(1)} %shard_map.49.turned_ref, bf16[224,256]{1,0:T(8,128)(2,1)S(1)} %add_convert_fusion.1.refs_0_, bf16[224,256]{1,0:T(8,128)(2,1)S(1)} %collective-permute-done.103.refs_1_, ...), custom_call_target="tpu_custom_call" | custom-call | flops 469762048 | bytes 2097152 | tf_op jit(solution)/shard_map/pallas_call | solution.py:436
  108.7 1.4 %collective-permute-start.112 = (f32[8,128]{1,0:T(8,128)S(1)}, f32[8,128]{1,0:T(8,128)S(1)}, u32[]{:S(2)}, u32[]{:S(2)}) collective-permute-start(f32[8,128]{1,0:T(8,128)S(1)} %add.284), channel_id=1, source_target_pairs={{0,1},{1,2},{2,3},{3,0},{4,5},{5,6},{6,7},{7,4},{8,9},{9,10},{10,1... | collective-permute-start | bytes 12296 | tf_op jit(solution)/shard_map/ppermute | solution.py:28
  110.9 1.0 collective-permute-done.113
  111.9 1.1 collective-permute-done.112
  113.0 2.1 %collective-permute-start.115 = (f32[8,128]{1,0:T(8,128)S(1)}, f32[8,128]{1,0:T(8,128)S(1)}, u32[]{:S(2)}, u32[]{:S(2)}) collective-permute-start(f32[8,128]{1,0:T(8,128)S(1)} %add_add_fusion.32.own_ref), channel_id=1, source_target_pairs={{0,4},{4,0},{8,12},{12,8},{16,20},{20,16},{24,28},{28,24},{1,5},{5... | collective-permute-start | bytes 12296 | tf_op jit(solution)/shard_map/ppermute | solution.py:22
  115.9 1.7 %shard_map.53 = f32[1024,512]{1,0:T(8,128)} custom-call(f32[8,128]{1,0:T(8,128)S(1)} %add_add_fusion.32.own_ref, f32[8,128]{1,0:T(8,128)S(1)} %collective-permute-done.115.other_ref, f32[1024,512]{1,0:T(8,128)S(1)} %get-tuple-element.396.halves_ref, f32[1024,256]{1,0:T(8,128)S(1)} %get-tuple-element.397.refs_0_, f32[1024,256]{1,0:T(8,128)S(1)} %get-tuple-element.398.refs_1_, ...), custom_call_target="tpu_custom_call" | custom-call | tf_op jit(solution)/shard_map/pallas_call | solution.py:460
  (68 shorter events, 9.6 us)
Async XLA Ops:
  0.0 54.3 %collective-permute-start.96 = (f32[1024,512]{1,0:T(8,128)}, f32[1024,512]{1,0:T(8,128)}, u32[]{:S(2)}, u32[]{:S(2)}) collective-permute-start(f32[1024,512]{1,0:T(8,128)} %bitcast.8), channel_id=1, source_target_pairs={{0,4},{4,0},{8,12},{12,8},{16,20},{20,16},{24,28},{28,24},{1,5},{5... | collective-permute-start | bytes 6291464 | tf_op jit(solution)/shard_map/ppermute | solution.py:22
  4.7 49.6 %collective-permute-start.97 = (bf16[256,1024]{1,0:T(8,128)(2,1)}, bf16[256,1024]{1,0:T(8,128)(2,1)S(1)}, u32[]{:S(2)}, u32[]{:S(2)}) collective-permute-start(bf16[256,1024]{1,0:T(8,128)(2,1)} %get-tuple-element.376), channel_id=1, source_target_pairs={{0,2},{1,3},{2,0},{3,1},{4,6},{5,7},{6,4},{7,5},{8,10},{9,11},{10,... | collective-permute-start | bytes 1572872 | tf_op jit(solution)/shard_map/ppermute | solution.py:28
  16.3 26.8 %copy-start.3 = (bf16[208,1024]{1,0:T(8,128)(2,1)}, bf16[208,1024]{1,0:T(8,128)(2,1)S(1)}, u32[]{:S(2)}) copy-start(bf16[208,1024]{1,0:T(8,128)(2,1)S(1)} %get-tuple-element.373) | copy-start | bytes 1277956
  16.3 26.8 %copy-start.4 = (bf16[208,1024]{1,0:T(8,128)(2,1)}, bf16[208,1024]{1,0:T(8,128)(2,1)S(1)}, u32[]{:S(2)}) copy-start(bf16[208,1024]{1,0:T(8,128)(2,1)S(1)} %get-tuple-element.374) | copy-start | bytes 1277956
  17.4 2.7 %collective-permute-start.53 = (bf16[32,1024]{1,0:T(8,128)(2,1)S(1)}, bf16[32,1024]{1,0:T(8,128)(2,1)S(1)}, u32[]{:S(2)}, u32[]{:S(2)}) collective-permute-start(bf16[32,1024]{1,0:T(8,128)(2,1)S(1)} %slice.223), channel_id=1, source_target_pairs={{2,1},{6,5},{10,9},{14,13},{18,17},{22,21},{26,25},{30,29}} | collective-permute-start | bytes 196616 | tf_op jit(solution)/shard_map/cond/branch_2_fun/ppermute | solution.py:299
  18.0 2.0 %collective-permute-start.52 = (bf16[32,1024]{1,0:T(8,128)(2,1)S(1)}, bf16[32,1024]{1,0:T(8,128)(2,1)S(1)}, u32[]{:S(2)}, u32[]{:S(2)}) collective-permute-start(bf16[32,1024]{1,0:T(8,128)(2,1)S(1)} %slice.222), channel_id=1, source_target_pairs={{2,3},{6,7},{10,11},{14,15},{18,19},{22,23},{26,27},{30,31}} | collective-permute-start | bytes 196616 | tf_op jit(solution)/shard_map/cond/branch_2_fun/ppermute | solution.py:299
  18.7 24.3 %collective-permute-start.51 = (bf16[32,1024]{1,0:T(8,128)(2,1)S(1)}, bf16[32,1024]{1,0:T(8,128)(2,1)S(1)}, u32[]{:S(2)}, u32[]{:S(2)}) collective-permute-start(bf16[32,1024]{1,0:T(8,128)(2,1)S(1)} %slice.221), channel_id=1, source_target_pairs={{2,0},{6,4},{10,8},{14,12},{18,16},{22,20},{26,24},{30,28}} | collective-permute-start | bytes 196616 | tf_op jit(solution)/shard_map/cond/branch_2_fun/ppermute | solution.py:299
  43.9 4.6 %collective-permute-start.26 = (bf16[16,1024]{1,0:T(8,128)(2,1)S(1)}, bf16[16,1024]{1,0:T(8,128)(2,1)S(1)}, u32[]{:S(2)}, u32[]{:S(2)}) collective-permute-start(bf16[16,1024]{1,0:T(8,128)(2,1)S(1)} %slice.199), channel_id=1, source_target_pairs={{1,0},{5,4},{9,8},{13,12},{17,16},{21,20},{25,24},{29,28}} | collective-permute-start | bytes 98312 | tf_op jit(solution)/shard_map/cond/branch_1_fun/ppermute | solution.py:299
  45.2 3.4 %collective-permute-start.25 = (bf16[16,1024]{1,0:T(8,128)(2,1)S(1)}, bf16[16,1024]{1,0:T(8,128)(2,1)S(1)}, u32[]{:S(2)}, u32[]{:S(2)}) collective-permute-start(bf16[16,1024]{1,0:T(8,128)(2,1)S(1)} %slice.198), channel_id=1, source_target_pairs={{1,2},{5,6},{9,10},{13,14},{17,18},{21,22},{25,26},{29,30}} | collective-permute-start | bytes 98312 | tf_op jit(solution)/shard_map/cond/branch_1_fun/ppermute | solution.py:299
  45.9 2.7 %collective-permute-start.24 = (bf16[16,1024]{1,0:T(8,128)(2,1)S(1)}, bf16[16,1024]{1,0:T(8,128)(2,1)S(1)}, u32[]{:S(2)}, u32[]{:S(2)}) collective-permute-start(bf16[16,1024]{1,0:T(8,128)(2,1)S(1)} %slice.197), channel_id=1, source_target_pairs={{1,3},{5,7},{9,11},{13,15},{17,19},{21,23},{25,27},{29,31}} | collective-permute-start | bytes 98312 | tf_op jit(solution)/shard_map/cond/branch_1_fun/ppermute | solution.py:299
  49.4 4.9 %copy-start.1 = (bf16[1,448,512]{2,1,0:T(8,128)(2,1)S(1)}, bf16[1,448,512]{2,1,0:T(8,128)(2,1)}, u32[]{:S(2)}) copy-start(bf16[1,448,512]{2,1,0:T(8,128)(2,1)} %param.41) | copy-start | bytes 1376260
  49.4 4.9 %copy-start.2 = (s32[1,28]{1,0:T(1,128)S(1)}, s32[1,28]{1,0:T(1,128)}, u32[]{:S(2)}) copy-start(s32[1,28]{1,0:T(1,128)} %lengths_ref.8) | copy-start | bytes 340
  49.4 17.4 %collective-permute-start.98 = (bf16[256,1024]{1,0:T(8,128)(2,1)}, bf16[256,1024]{1,0:T(8,128)(2,1)S(1)}, u32[]{:S(2)}, u32[]{:S(2)}) collective-permute-start(bf16[256,1024]{1,0:T(8,128)(2,1)} %get-tuple-element.382), channel_id=1, source_target_pairs={{0,1},{1,2},{2,3},{3,0},{4,5},{5,6},{6,7},{7,4},{8,9},{9,10},{10,1... | collective-permute-start | bytes 1572872 | tf_op jit(solution)/shard_map/ppermute | solution.py:28
  51.8 22.5 %collective-permute-start.99 = (bf16[256,1024]{1,0:T(8,128)(2,1)}, bf16[256,1024]{1,0:T(8,128)(2,1)S(1)}, u32[]{:S(2)}, u32[]{:S(2)}) collective-permute-start(bf16[256,1024]{1,0:T(8,128)(2,1)} %get-tuple-element.383), channel_id=1, source_target_pairs={{0,3},{1,0},{2,1},{3,2},{4,7},{5,4},{6,5},{7,6},{8,11},{9,8},{10,9... | collective-permute-start | bytes 1572872 | tf_op jit(solution)/shard_map/ppermute | solution.py:28
  75.6 13.6 %collective-permute-start.106 = (bf16[224,256]{1,0:T(8,128)(2,1)S(1)}, bf16[224,256]{1,0:T(8,128)(2,1)S(1)}, u32[]{:S(2)}, u32[]{:S(2)}) collective-permute-start(bf16[224,256]{1,0:T(8,128)(2,1)S(1)} %get-tuple-element.392), channel_id=1, source_target_pairs={{0,1},{1,2},{2,3},{3,0},{4,5},{5,6},{6,7},{7,4},{8,9},{9,10},{10,1... | collective-permute-start | bytes 344072 | tf_op jit(solution)/shard_map/ppermute | solution.py:28
  85.4 5.6 %collective-permute-start.107 = (bf16[224,256]{1,0:T(8,128)(2,1)S(1)}, bf16[224,256]{1,0:T(8,128)(2,1)S(1)}, u32[]{:S(2)}, u32[]{:S(2)}) collective-permute-start(bf16[224,256]{1,0:T(8,128)(2,1)S(1)} %get-tuple-element.393), channel_id=1, source_target_pairs={{0,2},{1,3},{2,0},{3,1},{4,6},{5,7},{6,4},{7,5},{8,10},{9,11},{10,... | collective-permute-start | bytes 344072 | tf_op jit(solution)/shard_map/ppermute | solution.py:28
  85.4 5.6 %collective-permute-start.108 = (bf16[224,256]{1,0:T(8,128)(2,1)S(1)}, bf16[224,256]{1,0:T(8,128)(2,1)S(1)}, u32[]{:S(2)}, u32[]{:S(2)}) collective-permute-start(bf16[224,256]{1,0:T(8,128)(2,1)S(1)} %get-tuple-element.394), channel_id=1, source_target_pairs={{0,3},{1,0},{2,1},{3,2},{4,7},{5,4},{6,5},{7,6},{8,11},{9,8},{10,9... | collective-permute-start | bytes 344072 | tf_op jit(solution)/shard_map/ppermute | solution.py:28
  87.5 8.7 %collective-permute-start.100 = (bf16[224,256]{1,0:T(8,128)(2,1)S(1)}, bf16[224,256]{1,0:T(8,128)(2,1)S(1)}, u32[]{:S(2)}, u32[]{:S(2)}) collective-permute-start(bf16[224,256]{1,0:T(8,128)(2,1)S(1)} %get-tuple-element.387), channel_id=1, source_target_pairs={{0,1},{1,2},{2,3},{3,0},{4,5},{5,6},{6,7},{7,4},{8,9},{9,10},{10,1... | collective-permute-start | bytes 344072 | tf_op jit(solution)/shard_map/ppermute | solution.py:28
  87.5 8.7 %collective-permute-start.101 = (bf16[224,256]{1,0:T(8,128)(2,1)S(1)}, bf16[224,256]{1,0:T(8,128)(2,1)S(1)}, u32[]{:S(2)}, u32[]{:S(2)}) collective-permute-start(bf16[224,256]{1,0:T(8,128)(2,1)S(1)} %get-tuple-element.388), channel_id=1, source_target_pairs={{0,2},{1,3},{2,0},{3,1},{4,6},{5,7},{6,4},{7,5},{8,10},{9,11},{10,... | collective-permute-start | bytes 344072 | tf_op jit(solution)/shard_map/ppermute | solution.py:28
  89.2 7.0 %collective-permute-start.102 = (bf16[224,256]{1,0:T(8,128)(2,1)S(1)}, bf16[224,256]{1,0:T(8,128)(2,1)S(1)}, u32[]{:S(2)}, u32[]{:S(2)}) collective-permute-start(bf16[224,256]{1,0:T(8,128)(2,1)S(1)} %get-tuple-element.389), channel_id=1, source_target_pairs={{0,3},{1,0},{2,1},{3,2},{4,7},{5,4},{6,5},{7,6},{8,11},{9,8},{10,9... | collective-permute-start | bytes 344072 | tf_op jit(solution)/shard_map/ppermute | solution.py:28
  91.0 8.6 %collective-permute-start.111 = (bf16[224,256]{1,0:T(8,128)(2,1)S(1)}, bf16[224,256]{1,0:T(8,128)(2,1)S(1)}, u32[]{:S(2)}, u32[]{:S(2)}) collective-permute-start(bf16[224,256]{1,0:T(8,128)(2,1)S(1)} %add_convert_fusion.refs_0_), channel_id=1, source_target_pairs={{0,3},{1,0},{2,1},{3,2},{4,7},{5,4},{6,5},{7,6},{8,11},{9,8},{10,9... | collective-permute-start | bytes 344072 | tf_op jit(solution)/shard_map/ppermute | solution.py:28
  93.6 8.6 %collective-permute-start.110 = (bf16[224,256]{1,0:T(8,128)(2,1)S(1)}, bf16[224,256]{1,0:T(8,128)(2,1)S(1)}, u32[]{:S(2)}, u32[]{:S(2)}) collective-permute-start(bf16[224,256]{1,0:T(8,128)(2,1)S(1)} %add_convert_fusion.refs_0_), channel_id=1, source_target_pairs={{0,2},{1,3},{2,0},{3,1},{4,6},{5,7},{6,4},{7,5},{8,10},{9,11},{10,... | collective-permute-start | bytes 344072 | tf_op jit(solution)/shard_map/ppermute | solution.py:28
  96.2 6.0 %collective-permute-start.109 = (bf16[224,256]{1,0:T(8,128)(2,1)S(1)}, bf16[224,256]{1,0:T(8,128)(2,1)S(1)}, u32[]{:S(2)}, u32[]{:S(2)}) collective-permute-start(bf16[224,256]{1,0:T(8,128)(2,1)S(1)} %add_convert_fusion.refs_0_), channel_id=1, source_target_pairs={{0,1},{1,2},{2,3},{3,0},{4,5},{5,6},{6,7},{7,4},{8,9},{9,10},{10,1... | collective-permute-start | bytes 344072 | tf_op jit(solution)/shard_map/ppermute | solution.py:28
  96.3 7.2 %collective-permute-start.105 = (bf16[224,256]{1,0:T(8,128)(2,1)S(1)}, bf16[224,256]{1,0:T(8,128)(2,1)S(1)}, u32[]{:S(2)}, u32[]{:S(2)}) collective-permute-start(bf16[224,256]{1,0:T(8,128)(2,1)S(1)} %add_convert_fusion.1.refs_0_), channel_id=1, source_target_pairs={{0,3},{1,0},{2,1},{3,2},{4,7},{5,4},{6,5},{7,6},{8,11},{9,8},{10,9... | collective-permute-start | bytes 344072 | tf_op jit(solution)/shard_map/ppermute | solution.py:28
  99.6 7.4 %collective-permute-start.104 = (bf16[224,256]{1,0:T(8,128)(2,1)S(1)}, bf16[224,256]{1,0:T(8,128)(2,1)S(1)}, u32[]{:S(2)}, u32[]{:S(2)}) collective-permute-start(bf16[224,256]{1,0:T(8,128)(2,1)S(1)} %add_convert_fusion.1.refs_0_), channel_id=1, source_target_pairs={{0,2},{1,3},{2,0},{3,1},{4,6},{5,7},{6,4},{7,5},{8,10},{9,11},{10,... | collective-permute-start | bytes 344072 | tf_op jit(solution)/shard_map/ppermute | solution.py:28
  99.6 7.4 %collective-permute-start.103 = (bf16[224,256]{1,0:T(8,128)(2,1)S(1)}, bf16[224,256]{1,0:T(8,128)(2,1)S(1)}, u32[]{:S(2)}, u32[]{:S(2)}) collective-permute-start(bf16[224,256]{1,0:T(8,128)(2,1)S(1)} %add_convert_fusion.1.refs_0_), channel_id=1, source_target_pairs={{0,1},{1,2},{2,3},{3,0},{4,5},{5,6},{6,7},{7,4},{8,9},{9,10},{10,1... | collective-permute-start | bytes 344072 | tf_op jit(solution)/shard_map/ppermute | solution.py:28
  103.4 12.5 %collective-permute-start.117 = (bf16[1024,256]{1,0:T(8,128)(2,1)S(1)}, bf16[1024,256]{1,0:T(8,128)(2,1)S(1)}, u32[]{:S(2)}, u32[]{:S(2)}) collective-permute-start(bf16[1024,256]{1,0:T(8,128)(2,1)S(1)} %get-tuple-element.400), channel_id=1, source_target_pairs={{0,4},{4,0},{8,12},{12,8},{16,20},{20,16},{24,28},{28,24},{1,5},{5... | collective-permute-start | bytes 1572872 | tf_op jit(solution)/shard_map/ppermute | solution.py:22
  108.3 7.6 %collective-permute-start.116 = (bf16[1024,256]{1,0:T(8,128)(2,1)S(1)}, bf16[1024,256]{1,0:T(8,128)(2,1)S(1)}, u32[]{:S(2)}, u32[]{:S(2)}) collective-permute-start(bf16[1024,256]{1,0:T(8,128)(2,1)S(1)} %get-tuple-element.399), channel_id=1, source_target_pairs={{0,4},{4,0},{8,12},{12,8},{16,20},{20,16},{24,28},{28,24},{1,5},{5... | collective-permute-start | bytes 1572872 | tf_op jit(solution)/shard_map/ppermute | solution.py:22
  108.4 2.5 %collective-permute-start.114 = (f32[8,128]{1,0:T(8,128)S(1)}, f32[8,128]{1,0:T(8,128)S(1)}, u32[]{:S(2)}, u32[]{:S(2)}) collective-permute-start(f32[8,128]{1,0:T(8,128)S(1)} %add.284), channel_id=1, source_target_pairs={{0,3},{1,0},{2,1},{3,2},{4,7},{5,4},{6,5},{7,6},{8,11},{9,8},{10,9... | collective-permute-start | bytes 12296 | tf_op jit(solution)/shard_map/ppermute | solution.py:28
  108.5 3.4 %collective-permute-start.113 = (f32[8,128]{1,0:T(8,128)S(1)}, f32[8,128]{1,0:T(8,128)S(1)}, u32[]{:S(2)}, u32[]{:S(2)}) collective-permute-start(f32[8,128]{1,0:T(8,128)S(1)} %add.284), channel_id=1, source_target_pairs={{0,2},{1,3},{2,0},{3,1},{4,6},{5,7},{6,4},{7,5},{8,10},{9,11},{10,... | collective-permute-start | bytes 12296 | tf_op jit(solution)/shard_map/ppermute | solution.py:28
  108.7 4.3 %collective-permute-start.112 = (f32[8,128]{1,0:T(8,128)S(1)}, f32[8,128]{1,0:T(8,128)S(1)}, u32[]{:S(2)}, u32[]{:S(2)}) collective-permute-start(f32[8,128]{1,0:T(8,128)S(1)} %add.284), channel_id=1, source_target_pairs={{0,1},{1,2},{2,3},{3,0},{4,5},{5,6},{6,7},{7,4},{8,9},{9,10},{10,1... | collective-permute-start | bytes 12296 | tf_op jit(solution)/shard_map/ppermute | solution.py:28
  113.0 2.9 %collective-permute-start.115 = (f32[8,128]{1,0:T(8,128)S(1)}, f32[8,128]{1,0:T(8,128)S(1)}, u32[]{:S(2)}, u32[]{:S(2)}) collective-permute-start(f32[8,128]{1,0:T(8,128)S(1)} %add_add_fusion.32.own_ref), channel_id=1, source_target_pairs={{0,4},{4,0},{8,12},{12,8},{16,20},{20,16},{24,28},{28,24},{1,5},{5... | collective-permute-start | bytes 12296 | tf_op jit(solution)/shard_map/ppermute | solution.py:22
  (4 other events, 7.4 us)

commit v2 on v1

--- a/solution.py
+++ b/solution.py
@@ -66,6 +66,11 @@
 def picking(places, start, rows):
     row = lax.broadcasted_iota(jnp.int32, (rows, places.shape[1]), 0) + start
     return jnp.where(row == places, 1.0, 0.0).astype(jnp.bfloat16)
+
+
+def other_half(index):
+    half = index // 2
+    return [2 - half, 3 - 3 * half]
 
 
 class Block:
@@ -225,13 +230,17 @@
             jnp.dot(block_ref[...], low_ref[...], preferred_element_type=jnp.float32) * scale
         )
     share, width = sums[0].shape
+    count = len(sums) // HALVES
+    if members == 4:
+        owners = [[index], [jnp.bitwise_xor(index, 1)], other_half(index)]
+    else:
+        owners = [[lax.rem(index + i, members)] for i in range(members)]
     for half in range(HALVES):
-        for i in range(members):
-            owner = lax.rem(index + i, members)
-            rows = pl.ds(pl.multiple_of(owner * share, ALIGN), share)
-            out_ref = sums[half * members + i]
-            here = slice(half * width, (half + 1) * width)
-            out_ref[...] = total_ref[rows, here].astype(out_ref.dtype)
+        here = slice(half * width, (half + 1) * width)
+        for out_ref, group in zip(sums[half * count : (half + 1) * count], owners):
+            for n, owner in enumerate(group):
+                rows = pl.ds(pl.multiple_of(owner * share, ALIGN), share)
+                out_ref[n * share : (n + 1) * share] = total_ref[rows, here].astype(out_ref.dtype)
 
 
 def turn_kernel(members, near, lengths_ref, rows_ref, *refs):
@@ -247,12 +256,31 @@
 
 
 def gradient_kernel(members, turned_ref, *refs):
-    residuals, (gradient_ref, low_ref, squares_ref, all_ref) = refs[:members], refs[members:]
+    residuals, (gradient_ref, low_ref, squares_ref, all_ref) = refs[:-4], refs[-4:]
     index = lax.axis_index("fsdp")
     share = residuals[0].shape[0]
-    for i in range(members):
-        owner = lax.rem(index + members - i, members)
-        all_ref[pl.ds(pl.multiple_of(owner * share, ALIGN), share)] = residuals[i][...]
+
+    def put(owner, block):
+        all_ref[pl.ds(pl.multiple_of(owner * share, ALIGN), share)] = block
+
+    if members == 4:
+        own_ref, left_ref, right_ref, two_ref, pair_ref = residuals
+        inner, outer = other_half(index)
+        put(index, own_ref[...])
+        pl.when(index > 0)(lambda: put(index - 1, left_ref[...]))
+        pl.when(index < 3)(lambda: put(index + 1, right_ref[...]))
+
+        @pl.when((index == 1) | (index == 2))
+        def _():
+            put(outer, two_ref[...])
+
+        @pl.when((index == 0) | (index == 3))
+        def _():
+            put(inner, pair_ref[:share])
+            put(outer, pair_ref[share:])
+    else:
+        for i in range(members):
+            put(lax.rem(index + members - i, members), residuals[i][...])
     squares_ref[...] = jnp.zeros_like(squares_ref)
     height = min(256, turned_ref.shape[0])
 
@@ -300,6 +328,42 @@
         for i, block in zip(offsets, blocks)
     ]
     return jnp.pad(sum(moved[1:], moved[0]), ((0, blocks[0].shape[0] - size), (0, 0)))
+
+
+def sent_along(value, *pairs):
+    return lax.ppermute(value, "fsdp", pairs)
+
+
+def own_residual(sums):
+    members = lax.axis_size("fsdp")
+    if members == 4:
+        own, near, far = sums
+        share = own.shape[0]
+        handed = sent_along(far, (0, 1), (3, 2)).astype(jnp.float32)
+        far = (far.astype(jnp.float32) + handed).astype(far.dtype)
+        received = [
+            sent_along(far[:share], (1, 2), (2, 1)),
+            sent_along(far[share:], (1, 3), (2, 0)),
+            sent_along(near, (0, 1), (1, 0), (2, 3), (3, 2)),
+        ]
+    else:
+        own = sums[0]
+        received = [turned(sums[i], i) for i in range(1, members)]
+    for part in received:
+        own = own + part.astype(jnp.float32)
+    return own.astype(jnp.bfloat16)
+
+
+def all_residuals(residual):
+    members = lax.axis_size("fsdp")
+    if members == 4:
+        left = sent_along(residual, (0, 1), (1, 2), (2, 3))
+        right = sent_along(residual, (1, 0), (2, 1), (3, 2))
+        two = sent_along(residual, (0, 2), (3, 1))
+        inner = jnp.where(lax.axis_index("fsdp") < 2, right, left)
+        pair = sent_along(jnp.concatenate([inner, two]), (1, 0), (2, 3))
+        return [residual, left, right, two, pair]
+    return [residual] + [turned(residual, i) for i in range(1, members)]
 
 
 def local(activations, targets, weights, lengths):
@@ -402,19 +466,22 @@
     )(late_lengths, features, wanted, master, partner_master, held_far, *held_more)
 
     width = columns // HALVES
-    sum_shapes = [array(share, width, jnp.bfloat16 if i else jnp.float32) for i in range(members)]
+    counts = [1, 1, 2] if members == 4 else [1] * members
+    sum_shapes = [
+        array(n * share, width, jnp.bfloat16 if i else jnp.float32) for i, n in enumerate(counts)
+    ]
     *sums, _ = pl.pallas_call(
         functools.partial(keys_kernel, members, near, scale),
         in_specs=[smem, vmem, vmem] + [vmem] * len(near),
-        out_specs=[vmem] * (HALVES * members + 1),
+        out_specs=[vmem] * (HALVES * len(counts) + 1),
         out_shape=sum_shapes * HALVES + [array(places, columns, jnp.float32)],
-        input_output_aliases={2: HALVES * members},
+        input_output_aliases={2: HALVES * len(counts)},
         compiler_params=params,
         cost_estimate=cost(
             2 * len(near) * first * local_rows * columns, 8 * places * columns
         ),
     )(lengths, low, keys, *held)
-    sums = [sums[half * members : (half + 1) * members] for half in range(HALVES)]
+    sums = [sums[half * len(counts) : (half + 1) * len(counts)] for half in range(HALVES)]
 
     turned_rows = pl.pallas_call(
         functools.partial(turn_kernel, members, near),
@@ -428,14 +495,10 @@
 
     gradients, partners, squares = [], [], 0.0
     for half in range(HALVES):
-        residual = sums[half][0]
-        for i in range(1, members):
-            residual = residual + turned(sums[half][i], i).astype(jnp.float32)
-        residual = residual.astype(jnp.bfloat16)
-        residuals = [residual] + [turned(residual, i) for i in range(1, members)]
+        residuals = all_residuals(own_residual(sums[half]))
         gradient, low_gradient, own_squares = pl.pallas_call(
             functools.partial(gradient_kernel, members),
-            in_specs=[vmem] + [vmem] * members,
+            in_specs=[vmem] * (1 + len(residuals)),
             out_specs=[vmem] * 3,
             out_shape=[
                 array(local_rows, width, jnp.float32),

time: 117 us -> 134 us (1.15)
  the two profiles are of different devices: /device:TPU:7 before, /device:TPU:13 now
where the time goes in v2:
time: 134 us; the launch traced here: 132 us
  starting transfers between devices  69.1 us (52%)
  Pallas kernels  23.4 us (17%)
  waiting for transfers between devices  18.8 us (14%)
  local copies, waits for them, and re-layouts  15.4 us (11%)
  between operations  3.01 us (2%)
  other arithmetic  2.31 us (2%)
    ppermute x16, starting transfers between devices, sent_along(): return lax.ppermute(value, 'fsdp', pairs)  36.1 us
    ppermute x4, starting transfers between devices, swapped(): return lax.ppermute(value, axis, pairs)  22.3 us
    ppermute x3, waiting for transfers between devices, more_rows(): lax.ppermute(block[:size], 'fsdp', [(source, (source + i) % members)])  12.9 us
    pallas_call x2, Pallas kernels, sent_to(): pl.pallas_call(functools.partial(sent_kernel, members, offsets, sizes), i...  9.27 us
    unnamed x32, local copies, waits for them, and re-layouts  8.76 us
    ppermute x6, starting transfers between devices, turned(): return lax.ppermute(value, 'fsdp', ring)  8.17 us
    pallas_call x1, Pallas kernels, local(): pl.pallas_call(functools.partial(own_kernel, members, far, scale), in_spe...  6.39 us
    cond x2, local copies, waits for them, and re-layouts  3.61 us
  transfers between devices with their start and end apart: 29, of which 6 were waited for; matrix products, arithmetic and copies ran while one was open for 7% of the time, Pallas kernels for 15%

profile of v2, /device:TPU:13, one launch (start us, length us, event | category | flops | bytes accessed | tf_op | source)
XLA Modules:
  0.0 132.4 jit_solution(6612871008352263195)
XLA Ops:
  0.7 4.0 %shard_map.47 = (bf16[256,1024]{1,0:T(8,128)(2,1)}, bf16[208,1024]{1,0:T(8,128)(2,1)}, s32[4]{0:T(128)}) custom-call(s32[1,28]{1,0:T(1,128)} %lengths_ref.8, bf16[448,4096]{1,0:T(8,128)(2,1)} %bitcast.11), custom_call_target="tpu_custom_call" | custom-call | flops 234881024 | bytes 1441792 | tf_op jit(solution)/shard_map/pallas_call | solution.py:401
  4.7 2.4 %collective-permute-start.97 = (bf16[256,1024]{1,0:T(8,128)(2,1)}, bf16[256,1024]{1,0:T(8,128)(2,1)S(1)}, u32[]{:S(2)}, u32[]{:S(2)}) collective-permute-start(bf16[256,1024]{1,0:T(8,128)(2,1)} %get-tuple-element.374), channel_id=1, source_target_pairs={{0,2},{1,3},{2,0},{3,1},{4,6},{5,7},{6,4},{7,5},{8,10},{9,11},{10,... | collective-permute-start | bytes 1572872 | tf_op jit(solution)/shard_map/ppermute | solution.py:28
  7.1 1.3 %fusion.2 = (s32[1]{0:T(128)}, s32[1]{0:T(128)}, s32[1]{0:T(128)}, s32[1]{0:T(128)}) fusion(s32[4]{0:T(128)} %get-tuple-element.369), kind=kLoop, calls=%fused_computation.43 | loop fusion | bytes 32 | tf_op jit(solution)/shard_map/slice | solution.py:433
  9.6 5.3 %shard_map.46 = (bf16[256,1024]{1,0:T(8,128)(2,1)}, bf16[256,1024]{1,0:T(8,128)(2,1)}, bf16[208,1024]{1,0:T(8,128)(2,1)S(1)}, bf16[208,1024]{1,0:T(8,128)(2,1)S(1)}, s32[4]{0:T(128)}) custom-call(s32[1,28]{1,0:T(1,128)} %lengths_ref.8, bf16[448,4096]{1,0:T(8,128)(2,1)} %bitcast.12), custom_call_target="tpu_custom_call" | custom-call | flops 469762048 | bytes 2883584 | tf_op jit(solution)/shard_map/pallas_call | solution.py:401
  14.9 1.8 %conditional.7 = (bf16[208,1024]{1,0:T(8,128)(2,1)}) conditional(s32[]{:T(128)} %bitcast.4, bf16[208,1024]{1,0:T(8,128)(2,1)} %get-tuple-element.370, (bf16[208,1024]{1,0:T(8,128)(2,1)}, bf16[208,1024]{1,0:T(8,128)(2,1)S(1)}, bf16[208,1024]{1,0:T(8,128)(2,1)S(1)}) %tuple.114, (bf16[208,1024]{1,0:T(8,128)(2,1)}, ...), branch_computations={%region_27.28_spmd, %region_28.29_spmd, %region_29.30_spmd, %regio... | conditional | flops 425984 | bytes 6815872 | solution.py:432
  14.9 1.8 %copy.33 = bf16[208,1024]{1,0:T(8,128)(2,1)} copy(bf16[208,1024]{1,0:T(8,128)(2,1)} %param.27) | data formatting | bytes 851968 | tf_op jit(solution)/shard_map/cond
  16.7 17.3 %conditional.6 = (bf16[208,1024]{1,0:T(8,128)(2,1)}) conditional(s32[]{:T(128)} %bitcast.3, bf16[208,1024]{1,0:T(8,128)(2,1)} %get-tuple-element.370, (bf16[208,1024]{1,0:T(8,128)(2,1)}, bf16[208,1024]{1,0:T(8,128)(2,1)S(1)}, bf16[208,1024]{1,0:T(8,128)(2,1)S(1)}) %tuple.114, (bf16[208,1024]{1,0:T(8,128)(2,1)}, ...), branch_computations={%region_18.19_spmd, %region_19.20_spmd, %region_20.21_spmd, %regio... | conditional | flops 425984 | bytes 6815872 | solution.py:432
  20.2 12.9 %collective-permute-done.53 = bf16[32,1024]{1,0:T(8,128)(2,1)S(1)} collective-permute-done((bf16[32,1024]{1,0:T(8,128)(2,1)S(1)}, bf16[32,1024]{1,0:T(8,128)(2,1)S(1)}, u32[]{:S(2)}, u32[]{:S(2)}) %collective-permute-start.53) | collective-permute-done | bytes 65568 | tf_op jit(solution)/shard_map/cond/branch_2_fun/ppermute | solution.py:327
  34.6 1.8 %conditional.5 = (bf16[208,1024]{1,0:T(8,128)(2,1)}) conditional(s32[]{:T(128)} %bitcast.2, bf16[208,1024]{1,0:T(8,128)(2,1)} %get-tuple-element.370, (bf16[208,1024]{1,0:T(8,128)(2,1)}, bf16[208,1024]{1,0:T(8,128)(2,1)S(1)}, bf16[208,1024]{1,0:T(8,128)(2,1)S(1)}) %tuple.114, (bf16[208,1024]{1,0:T(8,128)(2,1)}, ...), branch_computations={%region_9.10_spmd, %region_10.11_spmd, %region_11.12_spmd, %region... | conditional | flops 425984 | bytes 6815872 | solution.py:432
  34.6 1.8 %copy.15 = bf16[208,1024]{1,0:T(8,128)(2,1)} copy(bf16[208,1024]{1,0:T(8,128)(2,1)} %param.9) | data formatting | bytes 851968 | tf_op jit(solution)/shard_map/cond
  37.3 1.5 %collective-permute-start.99 = (bf16[256,1024]{1,0:T(8,128)(2,1)}, bf16[256,1024]{1,0:T(8,128)(2,1)S(1)}, u32[]{:S(2)}, u32[]{:S(2)}) collective-permute-start(bf16[256,1024]{1,0:T(8,128)(2,1)} %get-tuple-element.381), channel_id=1, source_target_pairs={{0,3},{1,0},{2,1},{3,2},{4,7},{5,4},{6,5},{7,6},{8,11},{9,8},{10,9... | collective-permute-start | bytes 1572872 | tf_op jit(solution)/shard_map/ppermute | solution.py:28
  40.8 1.6 %copy-done.2 = f32[1,1024,512]{2,1,0:T(8,128)S(1)} copy-done((f32[1,1024,512]{2,1,0:T(8,128)S(1)}, f32[1,1024,512]{2,1,0:T(8,128)}, u32[]{:S(2)}) %copy-start.2) | copy-done | bytes 2097176
  42.4 1.6 %copy-done.4 = f32[1024,512]{1,0:T(8,128)S(1)} copy-done((f32[1024,512]{1,0:T(8,128)S(1)}, f32[1024,512]{1,0:T(8,128)}, u32[]{:S(2)}) %copy-start.4) | copy-done | bytes 2097176
  46.1 6.4 %shard_map.48 = (bf16[1360,1024]{1,0:T(8,128)(2,1)S(1)}, f32[1360,512]{1,0:T(8,128)S(1)}, bf16[1024,512]{1,0:T(8,128)(2,1)S(1)}, f32[1024,512]{1,0:T(8,128)S(1)}) custom-call(s32[1,28]{1,0:T(1,128)S(1)} %copy-done.13, bf16[448,4096]{1,0:T(8,128)(2,1)} %bitcast.13, bf16[448,512]{1,0:T(8,128)(2,1)S(1)} %bitcast.10, f32[1024,512]{1,0:T(8,128)S(1)} %bitcast.9, ...), custom_call_target="tpu_custom_call" | custom-call | flops 2047868928 | bytes 10485760 | tf_op jit(solution)/shard_map/pallas_call | solution.py:443
  52.5 2.1 %shard_map.50 = (f32[224,256]{1,0:T(8,128)S(1)}, bf16[224,256]{1,0:T(8,128)(2,1)S(1)}, bf16[448,256]{1,0:T(8,128)(2,1)S(1)}, f32[224,256]{1,0:T(8,128)S(1)}, bf1...) custom-call(s32[1,28]{1,0:T(1,128)S(1)} %copy-done.13, ...), custom_call_target="tpu_custom_call", output_to_operand_aliasing={{6}: (2, {})} | custom-call | flops 536870912 | bytes 5570560 | tf_op jit(solution)/shard_map/pallas_call | solution.py:473
  57.3 2.7 %collective-permute-start.111 = (bf16[224,256]{1,0:T(8,128)(2,1)}, bf16[224,256]{1,0:T(8,128)(2,1)S(1)}, u32[]{:S(2)}, u32[]{:S(2)}) collective-permute-start(bf16[224,256]{1,0:T(8,128)(2,1)} %copy-done.15), channel_id=1, source_target_pairs={{0,1},{1,0},{2,3},{3,2},{4,5},{5,4},{6,7},{7,6},{8,9},{9,8},{10,11... | collective-permute-start | bytes 344072 | tf_op jit(solution)/shard_map/ppermute | solution.py:334
  61.3 2.2 %collective-permute-start.103 = (bf16[224,256]{1,0:T(8,128)(2,1)}, bf16[224,256]{1,0:T(8,128)(2,1)S(1)}, u32[]{:S(2)}, u32[]{:S(2)}) collective-permute-start(bf16[224,256]{1,0:T(8,128)(2,1)} %copy-done.14), channel_id=1, source_target_pairs={{0,1},{1,0},{2,3},{3,2},{4,5},{5,4},{6,7},{7,6},{8,9},{9,8},{10,11... | collective-permute-start | bytes 344072 | tf_op jit(solution)/shard_map/ppermute | solution.py:334
  63.5 2.0 %collective-permute-done.108 = bf16[448,256]{1,0:T(8,128)(2,1)} collective-permute-done((bf16[448,256]{1,0:T(8,128)(2,1)}, bf16[448,256]{1,0:T(8,128)(2,1)}, u32[]{:S(2)}, u32[]{:S(2)}) %collective-permute-start.108) | collective-permute-done | bytes 229408 | tf_op jit(solution)/shard_map/ppermute | solution.py:334
  66.6 2.1 %collective-permute-start.109 = (bf16[224,256]{1,0:T(8,128)(2,1)S(1)}, bf16[224,256]{1,0:T(8,128)(2,1)S(1)}, u32[]{:S(2)}, u32[]{:S(2)}) collective-permute-start(bf16[224,256]{1,0:T(8,128)(2,1)S(1)} %get-tuple-element.397), channel_id=1, source_target_pairs={{1,2},{2,1},{5,6},{6,5},{9,10},{10,9},{13,14},{14,13},{17,18},{18,... | collective-permute-start | bytes 344072 | tf_op jit(solution)/shard_map/ppermute | solution.py:334
  71.0 3.6 %collective-permute-start.101 = (bf16[224,256]{1,0:T(8,128)(2,1)S(1)}, bf16[224,256]{1,0:T(8,128)(2,1)S(1)}, u32[]{:S(2)}, u32[]{:S(2)}) collective-permute-start(bf16[224,256]{1,0:T(8,128)(2,1)S(1)} %get-tuple-element.399), channel_id=1, source_target_pairs={{1,2},{2,1},{5,6},{6,5},{9,10},{10,9},{13,14},{14,13},{17,18},{18,... | collective-permute-start | bytes 344072 | tf_op jit(solution)/shard_map/ppermute | solution.py:334
  76.1 1.9 %collective-permute-start.112 = (bf16[224,256]{1,0:T(8,128)(2,1)S(1)}, bf16[224,256]{1,0:T(8,128)(2,1)S(1)}, u32[]{:S(2)}, u32[]{:S(2)}) collective-permute-start(bf16[224,256]{1,0:T(8,128)(2,1)S(1)} %add_convert_fusion.2.refs_0_), channel_id=1, source_target_pairs={{0,1},{1,2},{2,3},{4,5},{5,6},{6,7},{8,9},{9,10},{10,11},{12,13},{... | collective-permute-start | bytes 344072 | tf_op jit(solution)/shard_map/ppermute | solution.py:334
  78.0 3.4 %collective-permute-start.113 = (bf16[224,256]{1,0:T(8,128)(2,1)S(1)}, bf16[224,256]{1,0:T(8,128)(2,1)S(1)}, u32[]{:S(2)}, u32[]{:S(2)}) collective-permute-start(bf16[224,256]{1,0:T(8,128)(2,1)S(1)} %add_convert_fusion.2.refs_0_), channel_id=1, source_target_pairs={{1,0},{2,1},{3,2},{5,4},{6,5},{7,6},{9,8},{10,9},{11,10},{13,12},{... | collective-permute-start | bytes 344072 | tf_op jit(solution)/shard_map/ppermute | solution.py:334
  82.8 1.9 %collective-permute-start.104 = (bf16[224,256]{1,0:T(8,128)(2,1)S(1)}, bf16[224,256]{1,0:T(8,128)(2,1)S(1)}, u32[]{:S(2)}, u32[]{:S(2)}) collective-permute-start(bf16[224,256]{1,0:T(8,128)(2,1)S(1)} %add_convert_fusion.3.refs_0_), channel_id=1, source_target_pairs={{0,1},{1,2},{2,3},{4,5},{5,6},{6,7},{8,9},{9,10},{10,11},{12,13},{... | collective-permute-start | bytes 344072 | tf_op jit(solution)/shard_map/ppermute | solution.py:334
  84.7 3.4 %collective-permute-start.105 = (bf16[224,256]{1,0:T(8,128)(2,1)S(1)}, bf16[224,256]{1,0:T(8,128)(2,1)S(1)}, u32[]{:S(2)}, u32[]{:S(2)}) collective-permute-start(bf16[224,256]{1,0:T(8,128)(2,1)S(1)} %add_convert_fusion.3.refs_0_), channel_id=1, source_target_pairs={{1,0},{2,1},{3,2},{5,4},{6,5},{7,6},{9,8},{10,9},{11,10},{13,12},{... | collective-permute-start | bytes 344072 | tf_op jit(solution)/shard_map/ppermute | solution.py:334
  89.4 5.5 %collective-permute-start.115 = (bf16[448,256]{1,0:T(8,128)(2,1)S(1)}, bf16[448,256]{1,0:T(8,128)(2,1)S(1)}, u32[]{:S(2)}, u32[]{:S(2)}) collective-permute-start(bf16[448,256]{1,0:T(8,128)(2,1)S(1)} %pad_maximum_fusion.1), channel_id=1, source_target_pairs={{1,0},{2,3},{5,4},{6,7},{9,8},{10,11},{13,12},{14,15},{17,16},{18,... | collective-permute-start | bytes 688136 | tf_op jit(solution)/shard_map/ppermute | solution.py:334
  95.1 1.6 %collective-permute-start.107 = (bf16[448,256]{1,0:T(8,128)(2,1)S(1)}, bf16[448,256]{1,0:T(8,128)(2,1)S(1)}, u32[]{:S(2)}, u32[]{:S(2)}) collective-permute-start(bf16[448,256]{1,0:T(8,128)(2,1)S(1)} %pad_maximum_fusion), channel_id=1, source_target_pairs={{1,0},{2,3},{5,4},{6,7},{9,8},{10,11},{13,12},{14,15},{17,16},{18,... | collective-permute-start | bytes 688136 | tf_op jit(solution)/shard_map/ppermute | solution.py:334
  96.7 1.4 %shard_map.49.turned_ref = bf16[1024,896]{1,0:T(8,128)(2,1)S(1)} custom-call(s32[1,28]{1,0:T(1,128)S(1)} %copy-done.13, bf16[1360,1024]{1,0:T(8,128)(2,1)S(1)} %get-tuple-element.379.rows_ref, bf16[256,1024]{1,0:T(8,128)(2,1)S(1)} %collective-permute-done.98.refs_0_, bf16[256,1024]{1,0:T(8,128)(2,1)S(1)} %copy-done.1), custom_call_target="tpu_custom_call" | custom-call | bytes 3670016 | tf_op jit(solution)/shard_map/pallas_call | solution.py:486
  100.0 19.0 %collective-permute-start.121 = (bf16[1024,256]{1,0:T(8,128)(2,1)S(1)}, bf16[1024,256]{1,0:T(8,128)(2,1)S(1)}, u32[]{:S(2)}, u32[]{:S(2)}) collective-permute-start(bf16[1024,256]{1,0:T(8,128)(2,1)S(1)} %get-tuple-element.396), channel_id=1, source_target_pairs={{0,4},{4,0},{8,12},{12,8},{16,20},{20,16},{24,28},{28,24},{1,5},{5... | collective-permute-start | bytes 1572872 | tf_op jit(solution)/shard_map/ppermute | solution.py:22
  121.8 3.6 %collective-permute-start.117 = (f32[8,128]{1,0:T(8,128)S(1)}, f32[8,128]{1,0:T(8,128)S(1)}, u32[]{:S(2)}, u32[]{:S(2)}) collective-permute-start(f32[8,128]{1,0:T(8,128)S(1)} %add.292), channel_id=1, source_target_pairs={{0,2},{1,3},{2,0},{3,1},{4,6},{5,7},{6,4},{7,5},{8,10},{9,11},{10,... | collective-permute-start | bytes 12296 | tf_op jit(solution)/shard_map/ppermute | solution.py:28
  126.4 1.4 %collective-permute-done.118 = f32[8,128]{1,0:T(8,128)S(1)} collective-permute-done((f32[8,128]{1,0:T(8,128)S(1)}, f32[8,128]{1,0:T(8,128)S(1)}, u32[]{:S(2)}, u32[]{:S(2)}) %collective-permute-start.118) | collective-permute-done | bytes 4128 | tf_op jit(solution)/shard_map/ppermute | solution.py:28
  127.9 1.8 %collective-permute-start.119 = (f32[8,128]{1,0:T(8,128)S(1)}, f32[8,128]{1,0:T(8,128)S(1)}, u32[]{:S(2)}, u32[]{:S(2)}) collective-permute-start(f32[8,128]{1,0:T(8,128)S(1)} %add_add_fusion.32.own_ref), channel_id=1, source_target_pairs={{0,4},{4,0},{8,12},{12,8},{16,20},{20,16},{24,28},{28,24},{1,5},{5... | collective-permute-start | bytes 12296 | tf_op jit(solution)/shard_map/ppermute | solution.py:22
  130.5 1.7 %shard_map.53 = f32[1024,512]{1,0:T(8,128)} custom-call(f32[8,128]{1,0:T(8,128)S(1)} %add_add_fusion.32.own_ref, f32[8,128]{1,0:T(8,128)S(1)} %collective-permute-done.119.other_ref, f32[1024,512]{1,0:T(8,128)S(1)} %copy-done.6, f32[1024,256]{1,0:T(8,128)S(1)} %get-tuple-element.393.refs_0_, f32[1024,256]{1,0:T(8,128)S(1)} %get-tuple-element.394.refs_1_, ...), custom_call_target="tpu_custom_call" | custom-call | tf_op jit(solution)/shard_map/pallas_call | solution.py:523
  (90 shorter events, 27.5 us)
Async XLA Ops:
  0.0 39.5 %collective-permute-start.96 = (f32[1024,512]{1,0:T(8,128)}, f32[1024,512]{1,0:T(8,128)S(1)}, u32[]{:S(2)}, u32[]{:S(2)}) collective-permute-start(f32[1024,512]{1,0:T(8,128)} %bitcast.8), channel_id=1, source_target_pairs={{0,4},{4,0},{8,12},{12,8},{16,20},{20,16},{24,28},{28,24},{1,5},{5... | collective-permute-start | bytes 6291464 | tf_op jit(solution)/shard_map/ppermute | solution.py:22
  4.7 34.0 %collective-permute-start.97 = (bf16[256,1024]{1,0:T(8,128)(2,1)}, bf16[256,1024]{1,0:T(8,128)(2,1)S(1)}, u32[]{:S(2)}, u32[]{:S(2)}) collective-permute-start(bf16[256,1024]{1,0:T(8,128)(2,1)} %get-tuple-element.374), channel_id=1, source_target_pairs={{0,2},{1,3},{2,0},{3,1},{4,6},{5,7},{6,4},{7,5},{8,10},{9,11},{10,... | collective-permute-start | bytes 1572872 | tf_op jit(solution)/shard_map/ppermute | solution.py:28
  17.5 2.7 %collective-permute-start.51 = (bf16[32,1024]{1,0:T(8,128)(2,1)S(1)}, bf16[32,1024]{1,0:T(8,128)(2,1)S(1)}, u32[]{:S(2)}, u32[]{:S(2)}) collective-permute-start(bf16[32,1024]{1,0:T(8,128)(2,1)S(1)} %slice.229), channel_id=1, source_target_pairs={{2,0},{6,4},{10,8},{14,12},{18,16},{22,20},{26,24},{30,28}} | collective-permute-start | bytes 196616 | tf_op jit(solution)/shard_map/cond/branch_2_fun/ppermute | solution.py:327
  18.2 2.0 %collective-permute-start.52 = (bf16[32,1024]{1,0:T(8,128)(2,1)S(1)}, bf16[32,1024]{1,0:T(8,128)(2,1)S(1)}, u32[]{:S(2)}, u32[]{:S(2)}) collective-permute-start(bf16[32,1024]{1,0:T(8,128)(2,1)S(1)} %slice.230), channel_id=1, source_target_pairs={{2,3},{6,7},{10,11},{14,15},{18,19},{22,23},{26,27},{30,31}} | collective-permute-start | bytes 196616 | tf_op jit(solution)/shard_map/cond/branch_2_fun/ppermute | solution.py:327
  18.9 14.2 %collective-permute-start.53 = (bf16[32,1024]{1,0:T(8,128)(2,1)S(1)}, bf16[32,1024]{1,0:T(8,128)(2,1)S(1)}, u32[]{:S(2)}, u32[]{:S(2)}) collective-permute-start(bf16[32,1024]{1,0:T(8,128)(2,1)S(1)} %slice.231), channel_id=1, source_target_pairs={{2,1},{6,5},{10,9},{14,13},{18,17},{22,21},{26,25},{30,29}} | collective-permute-start | bytes 196616 | tf_op jit(solution)/shard_map/cond/branch_2_fun/ppermute | solution.py:327
  37.2 15.3 %collective-permute-start.98 = (bf16[256,1024]{1,0:T(8,128)(2,1)}, bf16[256,1024]{1,0:T(8,128)(2,1)S(1)}, u32[]{:S(2)}, u32[]{:S(2)}) collective-permute-start(bf16[256,1024]{1,0:T(8,128)(2,1)} %get-tuple-element.380), channel_id=1, source_target_pairs={{0,1},{1,2},{2,3},{3,0},{4,5},{5,6},{6,7},{7,4},{8,9},{9,10},{10,1... | collective-permute-start | bytes 1572872 | tf_op jit(solution)/shard_map/ppermute | solution.py:28
  37.3 15.2 %collective-permute-start.99 = (bf16[256,1024]{1,0:T(8,128)(2,1)}, bf16[256,1024]{1,0:T(8,128)(2,1)S(1)}, u32[]{:S(2)}, u32[]{:S(2)}) collective-permute-start(bf16[256,1024]{1,0:T(8,128)(2,1)} %get-tuple-element.381), channel_id=1, source_target_pairs={{0,3},{1,0},{2,1},{3,2},{4,7},{5,4},{6,5},{7,6},{8,11},{9,8},{10,9... | collective-permute-start | bytes 1572872 | tf_op jit(solution)/shard_map/ppermute | solution.py:28
  56.0 9.5 %collective-permute-start.108 = (bf16[448,256]{1,0:T(8,128)(2,1)}, bf16[448,256]{1,0:T(8,128)(2,1)}, u32[]{:S(2)}, u32[]{:S(2)}) collective-permute-start(bf16[448,256]{1,0:T(8,128)(2,1)} %get-tuple-element.389), channel_id=1, source_target_pairs={{0,1},{3,2},{4,5},{7,6},{8,9},{11,10},{12,13},{15,14},{16,17},{19,... | collective-permute-start | bytes 688136 | tf_op jit(solution)/shard_map/ppermute | solution.py:334
  57.3 18.7 %copy-start.11 = (f32[224,256]{1,0:T(8,128)S(1)}, f32[224,256]{1,0:T(8,128)}, u32[]{:S(2)}) copy-start(f32[224,256]{1,0:T(8,128)} %copy-done.10) | copy-start | bytes 688132
  57.3 17.4 %collective-permute-start.111 = (bf16[224,256]{1,0:T(8,128)(2,1)}, bf16[224,256]{1,0:T(8,128)(2,1)S(1)}, u32[]{:S(2)}, u32[]{:S(2)}) collective-permute-start(bf16[224,256]{1,0:T(8,128)(2,1)} %copy-done.15), channel_id=1, source_target_pairs={{0,1},{1,0},{2,3},{3,2},{4,5},{5,4},{6,7},{7,6},{8,9},{9,8},{10,11... | collective-permute-start | bytes 344072 | tf_op jit(solution)/shard_map/ppermute | solution.py:334
  60.0 10.0 %collective-permute-start.100 = (bf16[448,256]{1,0:T(8,128)(2,1)}, bf16[448,256]{1,0:T(8,128)(2,1)S(1)}, u32[]{:S(2)}, u32[]{:S(2)}) collective-permute-start(bf16[448,256]{1,0:T(8,128)(2,1)} %copy-done.12), channel_id=1, source_target_pairs={{0,1},{3,2},{4,5},{7,6},{8,9},{11,10},{12,13},{15,14},{16,17},{19,... | collective-permute-start | bytes 688136 | tf_op jit(solution)/shard_map/ppermute | solution.py:334
  61.3 20.1 %collective-permute-start.103 = (bf16[224,256]{1,0:T(8,128)(2,1)}, bf16[224,256]{1,0:T(8,128)(2,1)S(1)}, u32[]{:S(2)}, u32[]{:S(2)}) collective-permute-start(bf16[224,256]{1,0:T(8,128)(2,1)} %copy-done.14), channel_id=1, source_target_pairs={{0,1},{1,0},{2,3},{3,2},{4,5},{5,4},{6,7},{7,6},{8,9},{9,8},{10,11... | collective-permute-start | bytes 344072 | tf_op jit(solution)/shard_map/ppermute | solution.py:334
  66.6 30.1 %copy-start.1 = (bf16[256,1024]{1,0:T(8,128)(2,1)S(1)}, bf16[256,1024]{1,0:T(8,128)(2,1)}, u32[]{:S(2)}) copy-start(bf16[256,1024]{1,0:T(8,128)(2,1)} %copy-done) | copy-start | bytes 1572868
  66.6 9.4 %collective-permute-start.109 = (bf16[224,256]{1,0:T(8,128)(2,1)S(1)}, bf16[224,256]{1,0:T(8,128)(2,1)S(1)}, u32[]{:S(2)}, u32[]{:S(2)}) collective-permute-start(bf16[224,256]{1,0:T(8,128)(2,1)S(1)} %get-tuple-element.397), channel_id=1, source_target_pairs={{1,2},{2,1},{5,6},{6,5},{9,10},{10,9},{13,14},{14,13},{17,18},{18,... | collective-permute-start | bytes 344072 | tf_op jit(solution)/shard_map/ppermute | solution.py:334
  68.7 7.3 %collective-permute-start.110 = (bf16[224,256]{1,0:T(8,128)(2,1)S(1)}, bf16[224,256]{1,0:T(8,128)(2,1)S(1)}, u32[]{:S(2)}, u32[]{:S(2)}) collective-permute-start(bf16[224,256]{1,0:T(8,128)(2,1)S(1)} %get-tuple-element.398), channel_id=1, source_target_pairs={{1,3},{2,0},{5,7},{6,4},{9,11},{10,8},{13,15},{14,12},{17,19},{18,... | collective-permute-start | bytes 344072 | tf_op jit(solution)/shard_map/ppermute | solution.py:334
  71.0 11.6 %collective-permute-start.101 = (bf16[224,256]{1,0:T(8,128)(2,1)S(1)}, bf16[224,256]{1,0:T(8,128)(2,1)S(1)}, u32[]{:S(2)}, u32[]{:S(2)}) collective-permute-start(bf16[224,256]{1,0:T(8,128)(2,1)S(1)} %get-tuple-element.399), channel_id=1, source_target_pairs={{1,2},{2,1},{5,6},{6,5},{9,10},{10,9},{13,14},{14,13},{17,18},{18,... | collective-permute-start | bytes 344072 | tf_op jit(solution)/shard_map/ppermute | solution.py:334
  74.7 8.0 %collective-permute-start.102 = (bf16[224,256]{1,0:T(8,128)(2,1)S(1)}, bf16[224,256]{1,0:T(8,128)(2,1)S(1)}, u32[]{:S(2)}, u32[]{:S(2)}) collective-permute-start(bf16[224,256]{1,0:T(8,128)(2,1)S(1)} %get-tuple-element.400), channel_id=1, source_target_pairs={{1,3},{2,0},{5,7},{6,4},{9,11},{10,8},{13,15},{14,12},{17,19},{18,... | collective-permute-start | bytes 344072 | tf_op jit(solution)/shard_map/ppermute | solution.py:334
  76.1 12.0 %collective-permute-start.112 = (bf16[224,256]{1,0:T(8,128)(2,1)S(1)}, bf16[224,256]{1,0:T(8,128)(2,1)S(1)}, u32[]{:S(2)}, u32[]{:S(2)}) collective-permute-start(bf16[224,256]{1,0:T(8,128)(2,1)S(1)} %add_convert_fusion.2.refs_0_), channel_id=1, source_target_pairs={{0,1},{1,2},{2,3},{4,5},{5,6},{6,7},{8,9},{9,10},{10,11},{12,13},{... | collective-permute-start | bytes 344072 | tf_op jit(solution)/shard_map/ppermute | solution.py:334
  78.0 11.4 %collective-permute-start.113 = (bf16[224,256]{1,0:T(8,128)(2,1)S(1)}, bf16[224,256]{1,0:T(8,128)(2,1)S(1)}, u32[]{:S(2)}, u32[]{:S(2)}) collective-permute-start(bf16[224,256]{1,0:T(8,128)(2,1)S(1)} %add_convert_fusion.2.refs_0_), channel_id=1, source_target_pairs={{1,0},{2,1},{3,2},{5,4},{6,5},{7,6},{9,8},{10,9},{11,10},{13,12},{... | collective-permute-start | bytes 344072 | tf_op jit(solution)/shard_map/ppermute | solution.py:334
  81.4 8.0 %collective-permute-start.114 = (bf16[224,256]{1,0:T(8,128)(2,1)S(1)}, bf16[224,256]{1,0:T(8,128)(2,1)S(1)}, u32[]{:S(2)}, u32[]{:S(2)}) collective-permute-start(bf16[224,256]{1,0:T(8,128)(2,1)S(1)} %add_convert_fusion.2.refs_0_), channel_id=1, source_target_pairs={{0,2},{3,1},{4,6},{7,5},{8,10},{11,9},{12,14},{15,13},{16,18},{19,... | collective-permute-start | bytes 344072 | tf_op jit(solution)/shard_map/ppermute | solution.py:334
  82.8 12.2 %collective-permute-start.104 = (bf16[224,256]{1,0:T(8,128)(2,1)S(1)}, bf16[224,256]{1,0:T(8,128)(2,1)S(1)}, u32[]{:S(2)}, u32[]{:S(2)}) collective-permute-start(bf16[224,256]{1,0:T(8,128)(2,1)S(1)} %add_convert_fusion.3.refs_0_), channel_id=1, source_target_pairs={{0,1},{1,2},{2,3},{4,5},{5,6},{6,7},{8,9},{9,10},{10,11},{12,13},{... | collective-permute-start | bytes 344072 | tf_op jit(solution)/shard_map/ppermute | solution.py:334
  84.7 10.3 %collective-permute-start.105 = (bf16[224,256]{1,0:T(8,128)(2,1)S(1)}, bf16[224,256]{1,0:T(8,128)(2,1)S(1)}, u32[]{:S(2)}, u32[]{:S(2)}) collective-permute-start(bf16[224,256]{1,0:T(8,128)(2,1)S(1)} %add_convert_fusion.3.refs_0_), channel_id=1, source_target_pairs={{1,0},{2,1},{3,2},{5,4},{6,5},{7,6},{9,8},{10,9},{11,10},{13,12},{... | collective-permute-start | bytes 344072 | tf_op jit(solution)/shard_map/ppermute | solution.py:334
  88.1 7.0 %collective-permute-start.106 = (bf16[224,256]{1,0:T(8,128)(2,1)S(1)}, bf16[224,256]{1,0:T(8,128)(2,1)S(1)}, u32[]{:S(2)}, u32[]{:S(2)}) collective-permute-start(bf16[224,256]{1,0:T(8,128)(2,1)S(1)} %add_convert_fusion.3.refs_0_), channel_id=1, source_target_pairs={{0,2},{3,1},{4,6},{7,5},{8,10},{11,9},{12,14},{15,13},{16,18},{19,... | collective-permute-start | bytes 344072 | tf_op jit(solution)/shard_map/ppermute | solution.py:334
  89.4 9.3 %collective-permute-start.115 = (bf16[448,256]{1,0:T(8,128)(2,1)S(1)}, bf16[448,256]{1,0:T(8,128)(2,1)S(1)}, u32[]{:S(2)}, u32[]{:S(2)}) collective-permute-start(bf16[448,256]{1,0:T(8,128)(2,1)S(1)} %pad_maximum_fusion.1), channel_id=1, source_target_pairs={{1,0},{2,3},{5,4},{6,7},{9,8},{10,11},{13,12},{14,15},{17,16},{18,... | collective-permute-start | bytes 688136 | tf_op jit(solution)/shard_map/ppermute | solution.py:334
  95.1 24.0 %collective-permute-start.107 = (bf16[448,256]{1,0:T(8,128)(2,1)S(1)}, bf16[448,256]{1,0:T(8,128)(2,1)S(1)}, u32[]{:S(2)}, u32[]{:S(2)}) collective-permute-start(bf16[448,256]{1,0:T(8,128)(2,1)S(1)} %pad_maximum_fusion), channel_id=1, source_target_pairs={{1,0},{2,3},{5,4},{6,7},{9,8},{10,11},{13,12},{14,15},{17,16},{18,... | collective-permute-start | bytes 688136 | tf_op jit(solution)/shard_map/ppermute | solution.py:334
  98.1 32.4 %copy-start.6 = (f32[1024,512]{1,0:T(8,128)S(1)}, f32[1024,512]{1,0:T(8,128)}, u32[]{:S(2)}) copy-start(f32[1024,512]{1,0:T(8,128)} %copy-done.5) | copy-start | bytes 6291460
  100.0 30.5 %collective-permute-start.121 = (bf16[1024,256]{1,0:T(8,128)(2,1)S(1)}, bf16[1024,256]{1,0:T(8,128)(2,1)S(1)}, u32[]{:S(2)}, u32[]{:S(2)}) collective-permute-start(bf16[1024,256]{1,0:T(8,128)(2,1)S(1)} %get-tuple-element.396), channel_id=1, source_target_pairs={{0,4},{4,0},{8,12},{12,8},{16,20},{20,16},{24,28},{28,24},{1,5},{5... | collective-permute-start | bytes 1572872 | tf_op jit(solution)/shard_map/ppermute | solution.py:22
  120.3 10.2 %collective-permute-start.120 = (bf16[1024,256]{1,0:T(8,128)(2,1)S(1)}, bf16[1024,256]{1,0:T(8,128)(2,1)S(1)}, u32[]{:S(2)}, u32[]{:S(2)}) collective-permute-start(bf16[1024,256]{1,0:T(8,128)(2,1)S(1)} %get-tuple-element.395), channel_id=1, source_target_pairs={{0,4},{4,0},{8,12},{12,8},{16,20},{20,16},{24,28},{28,24},{1,5},{5... | collective-permute-start | bytes 1572872 | tf_op jit(solution)/shard_map/ppermute | solution.py:22
  121.1 4.3 %collective-permute-start.116 = (f32[8,128]{1,0:T(8,128)S(1)}, f32[8,128]{1,0:T(8,128)S(1)}, u32[]{:S(2)}, u32[]{:S(2)}) collective-permute-start(f32[8,128]{1,0:T(8,128)S(1)} %add.292), channel_id=1, source_target_pairs={{0,1},{1,2},{2,3},{3,0},{4,5},{5,6},{6,7},{7,4},{8,9},{9,10},{10,1... | collective-permute-start | bytes 12296 | tf_op jit(solution)/shard_map/ppermute | solution.py:28
  121.8 4.7 %collective-permute-start.117 = (f32[8,128]{1,0:T(8,128)S(1)}, f32[8,128]{1,0:T(8,128)S(1)}, u32[]{:S(2)}, u32[]{:S(2)}) collective-permute-start(f32[8,128]{1,0:T(8,128)S(1)} %add.292), channel_id=1, source_target_pairs={{0,2},{1,3},{2,0},{3,1},{4,6},{5,7},{6,4},{7,5},{8,10},{9,11},{10,... | collective-permute-start | bytes 12296 | tf_op jit(solution)/shard_map/ppermute | solution.py:28
  125.4 2.5 %collective-permute-start.118 = (f32[8,128]{1,0:T(8,128)S(1)}, f32[8,128]{1,0:T(8,128)S(1)}, u32[]{:S(2)}, u32[]{:S(2)}) collective-permute-start(f32[8,128]{1,0:T(8,128)S(1)} %add.292), channel_id=1, source_target_pairs={{0,3},{1,0},{2,1},{3,2},{4,7},{5,4},{6,5},{7,6},{8,11},{9,8},{10,9... | collective-permute-start | bytes 12296 | tf_op jit(solution)/shard_map/ppermute | solution.py:28
  127.9 2.6 %collective-permute-start.119 = (f32[8,128]{1,0:T(8,128)S(1)}, f32[8,128]{1,0:T(8,128)S(1)}, u32[]{:S(2)}, u32[]{:S(2)}) collective-permute-start(f32[8,128]{1,0:T(8,128)S(1)} %add_add_fusion.32.own_ref), channel_id=1, source_target_pairs={{0,4},{4,0},{8,12},{12,8},{16,20},{20,16},{24,28},{28,24},{1,5},{5... | collective-permute-start | bytes 12296 | tf_op jit(solution)/shard_map/ppermute | solution.py:22
  (13 other events, 20.7 us)

commit v3 on v1

--- a/solution.py
+++ b/solution.py
@@ -26,6 +26,19 @@
     members = lax.axis_size("fsdp")
     ring = [(source, (source + distance) % members) for source in range(members)]
     return lax.ppermute(value, "fsdp", ring)
+
+
+def sent_across(value, bit, distance):
+    members = lax.axis_size("fsdp")
+    pairs = [
+        (
+            replica * members + member,
+            (replica ^ 2**bit) * members + (member + distance) % members,
+        )
+        for replica in range(lax.axis_size("replica"))
+        for member in range(members)
+    ]
+    return lax.ppermute(value, ("replica", "fsdp"), pairs)
 
 
 def live_before(lengths_ref, members):
@@ -104,8 +117,8 @@
 
 def sent_kernel(members, offsets, sizes, lengths_ref, features_ref, *refs):
     count = len(offsets)
-    outs, choice_ref = refs[: 2 * count], refs[2 * count]
-    block_ref, first_ref, more_ref, sems, out_sems, more_sems = refs[2 * count + 1 :]
+    outs, choice_refs = refs[: 2 * count], refs[2 * count : -6]
+    block_ref, first_ref, more_ref, sems, out_sems, more_sems = refs[-6:]
     index = lax.axis_index("fsdp")
     blocks = [
         Block(features_ref, lax.rem(index + i, members), block_ref.at[n], sems.at[n])
@@ -144,8 +157,8 @@
             copy.start()
             copy.wait()
 
-    for member, choice in enumerate(used_places(totals, first, sizes)):
-        choice_ref[member] = choice
+    for choice_ref, choice in zip(choice_refs, used_places(totals, first, sizes)):
+        choice_ref[0] = choice
     for copy in copies:
         copy.wait()
 
@@ -331,17 +344,17 @@
     def cost(flops, moved):
         return pl.CostEstimate(flops=flops, bytes_accessed=moved, transcendentals=0)
 
-    def sent_to(offsets):
+    def sent_to(offsets, choices):
         count = len(offsets)
         pieces = max(1, local_rows // 256)
-        *arrays, choice = pl.pallas_call(
+        arrays = pl.pallas_call(
             functools.partial(sent_kernel, members, offsets, sizes),
             in_specs=[smem, anywhere],
-            out_specs=[anywhere] * (2 * count) + [smem],
+            out_specs=[anywhere] * (2 * count) + [smem] * choices,
             out_shape=[
                 array(rows, local_rows, jnp.bfloat16) for rows in (first, more) for _ in offsets
             ]
-            + [jax.ShapeDtypeStruct((members,), jnp.int32)],
+            + [jax.ShapeDtypeStruct((1,), jnp.int32)] * choices,
             scratch_shapes=[
                 pltpu.VMEM((count, tokens_here, local_rows), jnp.bfloat16),
                 pltpu.VMEM((count, first, local_rows), jnp.bfloat16),
@@ -356,17 +369,17 @@
                 2 * count * (tokens_here + first) * local_rows,
             ),
         )(lengths, features)
-        return arrays[:count], arrays[count:], choice
+        return arrays[:count], arrays[count : 2 * count], arrays[2 * count :]
 
     far = members // 2
     near = [i for i in range(1, members) if i != far]
-    far_first, far_more, choice = sent_to([far])
-    near_first, near_more, _ = sent_to(near)
+    far_first, far_more, choice = sent_to([far], members)
+    near_first, near_more, _ = sent_to(near, 0)
     held_far = turned(far_first[0], far)
     offsets = [far] + near
     held_more = [
         lax.switch(
-            choice[source],
+            choice[source][0],
             [functools.partial(more_rows, size, source, offsets) for size in sizes],
             far_more + near_more,
         )
@@ -452,10 +465,11 @@
         partners.append(swapped(low_gradient, "replica", distance_bit))
         squares = squares + own_squares
 
-    total = squares
-    for i in range(1, members):
-        total = total + turned(squares, i)
-    partner_total = swapped(total, "replica", distance_bit)
+    total, partner_total = squares, 0.0
+    for i in range(members):
+        if i:
+            total = total + turned(squares, i)
+        partner_total = partner_total + sent_across(squares, distance_bit, i)
 
     averaged = pl.pallas_call(
         functools.partial(average_kernel, members * local_rows * columns),

time: 117 us -> 123 us (1.051)
  the two profiles are of different devices: /device:TPU:7 before, /device:TPU:2 now
where the time goes in v3:
time: 123 us; the launch traced here: 124 us
  starting transfers between devices  48.4 us (39%)
  waiting for transfers between devices  43.9 us (36%)
  Pallas kernels  23.7 us (19%)
  local copies, waits for them, and re-layouts  4.39 us (4%)
  between operations  2.92 us (2%)
    ppermute x18, starting transfers between devices, turned(): return lax.ppermute(value, 'fsdp', ring)  36.8 us
    ppermute x18, waiting for transfers between devices, turned(): return lax.ppermute(value, 'fsdp', ring)  32.1 us
    ppermute x6, waiting for transfers between devices, more_rows(): lax.ppermute(block[:size], 'fsdp', [(source, (source + i) % members)])  9.96 us
    pallas_call x2, Pallas kernels, sent_to(): pl.pallas_call(functools.partial(sent_kernel, members, offsets, sizes), i...  9.46 us
    ppermute x6, starting transfers between devices, more_rows(): lax.ppermute(block[:size], 'fsdp', [(source, (source + i) % members)])  8.29 us
    pallas_call x1, Pallas kernels, local(): pl.pallas_call(functools.partial(own_kernel, members, far, scale), in_spe...  7.35 us
    ppermute x4, starting transfers between devices, sent_across(): return lax.ppermute(value, ('replica', 'fsdp'), pairs)  3.18 us
    pallas_call x2, Pallas kernels, local(): pl.pallas_call(functools.partial(gradient_kernel, members), in_specs=[vme...  2.54 us
  transfers between devices with their start and end apart: 31, of which 13 were waited for; matrix products, arithmetic and copies ran while one was open for 2% of the time, Pallas kernels for 17%

profile of v3, /device:TPU:2, one launch (start us, length us, event | category | flops | bytes accessed | tf_op | source)
XLA Modules:
  0.0 123.9 jit_solution(10489513944680747558)
XLA Ops:
  0.0 4.1 %shard_map.47 = (bf16[256,1024]{1,0:T(8,128)(2,1)}, bf16[208,1024]{1,0:T(8,128)(2,1)S(1)}, s32[1]{0:T(128)}, s32[1]{0:T(128)}, s32[1]{0:T(128)}, /*index=5*/s32[1]{0:T(128)}) custom-call(s32[1,28]{1,0:T(1,128)} %lengths_ref.8, bf16[448,4096]{1,0:T(8,128)(2,1)} %bitcast.11), custom_call_target="tpu_custom_call" | custom-call | flops 234881024 | bytes 1441792 | tf_op jit(solution)/shard_map/pallas_call | solution.py:350
  4.1 2.6 %collective-permute-start.97 = (bf16[256,1024]{1,0:T(8,128)(2,1)}, bf16[256,1024]{1,0:T(8,128)(2,1)S(1)}, u32[]{:S(2)}, u32[]{:S(2)}) collective-permute-start(bf16[256,1024]{1,0:T(8,128)(2,1)} %get-tuple-element.382), channel_id=1, source_target_pairs={{0,2},{1,3},{2,0},{3,1},{4,6},{5,7},{6,4},{7,5},{8,10},{9,11},{10,... | collective-permute-start | bytes 1572872 | tf_op jit(solution)/shard_map/ppermute | solution.py:28
  9.2 5.4 %shard_map.46 = (bf16[256,1024]{1,0:T(8,128)(2,1)}, bf16[256,1024]{1,0:T(8,128)(2,1)}, bf16[208,1024]{1,0:T(8,128)(2,1)S(1)}, bf16[208,1024]{1,0:T(8,128)(2,1)S(1)}) custom-call(s32[1,28]{1,0:T(1,128)} %lengths_ref.8, bf16[448,4096]{1,0:T(8,128)(2,1)} %bitcast.12), custom_call_target="tpu_custom_call" | custom-call | flops 469762048 | bytes 2883584 | tf_op jit(solution)/shard_map/pallas_call | solution.py:350
  14.6 8.9 %conditional.7 = (bf16[208,1024]{1,0:T(8,128)(2,1)S(1)}) conditional(s32[]{:T(128)} %bitcast.4, bf16[208,1024]{1,0:T(8,128)(2,1)S(1)} %get-tuple-element.375, (bf16[208,1024]{1,0:T(8,128)(2,1)S(1)}, bf16[208,1024]{1,0:T(8,128)(2,1)S(1)}, bf16[208,1024]{1,0:T(8,128)(2,1)S(1)}) %tuple.114, ...), branch_computations={%region_27.28_spmd, %region_28.29_spmd, %region_29.30_spmd, %regio... | conditional | flops 425984 | bytes 6815872 | solution.py:381
  17.3 6.1 %collective-permute-done.73 = bf16[16,1024]{1,0:T(8,128)(2,1)S(1)} collective-permute-done((bf16[16,1024]{1,0:T(8,128)(2,1)S(1)}, bf16[16,1024]{1,0:T(8,128)(2,1)S(1)}, u32[]{:S(2)}, u32[]{:S(2)}) %collective-permute-start.73) | collective-permute-done | bytes 32800 | tf_op jit(solution)/shard_map/cond/branch_1_fun/ppermute | solution.py:312
  26.0 11.8 %conditional.4 = (bf16[208,1024]{1,0:T(8,128)(2,1)S(1)}) conditional(s32[]{:T(128)} %bitcast.1, bf16[208,1024]{1,0:T(8,128)(2,1)S(1)} %get-tuple-element.375, (bf16[208,1024]{1,0:T(8,128)(2,1)S(1)}, bf16[208,1024]{1,0:T(8,128)(2,1)}, bf16[208,1024]{1,0:T(8,128)(2,1)}) %tuple.160, (bf16[208,1024]{1,0:T(8,128)(2,1)S(1)}, ...), branch_computations={%region_0.0_spmd, %region_1.2_spmd, %region_2.3_spmd, %region_3.4_... | conditional | flops 425984 | bytes 6815872 | solution.py:381
  27.0 2.6 %collective-permute-start.8 = (bf16[48,1024]{1,0:T(8,128)(2,1)S(1)}, bf16[48,1024]{1,0:T(8,128)(2,1)S(1)}, u32[]{:S(2)}, u32[]{:S(2)}) collective-permute-start(bf16[48,1024]{1,0:T(8,128)(2,1)S(1)} %slice.176), channel_id=1, source_target_pairs={{0,3},{4,7},{8,11},{12,15},{16,19},{20,23},{24,27},{28,31}} | collective-permute-start | bytes 294920 | tf_op jit(solution)/shard_map/cond/branch_3_fun/ppermute | solution.py:312
  30.6 1.7 %collective-permute-start.7 = (bf16[48,1024]{1,0:T(8,128)(2,1)S(1)}, bf16[48,1024]{1,0:T(8,128)(2,1)S(1)}, u32[]{:S(2)}, u32[]{:S(2)}) collective-permute-start(bf16[48,1024]{1,0:T(8,128)(2,1)S(1)} %slice.175), channel_id=1, source_target_pairs={{0,1},{4,5},{8,9},{12,13},{16,17},{20,21},{24,25},{28,29}} | collective-permute-start | bytes 294920 | tf_op jit(solution)/shard_map/cond/branch_3_fun/ppermute | solution.py:312
  33.7 1.7 %collective-permute-done.7 = bf16[48,1024]{1,0:T(8,128)(2,1)S(1)} collective-permute-done((bf16[48,1024]{1,0:T(8,128)(2,1)S(1)}, bf16[48,1024]{1,0:T(8,128)(2,1)S(1)}, u32[]{:S(2)}, u32[]{:S(2)}) %collective-permute-start.7) | collective-permute-done | bytes 98336 | tf_op jit(solution)/shard_map/cond/branch_3_fun/ppermute | solution.py:312
  35.4 2.1 %collective-permute-done.6 = bf16[48,1024]{1,0:T(8,128)(2,1)S(1)} collective-permute-done((bf16[48,1024]{1,0:T(8,128)(2,1)S(1)}, bf16[48,1024]{1,0:T(8,128)(2,1)S(1)}, u32[]{:S(2)}, u32[]{:S(2)}) %collective-permute-start.6) | collective-permute-done | bytes 98336 | tf_op jit(solution)/shard_map/cond/branch_3_fun/ppermute | solution.py:312
  38.2 3.4 %collective-permute-start.99 = (bf16[256,1024]{1,0:T(8,128)(2,1)}, bf16[256,1024]{1,0:T(8,128)(2,1)S(1)}, u32[]{:S(2)}, u32[]{:S(2)}) collective-permute-start(bf16[256,1024]{1,0:T(8,128)(2,1)} %get-tuple-element.389), channel_id=1, source_target_pairs={{0,3},{1,0},{2,1},{3,2},{4,7},{5,4},{6,5},{7,6},{8,11},{9,8},{10,9... | collective-permute-start | bytes 1572872 | tf_op jit(solution)/shard_map/ppermute | solution.py:28
  41.6 7.4 %shard_map.48 = (bf16[1360,1024]{1,0:T(8,128)(2,1)S(1)}, f32[1360,512]{1,0:T(8,128)S(1)}, bf16[1024,512]{1,0:T(8,128)(2,1)S(1)}, f32[1024,512]{1,0:T(8,128)S(1)}) custom-call(s32[1,28]{1,0:T(1,128)S(1)} %copy-done.2, bf16[448,4096]{1,0:T(8,128)(2,1)} %bitcast.13, bf16[448,512]{1,0:T(8,128)(2,1)S(1)} %bitcast.10, f32[1024,512]{1,0:T(8,128)S(1)} %bitcast.9, ...), custom_call_target="tpu_custom_call" | custom-call | flops 2047868928 | bytes 10485760 | tf_op jit(solution)/shard_map/pallas_call | solution.py:392
  49.0 5.6 %collective-permute-done.98.refs_0_ = bf16[256,1024]{1,0:T(8,128)(2,1)S(1)} collective-permute-done((bf16[256,1024]{1,0:T(8,128)(2,1)}, bf16[256,1024]{1,0:T(8,128)(2,1)S(1)}, u32[]{:S(2)}, u32[]{:S(2)}) %collective-permute-start.98) | collective-permute-done | bytes 524320 | tf_op jit(solution)/shard_map/ppermute | solution.py:28
  54.6 10.5 %collective-permute-done.99.refs_1_ = bf16[256,1024]{1,0:T(8,128)(2,1)S(1)} collective-permute-done((bf16[256,1024]{1,0:T(8,128)(2,1)}, bf16[256,1024]{1,0:T(8,128)(2,1)S(1)}, u32[]{:S(2)}, u32[]{:S(2)}) %collective-permute-start.99) | collective-permute-done | bytes 524320 | tf_op jit(solution)/shard_map/ppermute | solution.py:28
  65.1 1.4 %shard_map.50 = (f32[224,256]{1,0:T(8,128)S(1)}, bf16[224,256]{1,0:T(8,128)(2,1)S(1)}, bf16[224,256]{1,0:T(8,128)(2,1)S(1)}, bf16[224,256]{1,0:T(8,128)(2,1)S(1)...) custom-call(s32[1,28]{1,0:T(1,128)S(1)} %copy-done.2, ...), custom_call_target="tpu_custom_call", output_to_operand_aliasing={{8}: (2, {})} | custom-call | flops 536870912 | bytes 5570560 | tf_op jit(solution)/shard_map/pallas_call | solution.py:419
  68.3 2.6 %collective-permute-start.108 = (bf16[224,256]{1,0:T(8,128)(2,1)S(1)}, bf16[224,256]{1,0:T(8,128)(2,1)S(1)}, u32[]{:S(2)}, u32[]{:S(2)}) collective-permute-start(bf16[224,256]{1,0:T(8,128)(2,1)S(1)} %get-tuple-element.400), channel_id=1, source_target_pairs={{0,3},{1,0},{2,1},{3,2},{4,7},{5,4},{6,5},{7,6},{8,11},{9,8},{10,9... | collective-permute-start | bytes 344072 | tf_op jit(solution)/shard_map/ppermute | solution.py:28
  70.9 1.5 %collective-permute-start.101 = (bf16[224,256]{1,0:T(8,128)(2,1)S(1)}, bf16[224,256]{1,0:T(8,128)(2,1)S(1)}, u32[]{:S(2)}, u32[]{:S(2)}) collective-permute-start(bf16[224,256]{1,0:T(8,128)(2,1)S(1)} %get-tuple-element.394), channel_id=1, source_target_pairs={{0,2},{1,3},{2,0},{3,1},{4,6},{5,7},{6,4},{7,5},{8,10},{9,11},{10,... | collective-permute-start | bytes 344072 | tf_op jit(solution)/shard_map/ppermute | solution.py:28
  72.4 2.0 %collective-permute-done.106 = bf16[224,256]{1,0:T(8,128)(2,1)S(1)} collective-permute-done((bf16[224,256]{1,0:T(8,128)(2,1)S(1)}, bf16[224,256]{1,0:T(8,128)(2,1)S(1)}, u32[]{:S(2)}, u32[]{:S(2)}) %collective-permute-start.106) | collective-permute-done | bytes 114720 | tf_op jit(solution)/shard_map/ppermute | solution.py:28
  75.3 4.1 %collective-permute-done.107 = bf16[224,256]{1,0:T(8,128)(2,1)S(1)} collective-permute-done((bf16[224,256]{1,0:T(8,128)(2,1)S(1)}, bf16[224,256]{1,0:T(8,128)(2,1)S(1)}, u32[]{:S(2)}, u32[]{:S(2)}) %collective-permute-start.107) | collective-permute-done | bytes 114720 | tf_op jit(solution)/shard_map/ppermute | solution.py:28
  79.4 3.0 %collective-permute-start.111 = (bf16[224,256]{1,0:T(8,128)(2,1)S(1)}, bf16[224,256]{1,0:T(8,128)(2,1)S(1)}, u32[]{:S(2)}, u32[]{:S(2)}) collective-permute-start(bf16[224,256]{1,0:T(8,128)(2,1)S(1)} %add_convert_fusion.refs_0_), channel_id=1, source_target_pairs={{0,3},{1,0},{2,1},{3,2},{4,7},{5,4},{6,5},{7,6},{8,11},{9,8},{10,9... | collective-permute-start | bytes 344072 | tf_op jit(solution)/shard_map/ppermute | solution.py:28
  82.4 5.5 %collective-permute-start.110 = (bf16[224,256]{1,0:T(8,128)(2,1)S(1)}, bf16[224,256]{1,0:T(8,128)(2,1)S(1)}, u32[]{:S(2)}, u32[]{:S(2)}) collective-permute-start(bf16[224,256]{1,0:T(8,128)(2,1)S(1)} %add_convert_fusion.refs_0_), channel_id=1, source_target_pairs={{0,2},{1,3},{2,0},{3,1},{4,6},{5,7},{6,4},{7,5},{8,10},{9,11},{10,... | collective-permute-start | bytes 344072 | tf_op jit(solution)/shard_map/ppermute | solution.py:28
  88.4 8.0 %collective-permute-start.105 = (bf16[224,256]{1,0:T(8,128)(2,1)S(1)}, bf16[224,256]{1,0:T(8,128)(2,1)S(1)}, u32[]{:S(2)}, u32[]{:S(2)}) collective-permute-start(bf16[224,256]{1,0:T(8,128)(2,1)S(1)} %add_convert_fusion.1.refs_0_), channel_id=1, source_target_pairs={{0,3},{1,0},{2,1},{3,2},{4,7},{5,4},{6,5},{7,6},{8,11},{9,8},{10,9... | collective-permute-start | bytes 344072 | tf_op jit(solution)/shard_map/ppermute | solution.py:28
  97.7 1.7 %collective-permute-start.103 = (bf16[224,256]{1,0:T(8,128)(2,1)S(1)}, bf16[224,256]{1,0:T(8,128)(2,1)S(1)}, u32[]{:S(2)}, u32[]{:S(2)}) collective-permute-start(bf16[224,256]{1,0:T(8,128)(2,1)S(1)} %add_convert_fusion.1.refs_0_), channel_id=1, source_target_pairs={{0,1},{1,2},{2,3},{3,0},{4,5},{5,6},{6,7},{7,4},{8,9},{9,10},{10,1... | collective-permute-start | bytes 344072 | tf_op jit(solution)/shard_map/ppermute | solution.py:28
  99.4 1.3 %shard_map.49.turned_ref = bf16[1024,896]{1,0:T(8,128)(2,1)S(1)} custom-call(s32[1,28]{1,0:T(1,128)S(1)} %copy-done.2, bf16[1360,1024]{1,0:T(8,128)(2,1)S(1)} %get-tuple-element.387.rows_ref, bf16[256,1024]{1,0:T(8,128)(2,1)S(1)} %collective-permute-done.98.refs_0_, bf16[256,1024]{1,0:T(8,128)(2,1)S(1)} %collective-permute-done.99.refs_1_), custom_call_target="tpu_custom_call" | custom-call | bytes 3670016 | tf_op jit(solution)/shard_map/pallas_call | solution.py:432
  100.8 4.6 %collective-permute-done.110.refs_2_ = bf16[224,256]{1,0:T(8,128)(2,1)S(1)} collective-permute-done((bf16[224,256]{1,0:T(8,128)(2,1)S(1)}, bf16[224,256]{1,0:T(8,128)(2,1)S(1)}, u32[]{:S(2)}, u32[]{:S(2)}) %collective-permute-start.110) | collective-permute-done | bytes 114720 | tf_op jit(solution)/shard_map/ppermute | solution.py:28
  106.8 2.9 %collective-permute-done.104.refs_2_ = bf16[224,256]{1,0:T(8,128)(2,1)S(1)} collective-permute-done((bf16[224,256]{1,0:T(8,128)(2,1)S(1)}, bf16[224,256]{1,0:T(8,128)(2,1)S(1)}, u32[]{:S(2)}, u32[]{:S(2)}) %collective-permute-start.104) | collective-permute-done | bytes 114720 | tf_op jit(solution)/shard_map/ppermute | solution.py:28
  111.2 1.5 %collective-permute-start.114 = (f32[8,128]{1,0:T(8,128)S(1)}, f32[8,128]{1,0:T(8,128)S(1)}, u32[]{:S(2)}, u32[]{:S(2)}) collective-permute-start(f32[8,128]{1,0:T(8,128)S(1)} %add.293), channel_id=1, source_target_pairs={{0,3},{1,0},{2,1},{3,2},{4,7},{5,4},{6,5},{7,6},{8,11},{9,8},{10,9... | collective-permute-start | bytes 12296 | tf_op jit(solution)/shard_map/ppermute | solution.py:28
  112.6 2.0 %collective-permute-start.113 = (f32[8,128]{1,0:T(8,128)S(1)}, f32[8,128]{1,0:T(8,128)S(1)}, u32[]{:S(2)}, u32[]{:S(2)}) collective-permute-start(f32[8,128]{1,0:T(8,128)S(1)} %add.293), channel_id=1, source_target_pairs={{0,2},{1,3},{2,0},{3,1},{4,6},{5,7},{6,4},{7,5},{8,10},{9,11},{10,... | collective-permute-start | bytes 12296 | tf_op jit(solution)/shard_map/ppermute | solution.py:28
  114.9 1.5 %collective-permute-start.117 = (f32[8,128]{1,0:T(8,128)S(1)}, f32[8,128]{1,0:T(8,128)S(1)}, u32[]{:S(2)}, u32[]{:S(2)}) collective-permute-start(f32[8,128]{1,0:T(8,128)S(1)} %add.293), channel_id=1, source_target_pairs={{0,6},{1,7},{2,4},{3,5},{4,2},{5,3},{6,0},{7,1},{8,14},{9,15},{10,... | collective-permute-start | bytes 12296 | tf_op jit(solution)/shard_map/ppermute | solution.py:41
  117.1 1.7 %collective-permute-start.116 = (f32[8,128]{1,0:T(8,128)S(1)}, f32[8,128]{1,0:T(8,128)S(1)}, u32[]{:S(2)}, u32[]{:S(2)}) collective-permute-start(f32[8,128]{1,0:T(8,128)S(1)} %add.293), channel_id=1, source_target_pairs={{0,5},{1,6},{2,7},{3,4},{4,1},{5,2},{6,3},{7,0},{8,13},{9,14},{10,... | collective-permute-start | bytes 12296 | tf_op jit(solution)/shard_map/ppermute | solution.py:41
  120.1 1.9 %collective-permute-done.116 = f32[8,128]{1,0:T(8,128)S(1)} collective-permute-done((f32[8,128]{1,0:T(8,128)S(1)}, f32[8,128]{1,0:T(8,128)S(1)}, u32[]{:S(2)}, u32[]{:S(2)}) %collective-permute-start.116) | collective-permute-done | bytes 4128 | tf_op jit(solution)/shard_map/ppermute | solution.py:41
  122.0 1.7 %shard_map.53 = f32[1024,512]{1,0:T(8,128)} custom-call(f32[8,128]{1,0:T(8,128)S(1)} %add_add_fusion.33.own_ref, f32[8,128]{1,0:T(8,128)S(1)} %add_add_fusion.32.other_ref, f32[1024,512]{1,0:T(8,128)S(1)} %get-tuple-element.402.halves_ref, f32[1024,256]{1,0:T(8,128)S(1)} %get-tuple-element.403.refs_0_, f32[1024,256]{1,0:T(8,128)S(1)} %get-tuple-element.404.refs_1_, ...), custom_call_target="tpu_custom_call" | custom-call | tf_op jit(solution)/shard_map/pallas_call | solution.py:474
  (75 shorter events, 18.5 us)
Async XLA Ops:
  0.0 41.6 %collective-permute-start.96 = (f32[1024,512]{1,0:T(8,128)}, f32[1024,512]{1,0:T(8,128)}, u32[]{:S(2)}, u32[]{:S(2)}) collective-permute-start(f32[1024,512]{1,0:T(8,128)} %bitcast.8), channel_id=1, source_target_pairs={{0,4},{4,0},{8,12},{12,8},{16,20},{20,16},{24,28},{28,24},{1,5},{5... | collective-permute-start | bytes 6291464 | tf_op jit(solution)/shard_map/ppermute | solution.py:22
  4.1 37.5 %collective-permute-start.97 = (bf16[256,1024]{1,0:T(8,128)(2,1)}, bf16[256,1024]{1,0:T(8,128)(2,1)S(1)}, u32[]{:S(2)}, u32[]{:S(2)}) collective-permute-start(bf16[256,1024]{1,0:T(8,128)(2,1)} %get-tuple-element.382), channel_id=1, source_target_pairs={{0,2},{1,3},{2,0},{3,1},{4,6},{5,7},{6,4},{7,5},{8,10},{9,11},{10,... | collective-permute-start | bytes 1572872 | tf_op jit(solution)/shard_map/ppermute | solution.py:28
  14.7 2.7 %collective-permute-start.74 = (bf16[16,1024]{1,0:T(8,128)(2,1)S(1)}, bf16[16,1024]{1,0:T(8,128)(2,1)S(1)}, u32[]{:S(2)}, u32[]{:S(2)}) collective-permute-start(bf16[16,1024]{1,0:T(8,128)(2,1)S(1)} %slice.233), channel_id=1, source_target_pairs={{3,2},{7,6},{11,10},{15,14},{19,18},{23,22},{27,26},{31,30}} | collective-permute-start | bytes 98312 | tf_op jit(solution)/shard_map/cond/branch_1_fun/ppermute | solution.py:312
  15.4 8.1 %collective-permute-start.73 = (bf16[16,1024]{1,0:T(8,128)(2,1)S(1)}, bf16[16,1024]{1,0:T(8,128)(2,1)S(1)}, u32[]{:S(2)}, u32[]{:S(2)}) collective-permute-start(bf16[16,1024]{1,0:T(8,128)(2,1)S(1)} %slice.232), channel_id=1, source_target_pairs={{3,0},{7,4},{11,8},{15,12},{19,16},{23,20},{27,24},{31,28}} | collective-permute-start | bytes 98312 | tf_op jit(solution)/shard_map/cond/branch_1_fun/ppermute | solution.py:312
  16.7 6.8 %collective-permute-start.72 = (bf16[16,1024]{1,0:T(8,128)(2,1)S(1)}, bf16[16,1024]{1,0:T(8,128)(2,1)S(1)}, u32[]{:S(2)}, u32[]{:S(2)}) collective-permute-start(bf16[16,1024]{1,0:T(8,128)(2,1)S(1)} %slice.231), channel_id=1, source_target_pairs={{3,1},{7,5},{11,9},{15,13},{19,17},{23,21},{27,25},{31,29}} | collective-permute-start | bytes 98312 | tf_op jit(solution)/shard_map/cond/branch_1_fun/ppermute | solution.py:312
  26.0 15.7 %copy-start.2 = (s32[1,28]{1,0:T(1,128)S(1)}, s32[1,28]{1,0:T(1,128)}, u32[]{:S(2)}) copy-start(s32[1,28]{1,0:T(1,128)} %lengths_ref.8) | copy-start | bytes 340
  27.0 6.6 %collective-permute-start.8 = (bf16[48,1024]{1,0:T(8,128)(2,1)S(1)}, bf16[48,1024]{1,0:T(8,128)(2,1)S(1)}, u32[]{:S(2)}, u32[]{:S(2)}) collective-permute-start(bf16[48,1024]{1,0:T(8,128)(2,1)S(1)} %slice.176), channel_id=1, source_target_pairs={{0,3},{4,7},{8,11},{12,15},{16,19},{20,23},{24,27},{28,31}} | collective-permute-start | bytes 294920 | tf_op jit(solution)/shard_map/cond/branch_3_fun/ppermute | solution.py:312
  30.6 4.8 %collective-permute-start.7 = (bf16[48,1024]{1,0:T(8,128)(2,1)S(1)}, bf16[48,1024]{1,0:T(8,128)(2,1)S(1)}, u32[]{:S(2)}, u32[]{:S(2)}) collective-permute-start(bf16[48,1024]{1,0:T(8,128)(2,1)S(1)} %slice.175), channel_id=1, source_target_pairs={{0,1},{4,5},{8,9},{12,13},{16,17},{20,21},{24,25},{28,29}} | collective-permute-start | bytes 294920 | tf_op jit(solution)/shard_map/cond/branch_3_fun/ppermute | solution.py:312
  32.3 5.1 %collective-permute-start.6 = (bf16[48,1024]{1,0:T(8,128)(2,1)S(1)}, bf16[48,1024]{1,0:T(8,128)(2,1)S(1)}, u32[]{:S(2)}, u32[]{:S(2)}) collective-permute-start(bf16[48,1024]{1,0:T(8,128)(2,1)S(1)} %slice.174), channel_id=1, source_target_pairs={{0,2},{4,6},{8,10},{12,14},{16,18},{20,22},{24,26},{28,30}} | collective-permute-start | bytes 294920 | tf_op jit(solution)/shard_map/cond/branch_3_fun/ppermute | solution.py:312
  37.7 16.9 %collective-permute-start.98 = (bf16[256,1024]{1,0:T(8,128)(2,1)}, bf16[256,1024]{1,0:T(8,128)(2,1)S(1)}, u32[]{:S(2)}, u32[]{:S(2)}) collective-permute-start(bf16[256,1024]{1,0:T(8,128)(2,1)} %get-tuple-element.388), channel_id=1, source_target_pairs={{0,1},{1,2},{2,3},{3,0},{4,5},{5,6},{6,7},{7,4},{8,9},{9,10},{10,1... | collective-permute-start | bytes 1572872 | tf_op jit(solution)/shard_map/ppermute | solution.py:28
  38.2 26.9 %collective-permute-start.99 = (bf16[256,1024]{1,0:T(8,128)(2,1)}, bf16[256,1024]{1,0:T(8,128)(2,1)S(1)}, u32[]{:S(2)}, u32[]{:S(2)}) collective-permute-start(bf16[256,1024]{1,0:T(8,128)(2,1)} %get-tuple-element.389), channel_id=1, source_target_pairs={{0,3},{1,0},{2,1},{3,2},{4,7},{5,4},{6,5},{7,6},{8,11},{9,8},{10,9... | collective-permute-start | bytes 1572872 | tf_op jit(solution)/shard_map/ppermute | solution.py:28
  66.5 7.9 %collective-permute-start.106 = (bf16[224,256]{1,0:T(8,128)(2,1)S(1)}, bf16[224,256]{1,0:T(8,128)(2,1)S(1)}, u32[]{:S(2)}, u32[]{:S(2)}) collective-permute-start(bf16[224,256]{1,0:T(8,128)(2,1)S(1)} %get-tuple-element.398), channel_id=1, source_target_pairs={{0,1},{1,2},{2,3},{3,0},{4,5},{5,6},{6,7},{7,4},{8,9},{9,10},{10,1... | collective-permute-start | bytes 344072 | tf_op jit(solution)/shard_map/ppermute | solution.py:28
  67.2 12.2 %collective-permute-start.107 = (bf16[224,256]{1,0:T(8,128)(2,1)S(1)}, bf16[224,256]{1,0:T(8,128)(2,1)S(1)}, u32[]{:S(2)}, u32[]{:S(2)}) collective-permute-start(bf16[224,256]{1,0:T(8,128)(2,1)S(1)} %get-tuple-element.399), channel_id=1, source_target_pairs={{0,2},{1,3},{2,0},{3,1},{4,6},{5,7},{6,4},{7,5},{8,10},{9,11},{10,... | collective-permute-start | bytes 344072 | tf_op jit(solution)/shard_map/ppermute | solution.py:28
  68.3 11.1 %collective-permute-start.108 = (bf16[224,256]{1,0:T(8,128)(2,1)S(1)}, bf16[224,256]{1,0:T(8,128)(2,1)S(1)}, u32[]{:S(2)}, u32[]{:S(2)}) collective-permute-start(bf16[224,256]{1,0:T(8,128)(2,1)S(1)} %get-tuple-element.400), channel_id=1, source_target_pairs={{0,3},{1,0},{2,1},{3,2},{4,7},{5,4},{6,5},{7,6},{8,11},{9,8},{10,9... | collective-permute-start | bytes 344072 | tf_op jit(solution)/shard_map/ppermute | solution.py:28
  70.9 17.0 %collective-permute-start.100 = (bf16[224,256]{1,0:T(8,128)(2,1)S(1)}, bf16[224,256]{1,0:T(8,128)(2,1)S(1)}, u32[]{:S(2)}, u32[]{:S(2)}) collective-permute-start(bf16[224,256]{1,0:T(8,128)(2,1)S(1)} %get-tuple-element.393), channel_id=1, source_target_pairs={{0,1},{1,2},{2,3},{3,0},{4,5},{5,6},{6,7},{7,4},{8,9},{9,10},{10,1... | collective-permute-start | bytes 344072 | tf_op jit(solution)/shard_map/ppermute | solution.py:28
  70.9 17.4 %collective-permute-start.101 = (bf16[224,256]{1,0:T(8,128)(2,1)S(1)}, bf16[224,256]{1,0:T(8,128)(2,1)S(1)}, u32[]{:S(2)}, u32[]{:S(2)}) collective-permute-start(bf16[224,256]{1,0:T(8,128)(2,1)S(1)} %get-tuple-element.394), channel_id=1, source_target_pairs={{0,2},{1,3},{2,0},{3,1},{4,6},{5,7},{6,4},{7,5},{8,10},{9,11},{10,... | collective-permute-start | bytes 344072 | tf_op jit(solution)/shard_map/ppermute | solution.py:28
  74.4 13.9 %collective-permute-start.102 = (bf16[224,256]{1,0:T(8,128)(2,1)S(1)}, bf16[224,256]{1,0:T(8,128)(2,1)S(1)}, u32[]{:S(2)}, u32[]{:S(2)}) collective-permute-start(bf16[224,256]{1,0:T(8,128)(2,1)S(1)} %get-tuple-element.395), channel_id=1, source_target_pairs={{0,3},{1,0},{2,1},{3,2},{4,7},{5,4},{6,5},{7,6},{8,11},{9,8},{10,9... | collective-permute-start | bytes 344072 | tf_op jit(solution)/shard_map/ppermute | solution.py:28
  79.4 18.3 %collective-permute-start.111 = (bf16[224,256]{1,0:T(8,128)(2,1)S(1)}, bf16[224,256]{1,0:T(8,128)(2,1)S(1)}, u32[]{:S(2)}, u32[]{:S(2)}) collective-permute-start(bf16[224,256]{1,0:T(8,128)(2,1)S(1)} %add_convert_fusion.refs_0_), channel_id=1, source_target_pairs={{0,3},{1,0},{2,1},{3,2},{4,7},{5,4},{6,5},{7,6},{8,11},{9,8},{10,9... | collective-permute-start | bytes 344072 | tf_op jit(solution)/shard_map/ppermute | solution.py:28
  82.4 23.0 %collective-permute-start.110 = (bf16[224,256]{1,0:T(8,128)(2,1)S(1)}, bf16[224,256]{1,0:T(8,128)(2,1)S(1)}, u32[]{:S(2)}, u32[]{:S(2)}) collective-permute-start(bf16[224,256]{1,0:T(8,128)(2,1)S(1)} %add_convert_fusion.refs_0_), channel_id=1, source_target_pairs={{0,2},{1,3},{2,0},{3,1},{4,6},{5,7},{6,4},{7,5},{8,10},{9,11},{10,... | collective-permute-start | bytes 344072 | tf_op jit(solution)/shard_map/ppermute | solution.py:28
  87.9 17.5 %collective-permute-start.109 = (bf16[224,256]{1,0:T(8,128)(2,1)S(1)}, bf16[224,256]{1,0:T(8,128)(2,1)S(1)}, u32[]{:S(2)}, u32[]{:S(2)}) collective-permute-start(bf16[224,256]{1,0:T(8,128)(2,1)S(1)} %add_convert_fusion.refs_0_), channel_id=1, source_target_pairs={{0,1},{1,2},{2,3},{3,0},{4,5},{5,6},{6,7},{7,4},{8,9},{9,10},{10,1... | collective-permute-start | bytes 344072 | tf_op jit(solution)/shard_map/ppermute | solution.py:28
  88.4 18.4 %collective-permute-start.105 = (bf16[224,256]{1,0:T(8,128)(2,1)S(1)}, bf16[224,256]{1,0:T(8,128)(2,1)S(1)}, u32[]{:S(2)}, u32[]{:S(2)}) collective-permute-start(bf16[224,256]{1,0:T(8,128)(2,1)S(1)} %add_convert_fusion.1.refs_0_), channel_id=1, source_target_pairs={{0,3},{1,0},{2,1},{3,2},{4,7},{5,4},{6,5},{7,6},{8,11},{9,8},{10,9... | collective-permute-start | bytes 344072 | tf_op jit(solution)/shard_map/ppermute | solution.py:28
  96.4 13.3 %collective-permute-start.104 = (bf16[224,256]{1,0:T(8,128)(2,1)S(1)}, bf16[224,256]{1,0:T(8,128)(2,1)S(1)}, u32[]{:S(2)}, u32[]{:S(2)}) collective-permute-start(bf16[224,256]{1,0:T(8,128)(2,1)S(1)} %add_convert_fusion.1.refs_0_), channel_id=1, source_target_pairs={{0,2},{1,3},{2,0},{3,1},{4,6},{5,7},{6,4},{7,5},{8,10},{9,11},{10,... | collective-permute-start | bytes 344072 | tf_op jit(solution)/shard_map/ppermute | solution.py:28
  97.7 12.0 %collective-permute-start.103 = (bf16[224,256]{1,0:T(8,128)(2,1)S(1)}, bf16[224,256]{1,0:T(8,128)(2,1)S(1)}, u32[]{:S(2)}, u32[]{:S(2)}) collective-permute-start(bf16[224,256]{1,0:T(8,128)(2,1)S(1)} %add_convert_fusion.1.refs_0_), channel_id=1, source_target_pairs={{0,1},{1,2},{2,3},{3,0},{4,5},{5,6},{6,7},{7,4},{8,9},{9,10},{10,1... | collective-permute-start | bytes 344072 | tf_op jit(solution)/shard_map/ppermute | solution.py:28
  106.7 15.3 %collective-permute-start.120 = (bf16[1024,256]{1,0:T(8,128)(2,1)S(1)}, bf16[1024,256]{1,0:T(8,128)(2,1)S(1)}, u32[]{:S(2)}, u32[]{:S(2)}) collective-permute-start(bf16[1024,256]{1,0:T(8,128)(2,1)S(1)} %get-tuple-element.406), channel_id=1, source_target_pairs={{0,4},{4,0},{8,12},{12,8},{16,20},{20,16},{24,28},{28,24},{1,5},{5... | collective-permute-start | bytes 1572872 | tf_op jit(solution)/shard_map/ppermute | solution.py:22
  111.0 11.0 %collective-permute-start.119 = (bf16[1024,256]{1,0:T(8,128)(2,1)S(1)}, bf16[1024,256]{1,0:T(8,128)(2,1)S(1)}, u32[]{:S(2)}, u32[]{:S(2)}) collective-permute-start(bf16[1024,256]{1,0:T(8,128)(2,1)S(1)} %get-tuple-element.405), channel_id=1, source_target_pairs={{0,4},{4,0},{8,12},{12,8},{16,20},{20,16},{24,28},{28,24},{1,5},{5... | collective-permute-start | bytes 1572872 | tf_op jit(solution)/shard_map/ppermute | solution.py:22
  111.1 3.6 %collective-permute-start.118 = (f32[8,128]{1,0:T(8,128)S(1)}, f32[8,128]{1,0:T(8,128)S(1)}, u32[]{:S(2)}, u32[]{:S(2)}) collective-permute-start(f32[8,128]{1,0:T(8,128)S(1)} %add.293), channel_id=1, source_target_pairs={{0,7},{1,4},{2,5},{3,6},{4,3},{5,0},{6,1},{7,2},{8,15},{9,12},{10,... | collective-permute-start | bytes 12296 | tf_op jit(solution)/shard_map/ppermute | solution.py:41
  111.2 3.7 %collective-permute-start.114 = (f32[8,128]{1,0:T(8,128)S(1)}, f32[8,128]{1,0:T(8,128)S(1)}, u32[]{:S(2)}, u32[]{:S(2)}) collective-permute-start(f32[8,128]{1,0:T(8,128)S(1)} %add.293), channel_id=1, source_target_pairs={{0,3},{1,0},{2,1},{3,2},{4,7},{5,4},{6,5},{7,6},{8,11},{9,8},{10,9... | collective-permute-start | bytes 12296 | tf_op jit(solution)/shard_map/ppermute | solution.py:28
  112.6 4.5 %collective-permute-start.113 = (f32[8,128]{1,0:T(8,128)S(1)}, f32[8,128]{1,0:T(8,128)S(1)}, u32[]{:S(2)}, u32[]{:S(2)}) collective-permute-start(f32[8,128]{1,0:T(8,128)S(1)} %add.293), channel_id=1, source_target_pairs={{0,2},{1,3},{2,0},{3,1},{4,6},{5,7},{6,4},{7,5},{8,10},{9,11},{10,... | collective-permute-start | bytes 12296 | tf_op jit(solution)/shard_map/ppermute | solution.py:28
  114.7 5.4 %collective-permute-start.112 = (f32[8,128]{1,0:T(8,128)S(1)}, f32[8,128]{1,0:T(8,128)S(1)}, u32[]{:S(2)}, u32[]{:S(2)}) collective-permute-start(f32[8,128]{1,0:T(8,128)S(1)} %add.293), channel_id=1, source_target_pairs={{0,1},{1,2},{2,3},{3,0},{4,5},{5,6},{6,7},{7,4},{8,9},{9,10},{10,1... | collective-permute-start | bytes 12296 | tf_op jit(solution)/shard_map/ppermute | solution.py:28
  114.9 5.3 %collective-permute-start.117 = (f32[8,128]{1,0:T(8,128)S(1)}, f32[8,128]{1,0:T(8,128)S(1)}, u32[]{:S(2)}, u32[]{:S(2)}) collective-permute-start(f32[8,128]{1,0:T(8,128)S(1)} %add.293), channel_id=1, source_target_pairs={{0,6},{1,7},{2,4},{3,5},{4,2},{5,3},{6,0},{7,1},{8,14},{9,15},{10,... | collective-permute-start | bytes 12296 | tf_op jit(solution)/shard_map/ppermute | solution.py:41
  117.1 4.8 %collective-permute-start.116 = (f32[8,128]{1,0:T(8,128)S(1)}, f32[8,128]{1,0:T(8,128)S(1)}, u32[]{:S(2)}, u32[]{:S(2)}) collective-permute-start(f32[8,128]{1,0:T(8,128)S(1)} %add.293), channel_id=1, source_target_pairs={{0,5},{1,6},{2,7},{3,4},{4,1},{5,2},{6,3},{7,0},{8,13},{9,14},{10,... | collective-permute-start | bytes 12296 | tf_op jit(solution)/shard_map/ppermute | solution.py:41
  120.1 1.9 %collective-permute-start.115 = (f32[8,128]{1,0:T(8,128)S(1)}, f32[8,128]{1,0:T(8,128)S(1)}, u32[]{:S(2)}, u32[]{:S(2)}) collective-permute-start(f32[8,128]{1,0:T(8,128)S(1)} %add.293), channel_id=1, source_target_pairs={{0,4},{1,5},{2,6},{3,7},{4,0},{5,1},{6,2},{7,3},{8,12},{9,13},{10,... | collective-permute-start | bytes 12296 | tf_op jit(solution)/shard_map/ppermute | solution.py:41
  (7 other events, 53.2 us)

commit v4 on v1

--- a/solution.py
+++ b/solution.py
@@ -66,6 +66,11 @@
 def picking(places, start, rows):
     row = lax.broadcasted_iota(jnp.int32, (rows, places.shape[1]), 0) + start
     return jnp.where(row == places, 1.0, 0.0).astype(jnp.bfloat16)
+
+
+def other_half(index):
+    half = index // 2
+    return [2 - half, 3 - 3 * half]
 
 
 class Block:
@@ -100,6 +105,10 @@
             choice = choice + jnp.where(used > first + size, 1, 0)
         choices.append(choice)
     return choices
+
+
+def choice_bits(sizes):
+    return (len(sizes) - 1).bit_length()
 
 
 def sent_kernel(members, offsets, sizes, lengths_ref, features_ref, *refs):
@@ -144,8 +153,10 @@
             copy.start()
             copy.wait()
 
+    packed = jnp.int32(0)
     for member, choice in enumerate(used_places(totals, first, sizes)):
-        choice_ref[member] = choice
+        packed = packed | (choice << (member * choice_bits(sizes)))
+    choice_ref[0] = packed
     for copy in copies:
         copy.wait()
 
@@ -247,12 +258,31 @@
 
 
 def gradient_kernel(members, turned_ref, *refs):
-    residuals, (gradient_ref, low_ref, squares_ref, all_ref) = refs[:members], refs[members:]
+    residuals, (gradient_ref, low_ref, squares_ref, all_ref) = refs[:-4], refs[-4:]
     index = lax.axis_index("fsdp")
     share = residuals[0].shape[0]
-    for i in range(members):
-        owner = lax.rem(index + members - i, members)
-        all_ref[pl.ds(pl.multiple_of(owner * share, ALIGN), share)] = residuals[i][...]
+
+    def put(owner, block):
+        all_ref[pl.ds(pl.multiple_of(owner * share, ALIGN), share)] = block
+
+    if len(residuals) > members:
+        own_ref, left_ref, right_ref, two_ref, pair_ref = residuals
+        inner, outer = other_half(index)
+        put(index, own_ref[...])
+        pl.when(index > 0)(lambda: put(index - 1, left_ref[...]))
+        pl.when(index < 3)(lambda: put(index + 1, right_ref[...]))
+
+        @pl.when((index == 1) | (index == 2))
+        def _():
+            put(outer, two_ref[...])
+
+        @pl.when((index == 0) | (index == 3))
+        def _():
+            put(inner, pair_ref[:share])
+            put(outer, pair_ref[share:])
+    else:
+        for i in range(members):
+            put(lax.rem(index + members - i, members), residuals[i][...])
     squares_ref[...] = jnp.zeros_like(squares_ref)
     height = min(256, turned_ref.shape[0])
 
@@ -302,6 +332,22 @@
     return jnp.pad(sum(moved[1:], moved[0]), ((0, blocks[0].shape[0] - size), (0, 0)))
 
 
+def sent_along(value, *pairs):
+    return lax.ppermute(value, "fsdp", pairs)
+
+
+def all_residuals(residual, last):
+    members = lax.axis_size("fsdp")
+    if members == 4 and not last:
+        left = sent_along(residual, (0, 1), (1, 2), (2, 3))
+        right = sent_along(residual, (1, 0), (2, 1), (3, 2))
+        two = sent_along(residual, (0, 2), (3, 1))
+        inner = jnp.where(lax.axis_index("fsdp") < 2, right, left)
+        pair = sent_along(jnp.concatenate([inner, two]), (1, 0), (2, 3))
+        return [residual, left, right, two, pair]
+    return [residual] + [turned(residual, i) for i in range(1, members)]
+
+
 def local(activations, targets, weights, lengths):
     features = activations[0]
     wanted = targets[0]
@@ -341,7 +387,7 @@
             out_shape=[
                 array(rows, local_rows, jnp.bfloat16) for rows in (first, more) for _ in offsets
             ]
-            + [jax.ShapeDtypeStruct((members,), jnp.int32)],
+            + [jax.ShapeDtypeStruct((1,), jnp.int32)],
             scratch_shapes=[
                 pltpu.VMEM((count, tokens_here, local_rows), jnp.bfloat16),
                 pltpu.VMEM((count, first, local_rows), jnp.bfloat16),
@@ -364,9 +410,10 @@
     near_first, near_more, _ = sent_to(near)
     held_far = turned(far_first[0], far)
     offsets = [far] + near
+    bits = choice_bits(sizes)
     held_more = [
         lax.switch(
-            choice[source],
+            lax.shift_right_logical(choice[0], jnp.int32(source * bits)) & (2**bits - 1),
             [functools.partial(more_rows, size, source, offsets) for size in sizes],
             far_more + near_more,
         )
@@ -432,10 +479,10 @@
         for i in range(1, members):
             residual = residual + turned(sums[half][i], i).astype(jnp.float32)
         residual = residual.astype(jnp.bfloat16)
-        residuals = [residual] + [turned(residual, i) for i in range(1, members)]
+        residuals = all_residuals(residual, half == HALVES - 1)
         gradient, low_gradient, own_squares = pl.pallas_call(
             functools.partial(gradient_kernel, members),
-            in_specs=[vmem] + [vmem] * members,
+            in_specs=[vmem] * (1 + len(residuals)),
             out_specs=[vmem] * 3,
             out_shape=[
                 array(local_rows, width, jnp.float32),

time: 117 us -> 126 us (1.077); the launches traced: 118 us -> 124 us
  local copies, waits for them, and re-layouts: 4.01 us -> 13.3 us
  waiting for transfers between devices: 44.8 us -> 37.5 us
  starting transfers between devices: 41.1 us -> 43.8 us
  other arithmetic: 0.14 us -> 2.01 us
    ppermute x6, waiting for transfers between devices: 25 us -> 10.2 us  [more_rows(): lax.ppermute(block[:size], 'fsdp', [(source, (source + i) % members)])]
    ppermute x0 -> x4, starting transfers between devices: none -> 9.62 us  [sent_along(): return lax.ppermute(value, 'fsdp', pairs)]
    ppermute x18 -> x15, starting transfers between devices: 33 us -> 24.2 us  [turned(): return lax.ppermute(value, 'fsdp', ring)]
    unnamed x16 -> x32, local copies, waits for them, and re-layouts: 2.43 us -> 9.2 us
    ppermute x18 -> x15, waiting for transfers between devices: 19 us -> 22.9 us  [turned(): return lax.ppermute(value, 'fsdp', ring)]
    ppermute x0 -> x4, waiting for transfers between devices: none -> 3.49 us  [sent_along(): return lax.ppermute(value, 'fsdp', pairs)]
    ppermute x4, starting transfers between devices: 2.88 us -> 4.76 us  [swapped(): return lax.ppermute(value, axis, pairs)]
    slice x6, local copies, waits for them, and re-layouts: 0.03 us -> 1.63 us  [more_rows(): block[:size]]
  transfers between devices with their start and end apart: 28 -> 29, of which waited for: 11 -> 12; matrix products, arithmetic and copies ran while one was open for 1% -> 5% of each run, Pallas kernels for 18% -> 17%
where the time goes in v4:
time: 126 us; the launch traced here: 124 us
  starting transfers between devices  43.8 us (35%)
  waiting for transfers between devices  37.5 us (30%)
  Pallas kernels  24.6 us (20%)
  local copies, waits for them, and re-layouts  13.3 us (11%)
  between operations  2.97 us (2%)
  other arithmetic  2.01 us (2%)
    ppermute x15, starting transfers between devices, turned(): return lax.ppermute(value, 'fsdp', ring)  24.2 us
    ppermute x15, waiting for transfers between devices, turned(): return lax.ppermute(value, 'fsdp', ring)  22.9 us
    ppermute x6, waiting for transfers between devices, more_rows(): lax.ppermute(block[:size], 'fsdp', [(source, (source + i) % members)])  10.2 us
    ppermute x4, starting transfers between devices, sent_along(): return lax.ppermute(value, 'fsdp', pairs)  9.62 us
    pallas_call x2, Pallas kernels, sent_to(): pl.pallas_call(functools.partial(sent_kernel, members, offsets, sizes), i...  9.27 us
    unnamed x32, local copies, waits for them, and re-layouts  9.2 us
    pallas_call x1, Pallas kernels, local(): pl.pallas_call(functools.partial(own_kernel, members, far, scale), in_spe...  7.38 us
    ppermute x6, starting transfers between devices, more_rows(): lax.ppermute(block[:size], 'fsdp', [(source, (source + i) % members)])  5.2 us
  transfers between devices with their start and end apart: 29, of which 12 were waited for; matrix products, arithmetic and copies ran while one was open for 5% of the time, Pallas kernels for 17%

profile of v4, /device:TPU:7, one launch (start us, length us, event | category | flops | bytes accessed | tf_op | source)
XLA Modules:
  0.0 124.2 jit_solution(17121672160428664072)
XLA Ops:
  0.7 4.0 %shard_map.47 = (bf16[256,1024]{1,0:T(8,128)(2,1)}, bf16[208,1024]{1,0:T(8,128)(2,1)S(1)}, s32[1]{0:T(128)}) custom-call(s32[1,28]{1,0:T(1,128)} %lengths_ref.8, bf16[448,4096]{1,0:T(8,128)(2,1)} %bitcast.11), custom_call_target="tpu_custom_call" | custom-call | flops 234881024 | bytes 1441792 | tf_op jit(solution)/shard_map/pallas_call | solution.py:383
  4.7 2.4 %collective-permute-start.97 = (bf16[256,1024]{1,0:T(8,128)(2,1)}, bf16[256,1024]{1,0:T(8,128)(2,1)S(1)}, u32[]{:S(2)}, u32[]{:S(2)}) collective-permute-start(bf16[256,1024]{1,0:T(8,128)(2,1)} %get-tuple-element.376), channel_id=1, source_target_pairs={{0,2},{1,3},{2,0},{3,1},{4,6},{5,7},{6,4},{7,5},{8,10},{9,11},{10,... | collective-permute-start | bytes 1572872 | tf_op jit(solution)/shard_map/ppermute | solution.py:28
  9.0 5.3 %shard_map.46 = (bf16[256,1024]{1,0:T(8,128)(2,1)}, bf16[256,1024]{1,0:T(8,128)(2,1)}, bf16[208,1024]{1,0:T(8,128)(2,1)S(1)}, bf16[208,1024]{1,0:T(8,128)(2,1)}, s32[1]{0:T(128)}) custom-call(s32[1,28]{1,0:T(1,128)} %lengths_ref.8, bf16[448,4096]{1,0:T(8,128)(2,1)} %bitcast.12), custom_call_target="tpu_custom_call" | custom-call | flops 469762048 | bytes 2883584 | tf_op jit(solution)/shard_map/pallas_call | solution.py:383
  14.3 8.9 %conditional.7 = (bf16[208,1024]{1,0:T(8,128)(2,1)}) conditional(s32[]{:T(128)} %bitcast.4, bf16[208,1024]{1,0:T(8,128)(2,1)S(1)} %get-tuple-element.372, (bf16[208,1024]{1,0:T(8,128)(2,1)S(1)}, bf16[208,1024]{1,0:T(8,128)(2,1)S(1)}, bf16[208,1024]{1,0:T(8,128)(2,1)}) %tuple.114, (bf16[208,1024]{1,0:T(8,128)(2,1)S(1)}, ...), branch_computations={%region_27.28_spmd, %region_28.29_spmd, %region_29.30_spmd, %regio... | conditional | flops 425984 | bytes 6815872 | solution.py:415
  15.0 1.3 %collective-permute-start.73 = (bf16[16,1024]{1,0:T(8,128)(2,1)S(1)}, bf16[16,1024]{1,0:T(8,128)(2,1)S(1)}, u32[]{:S(2)}, u32[]{:S(2)}) collective-permute-start(bf16[16,1024]{1,0:T(8,128)(2,1)S(1)} %slice.232), channel_id=1, source_target_pairs={{3,0},{7,4},{11,8},{15,12},{19,16},{23,20},{27,24},{31,28}} | collective-permute-start | bytes 98312 | tf_op jit(solution)/shard_map/cond/branch_1_fun/ppermute | solution.py:329
  17.7 4.6 %collective-permute-done.73 = bf16[16,1024]{1,0:T(8,128)(2,1)S(1)} collective-permute-done((bf16[16,1024]{1,0:T(8,128)(2,1)S(1)}, bf16[16,1024]{1,0:T(8,128)(2,1)S(1)}, u32[]{:S(2)}, u32[]{:S(2)}) %collective-permute-start.73) | collective-permute-done | bytes 32800 | tf_op jit(solution)/shard_map/cond/branch_1_fun/ppermute | solution.py:329
  23.1 10.0 %conditional.6 = (bf16[208,1024]{1,0:T(8,128)(2,1)}) conditional(s32[]{:T(128)} %bitcast.3, bf16[208,1024]{1,0:T(8,128)(2,1)S(1)} %get-tuple-element.372, (bf16[208,1024]{1,0:T(8,128)(2,1)S(1)}, bf16[208,1024]{1,0:T(8,128)(2,1)S(1)}, bf16[208,1024]{1,0:T(8,128)(2,1)}) %tuple.114, (bf16[208,1024]{1,0:T(8,128)(2,1)S(1)}, ...), branch_computations={%region_18.19_spmd, %region_19.20_spmd, %region_20.21_spmd, %regio... | conditional | flops 425984 | bytes 6815872 | solution.py:415
  26.6 5.7 %collective-permute-done.51 = bf16[32,1024]{1,0:T(8,128)(2,1)S(1)} collective-permute-done((bf16[32,1024]{1,0:T(8,128)(2,1)S(1)}, bf16[32,1024]{1,0:T(8,128)(2,1)S(1)}, u32[]{:S(2)}, u32[]{:S(2)}) %collective-permute-start.51) | collective-permute-done | bytes 65568 | tf_op jit(solution)/shard_map/cond/branch_2_fun/ppermute | solution.py:329
  36.3 2.4 %collective-permute-start.99 = (bf16[256,1024]{1,0:T(8,128)(2,1)}, bf16[256,1024]{1,0:T(8,128)(2,1)S(1)}, u32[]{:S(2)}, u32[]{:S(2)}) collective-permute-start(bf16[256,1024]{1,0:T(8,128)(2,1)} %get-tuple-element.383), channel_id=1, source_target_pairs={{0,3},{1,0},{2,1},{3,2},{4,7},{5,4},{6,5},{7,6},{8,11},{9,8},{10,9... | collective-permute-start | bytes 1572872 | tf_op jit(solution)/shard_map/ppermute | solution.py:28
  39.4 1.3 %copy-done.3 = f32[1024,512]{1,0:T(8,128)} copy-done((f32[1024,512]{1,0:T(8,128)}, f32[1024,512]{1,0:T(8,128)S(1)}, u32[]{:S(2)}) %copy-start.3) | copy-done | bytes 2097176
  40.8 1.6 %copy-done.2 = f32[1,1024,512]{2,1,0:T(8,128)S(1)} copy-done((f32[1,1024,512]{2,1,0:T(8,128)S(1)}, f32[1,1024,512]{2,1,0:T(8,128)}, u32[]{:S(2)}) %copy-start.2) | copy-done | bytes 2097176
  42.3 1.6 %copy-done.4 = f32[1024,512]{1,0:T(8,128)S(1)} copy-done((f32[1024,512]{1,0:T(8,128)S(1)}, f32[1024,512]{1,0:T(8,128)}, u32[]{:S(2)}) %copy-start.4) | copy-done | bytes 2097176
  46.0 7.4 %shard_map.48 = (bf16[1360,1024]{1,0:T(8,128)(2,1)S(1)}, f32[1360,512]{1,0:T(8,128)S(1)}, bf16[1024,512]{1,0:T(8,128)(2,1)S(1)}, f32[1024,512]{1,0:T(8,128)S(1)}) custom-call(s32[1,28]{1,0:T(1,128)S(1)} %copy-done.11, bf16[448,4096]{1,0:T(8,128)(2,1)} %bitcast.13, bf16[448,512]{1,0:T(8,128)(2,1)S(1)} %bitcast.10, f32[1024,512]{1,0:T(8,128)S(1)} %bitcast.9, ...), custom_call_target="tpu_custom_call" | custom-call | flops 2047868928 | bytes 10485760 | tf_op jit(solution)/shard_map/pallas_call | solution.py:426
  53.4 8.0 %collective-permute-done.99.refs_1_ = bf16[256,1024]{1,0:T(8,128)(2,1)S(1)} collective-permute-done((bf16[256,1024]{1,0:T(8,128)(2,1)}, bf16[256,1024]{1,0:T(8,128)(2,1)S(1)}, u32[]{:S(2)}, u32[]{:S(2)}) %collective-permute-start.99) | collective-permute-done | bytes 524320 | tf_op jit(solution)/shard_map/ppermute | solution.py:28
  61.4 1.4 %shard_map.50 = (f32[224,256]{1,0:T(8,128)S(1)}, bf16[224,256]{1,0:T(8,128)(2,1)S(1)}, bf16[224,256]{1,0:T(8,128)(2,1)S(1)}, bf16[224,256]{1,0:T(8,128)(2,1)S(1)...) custom-call(s32[1,28]{1,0:T(1,128)S(1)} %copy-done.11, ...), custom_call_target="tpu_custom_call", output_to_operand_aliasing={{8}: (2, {})} | custom-call | flops 536870912 | bytes 5570560 | tf_op jit(solution)/shard_map/pallas_call | solution.py:453
  62.8 1.5 %collective-permute-start.100 = (bf16[224,256]{1,0:T(8,128)(2,1)S(1)}, bf16[224,256]{1,0:T(8,128)(2,1)S(1)}, u32[]{:S(2)}, u32[]{:S(2)}) collective-permute-start(bf16[224,256]{1,0:T(8,128)(2,1)S(1)} %get-tuple-element.387), channel_id=1, source_target_pairs={{0,1},{1,2},{2,3},{3,0},{4,5},{5,6},{6,7},{7,4},{8,9},{9,10},{10,1... | collective-permute-start | bytes 344072 | tf_op jit(solution)/shard_map/ppermute | solution.py:28
  64.4 2.0 %collective-permute-start.102 = (bf16[224,256]{1,0:T(8,128)(2,1)S(1)}, bf16[224,256]{1,0:T(8,128)(2,1)S(1)}, u32[]{:S(2)}, u32[]{:S(2)}) collective-permute-start(bf16[224,256]{1,0:T(8,128)(2,1)S(1)} %get-tuple-element.389), channel_id=1, source_target_pairs={{0,3},{1,0},{2,1},{3,2},{4,7},{5,4},{6,5},{7,6},{8,11},{9,8},{10,9... | collective-permute-start | bytes 344072 | tf_op jit(solution)/shard_map/ppermute | solution.py:28
  66.4 2.5 %collective-permute-done.100 = bf16[224,256]{1,0:T(8,128)(2,1)S(1)} collective-permute-done((bf16[224,256]{1,0:T(8,128)(2,1)S(1)}, bf16[224,256]{1,0:T(8,128)(2,1)S(1)}, u32[]{:S(2)}, u32[]{:S(2)}) %collective-permute-start.100) | collective-permute-done | bytes 114720 | tf_op jit(solution)/shard_map/ppermute | solution.py:28
  69.0 5.7 %collective-permute-done.101 = bf16[224,256]{1,0:T(8,128)(2,1)S(1)} collective-permute-done((bf16[224,256]{1,0:T(8,128)(2,1)S(1)}, bf16[224,256]{1,0:T(8,128)(2,1)S(1)}, u32[]{:S(2)}, u32[]{:S(2)}) %collective-permute-start.101) | collective-permute-done | bytes 114720 | tf_op jit(solution)/shard_map/ppermute | solution.py:28
  74.7 4.6 %collective-permute-start.103 = (bf16[224,256]{1,0:T(8,128)(2,1)S(1)}, bf16[224,256]{1,0:T(8,128)(2,1)S(1)}, u32[]{:S(2)}, u32[]{:S(2)}) collective-permute-start(bf16[224,256]{1,0:T(8,128)(2,1)S(1)} %add_convert_fusion.1.refs_0_), channel_id=1, source_target_pairs={{0,1},{1,2},{2,3},{4,5},{5,6},{6,7},{8,9},{9,10},{10,11},{12,13},{... | collective-permute-start | bytes 344072 | tf_op jit(solution)/shard_map/ppermute | solution.py:336
  80.7 2.1 %collective-permute-start.107 = (bf16[224,256]{1,0:T(8,128)(2,1)}, bf16[224,256]{1,0:T(8,128)(2,1)S(1)}, u32[]{:S(2)}, u32[]{:S(2)}) collective-permute-start(bf16[224,256]{1,0:T(8,128)(2,1)} %copy-done.14), channel_id=1, source_target_pairs={{0,1},{1,2},{2,3},{3,0},{4,5},{5,6},{6,7},{7,4},{8,9},{9,10},{10,1... | collective-permute-start | bytes 344072 | tf_op jit(solution)/shard_map/ppermute | solution.py:28
  83.3 1.7 %collective-permute-start.109 = (bf16[224,256]{1,0:T(8,128)(2,1)}, bf16[224,256]{1,0:T(8,128)(2,1)S(1)}, u32[]{:S(2)}, u32[]{:S(2)}) collective-permute-start(bf16[224,256]{1,0:T(8,128)(2,1)} %copy-done.12), channel_id=1, source_target_pairs={{0,3},{1,0},{2,1},{3,2},{4,7},{5,4},{6,5},{7,6},{8,11},{9,8},{10,9... | collective-permute-start | bytes 344072 | tf_op jit(solution)/shard_map/ppermute | solution.py:28
  85.0 2.4 %collective-permute-start.105 = (bf16[224,256]{1,0:T(8,128)(2,1)S(1)}, bf16[224,256]{1,0:T(8,128)(2,1)S(1)}, u32[]{:S(2)}, u32[]{:S(2)}) collective-permute-start(bf16[224,256]{1,0:T(8,128)(2,1)S(1)} %add_convert_fusion.1.refs_0_), channel_id=1, source_target_pairs={{0,2},{3,1},{4,6},{7,5},{8,10},{11,9},{12,14},{15,13},{16,18},{19,... | collective-permute-start | bytes 344072 | tf_op jit(solution)/shard_map/ppermute | solution.py:336
  88.3 3.5 %collective-permute-done.105.refs_3_ = bf16[224,256]{1,0:T(8,128)(2,1)S(1)} collective-permute-done((bf16[224,256]{1,0:T(8,128)(2,1)S(1)}, bf16[224,256]{1,0:T(8,128)(2,1)S(1)}, u32[]{:S(2)}, u32[]{:S(2)}) %collective-permute-start.105) | collective-permute-done | bytes 114720 | tf_op jit(solution)/shard_map/ppermute | solution.py:336
  94.3 5.1 %collective-permute-start.110 = (bf16[224,256]{1,0:T(8,128)(2,1)S(1)}, bf16[224,256]{1,0:T(8,128)(2,1)S(1)}, u32[]{:S(2)}, u32[]{:S(2)}) collective-permute-start(bf16[224,256]{1,0:T(8,128)(2,1)S(1)} %add_convert_fusion.refs_0_), channel_id=1, source_target_pairs={{0,1},{1,2},{2,3},{3,0},{4,5},{5,6},{6,7},{7,4},{8,9},{9,10},{10,1... | collective-permute-start | bytes 344072 | tf_op jit(solution)/shard_map/ppermute | solution.py:28
  99.3 2.2 %collective-permute-start.112 = (bf16[224,256]{1,0:T(8,128)(2,1)S(1)}, bf16[224,256]{1,0:T(8,128)(2,1)S(1)}, u32[]{:S(2)}, u32[]{:S(2)}) collective-permute-start(bf16[224,256]{1,0:T(8,128)(2,1)S(1)} %add_convert_fusion.refs_0_), channel_id=1, source_target_pairs={{0,3},{1,0},{2,1},{3,2},{4,7},{5,4},{6,5},{7,6},{8,11},{9,8},{10,9... | collective-permute-start | bytes 344072 | tf_op jit(solution)/shard_map/ppermute | solution.py:28
  102.5 1.4 %shard_map.49.turned_ref = bf16[1024,896]{1,0:T(8,128)(2,1)S(1)} custom-call(s32[1,28]{1,0:T(1,128)S(1)} %copy-done.11, bf16[1360,1024]{1,0:T(8,128)(2,1)S(1)} %get-tuple-element.381.rows_ref, bf16[256,1024]{1,0:T(8,128)(2,1)S(1)} %collective-permute-done.98.refs_0_, bf16[256,1024]{1,0:T(8,128)(2,1)S(1)} %copy-done.1), custom_call_target="tpu_custom_call" | custom-call | bytes 3670016 | tf_op jit(solution)/shard_map/pallas_call | solution.py:466
  103.9 4.9 %collective-permute-done.111.refs_2_ = bf16[224,256]{1,0:T(8,128)(2,1)S(1)} collective-permute-done((bf16[224,256]{1,0:T(8,128)(2,1)S(1)}, bf16[224,256]{1,0:T(8,128)(2,1)S(1)}, u32[]{:S(2)}, u32[]{:S(2)}) %collective-permute-start.111) | collective-permute-done | bytes 114720 | tf_op jit(solution)/shard_map/ppermute | solution.py:28
  110.1 2.1 %collective-permute-start.118 = (bf16[1024,256]{1,0:T(8,128)(2,1)S(1)}, bf16[1024,256]{1,0:T(8,128)(2,1)S(1)}, u32[]{:S(2)}, u32[]{:S(2)}) collective-permute-start(bf16[1024,256]{1,0:T(8,128)(2,1)S(1)} %get-tuple-element.400), channel_id=1, source_target_pairs={{0,4},{4,0},{8,12},{12,8},{16,20},{20,16},{24,28},{28,24},{1,5},{5... | collective-permute-start | bytes 1572872 | tf_op jit(solution)/shard_map/ppermute | solution.py:22
  112.2 2.2 %shard_map.51 = (f32[1024,256]{1,0:T(8,128)S(1)}, bf16[1024,256]{1,0:T(8,128)(2,1)S(1)}, f32[8,128]{1,0:T(8,128)S(1)}) custom-call(bf16[1024,896]{1,0:T(8,128)(2,1)S(1)} %shard_map.49.turned_ref, bf16[224,256]{1,0:T(8,128)(2,1)S(1)} %add_convert_fusion.1.refs_0_, bf16[224,256]{1,0:T(8,128)(2,1)S(1)} %collective-permute-done.103.refs_1_, ...), custom_call_target="tpu_custom_call" | custom-call | flops 469762048 | bytes 2097152 | tf_op jit(solution)/shard_map/pallas_call | solution.py:483
  119.6 1.9 %collective-permute-start.116 = (f32[8,128]{1,0:T(8,128)S(1)}, f32[8,128]{1,0:T(8,128)S(1)}, u32[]{:S(2)}, u32[]{:S(2)}) collective-permute-start(f32[8,128]{1,0:T(8,128)S(1)} %add_add_fusion.32.own_ref), channel_id=1, source_target_pairs={{0,4},{4,0},{8,12},{12,8},{16,20},{20,16},{24,28},{28,24},{1,5},{5... | collective-permute-start | bytes 12296 | tf_op jit(solution)/shard_map/ppermute | solution.py:22
  122.3 1.7 %shard_map.53 = f32[1024,512]{1,0:T(8,128)} custom-call(f32[8,128]{1,0:T(8,128)S(1)} %add_add_fusion.32.own_ref, f32[8,128]{1,0:T(8,128)S(1)} %collective-permute-done.116.other_ref, f32[1024,512]{1,0:T(8,128)S(1)} %copy-done.6, f32[1024,256]{1,0:T(8,128)S(1)} %get-tuple-element.397.refs_0_, f32[1024,256]{1,0:T(8,128)S(1)} %get-tuple-element.398.refs_1_, ...), custom_call_target="tpu_custom_call" | custom-call | tf_op jit(solution)/shard_map/pallas_call | solution.py:507
  (87 shorter events, 27.7 us)
Async XLA Ops:
  0.0 39.4 %collective-permute-start.96 = (f32[1024,512]{1,0:T(8,128)}, f32[1024,512]{1,0:T(8,128)S(1)}, u32[]{:S(2)}, u32[]{:S(2)}) collective-permute-start(f32[1024,512]{1,0:T(8,128)} %bitcast.8), channel_id=1, source_target_pairs={{0,4},{4,0},{8,12},{12,8},{16,20},{20,16},{24,28},{28,24},{1,5},{5... | collective-permute-start | bytes 6291464 | tf_op jit(solution)/shard_map/ppermute | solution.py:22
  4.7 33.9 %collective-permute-start.97 = (bf16[256,1024]{1,0:T(8,128)(2,1)}, bf16[256,1024]{1,0:T(8,128)(2,1)S(1)}, u32[]{:S(2)}, u32[]{:S(2)}) collective-permute-start(bf16[256,1024]{1,0:T(8,128)(2,1)} %get-tuple-element.376), channel_id=1, source_target_pairs={{0,2},{1,3},{2,0},{3,1},{4,6},{5,7},{6,4},{7,5},{8,10},{9,11},{10,... | collective-permute-start | bytes 1572872 | tf_op jit(solution)/shard_map/ppermute | solution.py:28
  14.3 3.4 %collective-permute-start.72 = (bf16[16,1024]{1,0:T(8,128)(2,1)S(1)}, bf16[16,1024]{1,0:T(8,128)(2,1)S(1)}, u32[]{:S(2)}, u32[]{:S(2)}) collective-permute-start(bf16[16,1024]{1,0:T(8,128)(2,1)S(1)} %slice.231), channel_id=1, source_target_pairs={{3,1},{7,5},{11,9},{15,13},{19,17},{23,21},{27,25},{31,29}} | collective-permute-start | bytes 98312 | tf_op jit(solution)/shard_map/cond/branch_1_fun/ppermute | solution.py:329
  15.0 7.3 %collective-permute-start.73 = (bf16[16,1024]{1,0:T(8,128)(2,1)S(1)}, bf16[16,1024]{1,0:T(8,128)(2,1)S(1)}, u32[]{:S(2)}, u32[]{:S(2)}) collective-permute-start(bf16[16,1024]{1,0:T(8,128)(2,1)S(1)} %slice.232), channel_id=1, source_target_pairs={{3,0},{7,4},{11,8},{15,12},{19,16},{23,20},{27,24},{31,28}} | collective-permute-start | bytes 98312 | tf_op jit(solution)/shard_map/cond/branch_1_fun/ppermute | solution.py:329
  17.0 5.2 %collective-permute-start.74 = (bf16[16,1024]{1,0:T(8,128)(2,1)S(1)}, bf16[16,1024]{1,0:T(8,128)(2,1)S(1)}, u32[]{:S(2)}, u32[]{:S(2)}) collective-permute-start(bf16[16,1024]{1,0:T(8,128)(2,1)S(1)} %slice.233), channel_id=1, source_target_pairs={{3,2},{7,6},{11,10},{15,14},{19,18},{23,22},{27,26},{31,30}} | collective-permute-start | bytes 98312 | tf_op jit(solution)/shard_map/cond/branch_1_fun/ppermute | solution.py:329
  23.1 9.1 %collective-permute-start.51 = (bf16[32,1024]{1,0:T(8,128)(2,1)S(1)}, bf16[32,1024]{1,0:T(8,128)(2,1)S(1)}, u32[]{:S(2)}, u32[]{:S(2)}) collective-permute-start(bf16[32,1024]{1,0:T(8,128)(2,1)S(1)} %slice.213), channel_id=1, source_target_pairs={{2,0},{6,4},{10,8},{14,12},{18,16},{22,20},{26,24},{30,28}} | collective-permute-start | bytes 196616 | tf_op jit(solution)/shard_map/cond/branch_2_fun/ppermute | solution.py:329
  24.4 7.8 %collective-permute-start.52 = (bf16[32,1024]{1,0:T(8,128)(2,1)S(1)}, bf16[32,1024]{1,0:T(8,128)(2,1)S(1)}, u32[]{:S(2)}, u32[]{:S(2)}) collective-permute-start(bf16[32,1024]{1,0:T(8,128)(2,1)S(1)} %slice.214), channel_id=1, source_target_pairs={{2,3},{6,7},{10,11},{14,15},{18,19},{22,23},{26,27},{30,31}} | collective-permute-start | bytes 196616 | tf_op jit(solution)/shard_map/cond/branch_2_fun/ppermute | solution.py:329
  25.9 6.3 %collective-permute-start.53 = (bf16[32,1024]{1,0:T(8,128)(2,1)S(1)}, bf16[32,1024]{1,0:T(8,128)(2,1)S(1)}, u32[]{:S(2)}, u32[]{:S(2)}) collective-permute-start(bf16[32,1024]{1,0:T(8,128)(2,1)S(1)} %slice.215), channel_id=1, source_target_pairs={{2,1},{6,5},{10,9},{14,13},{18,17},{22,21},{26,25},{30,29}} | collective-permute-start | bytes 196616 | tf_op jit(solution)/shard_map/cond/branch_2_fun/ppermute | solution.py:329
  35.3 18.1 %collective-permute-start.98 = (bf16[256,1024]{1,0:T(8,128)(2,1)}, bf16[256,1024]{1,0:T(8,128)(2,1)S(1)}, u32[]{:S(2)}, u32[]{:S(2)}) collective-permute-start(bf16[256,1024]{1,0:T(8,128)(2,1)} %get-tuple-element.382), channel_id=1, source_target_pairs={{0,1},{1,2},{2,3},{3,0},{4,5},{5,6},{6,7},{7,4},{8,9},{9,10},{10,1... | collective-permute-start | bytes 1572872 | tf_op jit(solution)/shard_map/ppermute | solution.py:28
  36.3 25.1 %collective-permute-start.99 = (bf16[256,1024]{1,0:T(8,128)(2,1)}, bf16[256,1024]{1,0:T(8,128)(2,1)S(1)}, u32[]{:S(2)}, u32[]{:S(2)}) collective-permute-start(bf16[256,1024]{1,0:T(8,128)(2,1)} %get-tuple-element.383), channel_id=1, source_target_pairs={{0,3},{1,0},{2,1},{3,2},{4,7},{5,4},{6,5},{7,6},{8,11},{9,8},{10,9... | collective-permute-start | bytes 1572872 | tf_op jit(solution)/shard_map/ppermute | solution.py:28
  62.8 17.9 %copy-start.13 = (bf16[224,256]{1,0:T(8,128)(2,1)}, bf16[224,256]{1,0:T(8,128)(2,1)S(1)}, u32[]{:S(2)}) copy-start(bf16[224,256]{1,0:T(8,128)(2,1)S(1)} %get-tuple-element.393) | copy-start | bytes 344068
  62.8 17.9 %copy-start.14 = (bf16[224,256]{1,0:T(8,128)(2,1)}, bf16[224,256]{1,0:T(8,128)(2,1)S(1)}, u32[]{:S(2)}) copy-start(bf16[224,256]{1,0:T(8,128)(2,1)S(1)} %get-tuple-element.392) | copy-start | bytes 344068
  62.8 6.2 %collective-permute-start.100 = (bf16[224,256]{1,0:T(8,128)(2,1)S(1)}, bf16[224,256]{1,0:T(8,128)(2,1)S(1)}, u32[]{:S(2)}, u32[]{:S(2)}) collective-permute-start(bf16[224,256]{1,0:T(8,128)(2,1)S(1)} %get-tuple-element.387), channel_id=1, source_target_pairs={{0,1},{1,2},{2,3},{3,0},{4,5},{5,6},{6,7},{7,4},{8,9},{9,10},{10,1... | collective-permute-start | bytes 344072 | tf_op jit(solution)/shard_map/ppermute | solution.py:28
  64.3 10.4 %collective-permute-start.101 = (bf16[224,256]{1,0:T(8,128)(2,1)S(1)}, bf16[224,256]{1,0:T(8,128)(2,1)S(1)}, u32[]{:S(2)}, u32[]{:S(2)}) collective-permute-start(bf16[224,256]{1,0:T(8,128)(2,1)S(1)} %get-tuple-element.388), channel_id=1, source_target_pairs={{0,2},{1,3},{2,0},{3,1},{4,6},{5,7},{6,4},{7,5},{8,10},{9,11},{10,... | collective-permute-start | bytes 344072 | tf_op jit(solution)/shard_map/ppermute | solution.py:28
  64.4 10.2 %collective-permute-start.102 = (bf16[224,256]{1,0:T(8,128)(2,1)S(1)}, bf16[224,256]{1,0:T(8,128)(2,1)S(1)}, u32[]{:S(2)}, u32[]{:S(2)}) collective-permute-start(bf16[224,256]{1,0:T(8,128)(2,1)S(1)} %get-tuple-element.389), channel_id=1, source_target_pairs={{0,3},{1,0},{2,1},{3,2},{4,7},{5,4},{6,5},{7,6},{8,11},{9,8},{10,9... | collective-permute-start | bytes 344072 | tf_op jit(solution)/shard_map/ppermute | solution.py:28
  74.7 10.3 %collective-permute-start.103 = (bf16[224,256]{1,0:T(8,128)(2,1)S(1)}, bf16[224,256]{1,0:T(8,128)(2,1)S(1)}, u32[]{:S(2)}, u32[]{:S(2)}) collective-permute-start(bf16[224,256]{1,0:T(8,128)(2,1)S(1)} %add_convert_fusion.1.refs_0_), channel_id=1, source_target_pairs={{0,1},{1,2},{2,3},{4,5},{5,6},{6,7},{8,9},{9,10},{10,11},{12,13},{... | collective-permute-start | bytes 344072 | tf_op jit(solution)/shard_map/ppermute | solution.py:336
  79.4 8.0 %collective-permute-start.104 = (bf16[224,256]{1,0:T(8,128)(2,1)S(1)}, bf16[224,256]{1,0:T(8,128)(2,1)}, u32[]{:S(2)}, u32[]{:S(2)}) collective-permute-start(bf16[224,256]{1,0:T(8,128)(2,1)S(1)} %add_convert_fusion.1.refs_0_), channel_id=1, source_target_pairs={{1,0},{2,1},{3,2},{5,4},{6,5},{7,6},{9,8},{10,9},{11,10},{13,12},{... | collective-permute-start | bytes 344072 | tf_op jit(solution)/shard_map/ppermute | solution.py:336
  80.7 12.4 %collective-permute-start.107 = (bf16[224,256]{1,0:T(8,128)(2,1)}, bf16[224,256]{1,0:T(8,128)(2,1)S(1)}, u32[]{:S(2)}, u32[]{:S(2)}) collective-permute-start(bf16[224,256]{1,0:T(8,128)(2,1)} %copy-done.14), channel_id=1, source_target_pairs={{0,1},{1,2},{2,3},{3,0},{4,5},{5,6},{6,7},{7,4},{8,9},{9,10},{10,1... | collective-permute-start | bytes 344072 | tf_op jit(solution)/shard_map/ppermute | solution.py:28
  82.8 10.4 %collective-permute-start.108 = (bf16[224,256]{1,0:T(8,128)(2,1)}, bf16[224,256]{1,0:T(8,128)(2,1)S(1)}, u32[]{:S(2)}, u32[]{:S(2)}) collective-permute-start(bf16[224,256]{1,0:T(8,128)(2,1)} %copy-done.13), channel_id=1, source_target_pairs={{0,2},{1,3},{2,0},{3,1},{4,6},{5,7},{6,4},{7,5},{8,10},{9,11},{10,... | collective-permute-start | bytes 344072 | tf_op jit(solution)/shard_map/ppermute | solution.py:28
  83.3 10.0 %collective-permute-start.109 = (bf16[224,256]{1,0:T(8,128)(2,1)}, bf16[224,256]{1,0:T(8,128)(2,1)S(1)}, u32[]{:S(2)}, u32[]{:S(2)}) collective-permute-start(bf16[224,256]{1,0:T(8,128)(2,1)} %copy-done.12), channel_id=1, source_target_pairs={{0,3},{1,0},{2,1},{3,2},{4,7},{5,4},{6,5},{7,6},{8,11},{9,8},{10,9... | collective-permute-start | bytes 344072 | tf_op jit(solution)/shard_map/ppermute | solution.py:28
  85.0 6.8 %collective-permute-start.105 = (bf16[224,256]{1,0:T(8,128)(2,1)S(1)}, bf16[224,256]{1,0:T(8,128)(2,1)S(1)}, u32[]{:S(2)}, u32[]{:S(2)}) collective-permute-start(bf16[224,256]{1,0:T(8,128)(2,1)S(1)} %add_convert_fusion.1.refs_0_), channel_id=1, source_target_pairs={{0,2},{3,1},{4,6},{7,5},{8,10},{11,9},{12,14},{15,13},{16,18},{19,... | collective-permute-start | bytes 344072 | tf_op jit(solution)/shard_map/ppermute | solution.py:336
  91.8 20.4 %collective-permute-start.106 = (bf16[448,256]{1,0:T(8,128)(2,1)S(1)}, bf16[448,256]{1,0:T(8,128)(2,1)S(1)}, u32[]{:S(2)}, u32[]{:S(2)}) collective-permute-start(bf16[448,256]{1,0:T(8,128)(2,1)S(1)} %pad_maximum_fusion), channel_id=1, source_target_pairs={{1,0},{2,3},{5,4},{6,7},{9,8},{10,11},{13,12},{14,15},{17,16},{18,... | collective-permute-start | bytes 688136 | tf_op jit(solution)/shard_map/ppermute | solution.py:336
  94.3 9.6 %collective-permute-start.110 = (bf16[224,256]{1,0:T(8,128)(2,1)S(1)}, bf16[224,256]{1,0:T(8,128)(2,1)S(1)}, u32[]{:S(2)}, u32[]{:S(2)}) collective-permute-start(bf16[224,256]{1,0:T(8,128)(2,1)S(1)} %add_convert_fusion.refs_0_), channel_id=1, source_target_pairs={{0,1},{1,2},{2,3},{3,0},{4,5},{5,6},{6,7},{7,4},{8,9},{9,10},{10,1... | collective-permute-start | bytes 344072 | tf_op jit(solution)/shard_map/ppermute | solution.py:28
  99.3 9.4 %collective-permute-start.111 = (bf16[224,256]{1,0:T(8,128)(2,1)S(1)}, bf16[224,256]{1,0:T(8,128)(2,1)S(1)}, u32[]{:S(2)}, u32[]{:S(2)}) collective-permute-start(bf16[224,256]{1,0:T(8,128)(2,1)S(1)} %add_convert_fusion.refs_0_), channel_id=1, source_target_pairs={{0,2},{1,3},{2,0},{3,1},{4,6},{5,7},{6,4},{7,5},{8,10},{9,11},{10,... | collective-permute-start | bytes 344072 | tf_op jit(solution)/shard_map/ppermute | solution.py:28
  99.3 9.4 %collective-permute-start.112 = (bf16[224,256]{1,0:T(8,128)(2,1)S(1)}, bf16[224,256]{1,0:T(8,128)(2,1)S(1)}, u32[]{:S(2)}, u32[]{:S(2)}) collective-permute-start(bf16[224,256]{1,0:T(8,128)(2,1)S(1)} %add_convert_fusion.refs_0_), channel_id=1, source_target_pairs={{0,3},{1,0},{2,1},{3,2},{4,7},{5,4},{6,5},{7,6},{8,11},{9,8},{10,9... | collective-permute-start | bytes 344072 | tf_op jit(solution)/shard_map/ppermute | solution.py:28
  103.9 18.4 %copy-start.6 = (f32[1024,512]{1,0:T(8,128)S(1)}, f32[1024,512]{1,0:T(8,128)}, u32[]{:S(2)}) copy-start(f32[1024,512]{1,0:T(8,128)} %copy-done.5) | copy-start | bytes 6291460
  110.1 12.2 %collective-permute-start.118 = (bf16[1024,256]{1,0:T(8,128)(2,1)S(1)}, bf16[1024,256]{1,0:T(8,128)(2,1)S(1)}, u32[]{:S(2)}, u32[]{:S(2)}) collective-permute-start(bf16[1024,256]{1,0:T(8,128)(2,1)S(1)} %get-tuple-element.400), channel_id=1, source_target_pairs={{0,4},{4,0},{8,12},{12,8},{16,20},{20,16},{24,28},{28,24},{1,5},{5... | collective-permute-start | bytes 1572872 | tf_op jit(solution)/shard_map/ppermute | solution.py:22
  114.4 7.9 %collective-permute-start.117 = (bf16[1024,256]{1,0:T(8,128)(2,1)S(1)}, bf16[1024,256]{1,0:T(8,128)(2,1)S(1)}, u32[]{:S(2)}, u32[]{:S(2)}) collective-permute-start(bf16[1024,256]{1,0:T(8,128)(2,1)S(1)} %get-tuple-element.399), channel_id=1, source_target_pairs={{0,4},{4,0},{8,12},{12,8},{16,20},{20,16},{24,28},{28,24},{1,5},{5... | collective-permute-start | bytes 1572872 | tf_op jit(solution)/shard_map/ppermute | solution.py:22
  114.5 4.3 %collective-permute-start.113 = (f32[8,128]{1,0:T(8,128)S(1)}, f32[8,128]{1,0:T(8,128)S(1)}, u32[]{:S(2)}, u32[]{:S(2)}) collective-permute-start(f32[8,128]{1,0:T(8,128)S(1)} %add.284), channel_id=1, source_target_pairs={{0,1},{1,2},{2,3},{3,0},{4,5},{5,6},{6,7},{7,4},{8,9},{9,10},{10,1... | collective-permute-start | bytes 12296 | tf_op jit(solution)/shard_map/ppermute | solution.py:28
  115.7 3.4 %collective-permute-start.114 = (f32[8,128]{1,0:T(8,128)S(1)}, f32[8,128]{1,0:T(8,128)S(1)}, u32[]{:S(2)}, u32[]{:S(2)}) collective-permute-start(f32[8,128]{1,0:T(8,128)S(1)} %add.284), channel_id=1, source_target_pairs={{0,2},{1,3},{2,0},{3,1},{4,6},{5,7},{6,4},{7,5},{8,10},{9,11},{10,... | collective-permute-start | bytes 12296 | tf_op jit(solution)/shard_map/ppermute | solution.py:28
  116.9 2.8 %collective-permute-start.115 = (f32[8,128]{1,0:T(8,128)S(1)}, f32[8,128]{1,0:T(8,128)S(1)}, u32[]{:S(2)}, u32[]{:S(2)}) collective-permute-start(f32[8,128]{1,0:T(8,128)S(1)} %add.284), channel_id=1, source_target_pairs={{0,3},{1,0},{2,1},{3,2},{4,7},{5,4},{6,5},{7,6},{8,11},{9,8},{10,9... | collective-permute-start | bytes 12296 | tf_op jit(solution)/shard_map/ppermute | solution.py:28
  119.6 2.7 %collective-permute-start.116 = (f32[8,128]{1,0:T(8,128)S(1)}, f32[8,128]{1,0:T(8,128)S(1)}, u32[]{:S(2)}, u32[]{:S(2)}) collective-permute-start(f32[8,128]{1,0:T(8,128)S(1)} %add_add_fusion.32.own_ref), channel_id=1, source_target_pairs={{0,4},{4,0},{8,12},{12,8},{16,20},{20,16},{24,28},{28,24},{1,5},{5... | collective-permute-start | bytes 12296 | tf_op jit(solution)/shard_map/ppermute | solution.py:22
  (13 other events, 54.7 us)
